TPU v7x, 32 devices: a whole 2x2x4 slice. The times are simulated.
32 devices in a mesh: groups: 2 (over y), dp: 8 (over z, x), tensor: 2 (over core).
Axes of the slice: x: 2, y: 2, z: 4, core: 2. Of those that a mesh axis runs over, the one named last changes fastest.
Arguments:
- tokens: bfloat16 [16384, 8192], P(('groups', 'dp'), 'tensor'), parts along dimension 0, may hold values from -6 to 6
- key_weight: bfloat16 [8192, 1024], P('tensor'), may hold values from -0.0625 to 0.0625
- down_pool: bfloat16 [80, 64, 8192], P('dp', None, 'tensor'), may hold values from -0.0625 to 0.0625
- up_pool: bfloat16 [80, 64, 1024], P('dp', None, 'tensor'), may hold values from -0.75 to 0.75
- adapter_ids: int32 [16, 4], P('groups'), parts along dimension 0, may hold values from 0 to 79, as said below
- lengths: int32 [16, 4], P(('groups', 'dp')), parts along dimension 0, may hold values from 1 to 512, 1024 in all within a row
- owner_map: int32 [160], P('groups'), parts along dimension 0, may hold values from 0 to 79, as said below
Outputs:
- keys: bfloat16 [16384, 1024], P(('groups', 'dp'), 'tensor'), parts along dimension 0
There are 2 independent parts, one for each index of `groups`. A program takes and returns all parts, laid end to end along the dimension named above; an argument that names none is the same for every part. Nothing has to cross between parts.
Inputs may be any that keep to these rules, and one draw needn't show every extreme that they name: A permutation: adapter a sits in pool slot owner_map[a], held by dp index owner_map[a] // 10. `adapter_ids`: the 4 requests of one row name adapters held by 4 different dp indices.
All inputs are finite; a program needn't handle non-finite values.
Results may differ from a plain program's by a relative error of at most 0.001.
Values may be sent and summed in bfloat16 or wider, within the bound.
No kernel may reach another device: no remote copies, remote signals or barrier semaphores. Data moves between devices by JAX's collectives and lax.ppermute only.
A program may use at most 128 MiB of HBM per device.

v0:
```python
import functools

import jax
import jax.numpy as jnp
from jax import lax
from jax.experimental import pallas as pl
from jax.experimental.pallas import tpu as pltpu
from jax.sharding import PartitionSpec as P

ADAPTER_SCALE = 2.0
MIB = 1 << 20
ANY = pl.BlockSpec(memory_space=pl.ANY)
VMEM = pl.BlockSpec(memory_space=pltpu.VMEM)


def in_vmem(x):
    return pltpu.with_memory_space_constraint(x, pltpu.VMEM)


def in_hbm(x):
    return pltpu.with_memory_space_constraint(x, pltpu.HBM)


X_STEPS = 4
Z_STEPS = 6
NEVER = 1000.0
E_TABLE, O_TABLE, X_TABLE, PLACE, MISFIT = range(5)


def plan_kernel(held, planes, req, ids, owner_map, out):
    n = planes * req
    member = lax.axis_index("dp")
    plane, column = member // 2, member % 2
    lane = lax.broadcasted_iota(jnp.int32, (n, 128), 1)
    sub = lax.broadcasted_iota(jnp.int32, (n, 128), 0)
    lane_f, sub_f = lane.astype(jnp.float32), sub.astype(jnp.float32)

    def row_of(at):
        return sum([(at >= q * req).astype(jnp.float32) for q in range(1, planes)])

    dest_i, dest_k = row_of(lane), row_of(sub)

    def entries(c):
        by_lane = [jnp.full((n, 128), -1.0, jnp.float32) for _ in range(5)]
        by_sub = [jnp.full((n, 128), -2.0, jnp.float32) for _ in range(5)]
        for i in range(n):
            slot = owner_map[ids[i % req, 2 * (i // req) + c]]
            owner = slot // held
            values = (slot, owner, owner // 2, owner % 2, slot - owner * held)
            for v, value in enumerate(values):
                value = value.astype(jnp.float32)
                by_lane[v] = jnp.where(lane == i, value, by_lane[v])
                by_sub[v] = jnp.where(sub == i, value, by_sub[v])
        return by_lane, by_sub

    def over_x(by_lane, by_sub, c):
        (slot_i, owner_i, src_i, col_i, _), (slot_k, owner_k, src_k, col_k, _) = by_lane, by_sub
        c = c.astype(jnp.float32)
        same = slot_i == slot_k
        key_i = jnp.where(col_i == c, -1.0, jnp.abs(dest_i - src_i) * n + (n - 1 - lane_f))
        key_k = jnp.where(col_k == c, -1.0, jnp.abs(dest_k - src_k) * n + (n - 1 - sub_f))
        best_i = jnp.max(jnp.where(same, key_k, -1.0), axis=0, keepdims=True)
        best_k = jnp.max(jnp.where(same, key_i, -1.0), axis=1, keepdims=True)
        ahead = (key_k == best_k) & (key_k >= 0) & (owner_k == owner_i) & (key_k > best_i)
        pos = jnp.sum(jnp.where(ahead, 1.0, 0.0), axis=0, keepdims=True)
        return pos, (key_i == best_i) & (key_i >= 0)

    row = lax.broadcasted_iota(jnp.int32, (8, 128), 0)
    lane8 = lax.broadcasted_iota(jnp.int32, (8, 128), 1).astype(jnp.float32)
    row_f = row.astype(jnp.float32)
    links = planes - 1
    up = row < links
    last = float(planes - 1)
    link = jnp.where(up, row_f, row_f - links)

    def top(x):
        return jnp.broadcast_to(x[0:1, :], (8, 128))

    def schedule(by_lane, by_sub, xpos, c):
        slot_i, _, src_i, col_i, _ = by_lane
        same = slot_i == by_sub[0]
        dest, src = top(dest_i), top(src_i)
        d_dest, d_src = jnp.where(up, dest, last - dest), jnp.where(up, src, last - src)

        def beyond(sign):
            more = same & ((dest_k - dest_i) * sign > 0)
            return top(jnp.max(jnp.where(more, 1.0, 0.0), axis=0, keepdims=True))

        farther = jnp.where(up, beyond(1.0), beyond(-1.0))
        valid = (row < 2 * links) & (lane8 < n)
        lead = valid & (farther == 0.0) & (d_dest > d_src)
        on = lead & (d_src <= link) & (d_dest > link)
        starts = d_src == link
        local = top(col_i) == c.astype(jnp.float32)
        first = jnp.where(local, 0.0, top(jnp.broadcast_to(xpos, (8, 128))) + 1)
        ready = jnp.where(starts, first, NEVER)
        pos = jnp.full((8, 128), NEVER, jnp.float32)
        for t in range(Z_STEPS):
            open_ = on & (ready <= t) & (pos >= NEVER)
            key = jnp.where(open_, d_dest * 128 + (127 - lane8), -1.0)
            chosen = open_ & (key == jnp.max(key, axis=1, keepdims=True))
            pos = jnp.where(chosen, float(t), pos)
            before = jnp.concatenate([pos[7:8, :], pos[0:7, :]], axis=0)
            ready = jnp.where(starts, first, before + 1)
        misfit = jnp.max(jnp.where(on & (pos >= NEVER), 1.0, 0.0), axis=1, keepdims=True)
        return same, dest, src, local, on, starts, pos, jnp.max(misfit, axis=0, keepdims=True)

    by_lane, by_sub = entries(column)
    within_i = by_lane[4]
    xpos, _ = over_x(by_lane, by_sub, column)
    same, dest, src, local, on, starts, pos, misfit = schedule(by_lane, by_sub, xpos, column)
    other_lane, other_sub = entries(1 - column)
    other_xpos, other_lead = over_x(other_lane, other_sub, 1 - column)
    other_misfit = schedule(other_lane, other_sub, other_xpos, 1 - column)[-1]
    misfit = jnp.maximum(misfit, other_misfit)

    from_x = float(held)
    from_e = from_x + X_STEPS
    from_o = from_e + Z_STEPS
    own = jnp.where(local, top(within_i), from_x + top(jnp.broadcast_to(xpos, (8, 128))))

    def table(hit, source):
        return jnp.sum(jnp.where(hit, source + 1, 0.0), axis=1, keepdims=True) - 1

    def only(which, x):
        return jnp.sum(jnp.where(row == which, x, 0.0), axis=0, keepdims=True)

    def sent(which, passing_from):
        hit = only(which, jnp.where(on, 1.0, 0.0)) == 1.0
        fresh = only(which, jnp.where(starts, 1.0, 0.0)) == 1.0
        at, earlier = only(which, pos), only(which - 1, pos)
        source = jnp.where(fresh, own, passing_from + earlier)
        return table(hit & (at == row_f), source)

    e_row = jnp.where(plane % 2 == 0, plane, links + (planes - 1 - plane))
    o_row = jnp.where(plane == 1, 1, jnp.where(plane == 2, links + 1, 7))
    e_table = sent(e_row, from_o)
    o_table = sent(o_row, from_e)
    (_, owner_o, _, _, within_o) = other_lane
    mine = top(owner_o) == member.astype(jnp.float32)
    other_lead8 = top(jnp.where(other_lead, 1.0, 0.0)) == 1.0
    other_xpos8 = top(jnp.broadcast_to(other_xpos, (8, 128)))
    x_table = table(mine & other_lead8 & (other_xpos8 == row_f), top(within_o))

    arrival = jnp.zeros((8, 128), jnp.float32)
    for which in range(2 * links):
        one = jnp.broadcast_to(pos[which : which + 1, :], (n, 128))
        one_on = jnp.broadcast_to(jnp.where(on, 1.0, 0.0)[which : which + 1, :], (n, 128))
        by_k = jnp.sum(jnp.where((lane == sub) & (one_on == 1.0), one + 1, 0.0), axis=1, keepdims=True)
        arrives = jnp.max(jnp.where(same, by_k, 0.0), axis=0, keepdims=True) - 1
        if which < links:
            hit = (dest > src) & (dest == which + 1)
        else:
            hit = (dest < src) & (last - dest == which - links + 1)
        arrival = jnp.where(hit, arrives, arrival)
    odd = dest - 2 * jnp.floor(dest * 0.5)
    outer = jnp.where(dest > src, odd, 1 - odd) == 1.0
    final = jnp.where(dest == src, own, jnp.where(outer, from_e, from_o) + arrival)
    my_rows = lane8 == (plane * req).astype(jnp.float32) + row_f
    place = jnp.sum(jnp.where(my_rows & (row < req), final, 0.0), axis=1, keepdims=True)
    place = jnp.where(misfit == 1.0, 0.0, place)
    result = jnp.zeros((8, 128), jnp.float32)
    for at, values in ((E_TABLE, e_table), (O_TABLE, o_table), (X_TABLE, x_table), (PLACE, place), (MISFIT, misfit)):
        result = jnp.where(lane8 == at, values, result)
    out[...] = result.astype(jnp.int32)


def plan(held, adapter_ids, owner_map):
    rows, req = adapter_ids.shape
    return pl.pallas_call(
        functools.partial(plan_kernel, held, rows // 2, req),
        grid_spec=pltpu.PrefetchScalarGridSpec(
            num_scalar_prefetch=2, grid=(), in_specs=[], out_specs=VMEM
        ),
        out_shape=jax.ShapeDtypeStruct((8, 128), jnp.int32),
        compiler_params=pltpu.CompilerParams(vmem_limit_bytes=4 * MIB),
        name="plan",
    )(adapter_ids.T, owner_map)


def pick_kernel(step, size, lo, streams, held, piece, table, down, up, *refs):
    at = 0
    got = []
    for many in held:
        got.append(refs[at : at + many])
        at += many
    refs = list(refs[at:])
    if piece is not None:
        tokens, weight = refs.pop(0), refs.pop(0)
        held_weight, weight_sem = refs.pop(-2), refs.pop(-1)
        distance, shift = piece
        columns, wide = up.shape[2], held_weight.shape[1]
        to = lax.rem(lax.axis_index("tensor") + distance, 2)
        first = pl.multiple_of(to * columns + shift, 128)
        load = pltpu.make_async_copy(weight.at[:, pl.ds(first, wide)], held_weight, weight_sem)
        load.start()
    outs, sem = refs[: len(streams)], refs[-1]
    slots, _, width = down.shape
    from_x, from_e, from_o = slots, slots + X_STEPS, slots + X_STEPS + Z_STEPS
    over_x = [(from_x + t, ref) for t, ref in enumerate(got[2])]
    outer = [(from_e + t, ref) for t, ref in enumerate(got[0])]
    middle = [(from_o + t, ref) for t, ref in enumerate(got[1])]
    sources = {E_TABLE: over_x + middle, O_TABLE: over_x + outer, X_TABLE: []}
    rows = pl.ds(lo, size)
    for i, stream in enumerate(streams):
        code, out = table[step, stream], outs[i]

        @pl.when((code >= 0) & (code < slots))
        def _(code=code, out=out, i=i):
            pltpu.make_async_copy(
                down.at[code, rows, :], out.at[:, pl.ds(0, width)], sem.at[i]
            ).start()
            pltpu.make_async_copy(
                up.at[code, rows, :], out.at[:, pl.ds(width, up.shape[2])], sem.at[i]
            ).start()

        for number, ref in sources[stream]:

            @pl.when(code == number)
            def _(ref=ref, out=out, i=i):
                pltpu.make_async_copy(ref, out, sem.at[i]).start()

    if piece is not None:
        load.wait()
        product = refs[len(streams)]
        tile = min(256, product.shape[0])
        for at in range(0, product.shape[0], tile):
            product[at : at + tile, :] = jnp.dot(
                tokens[at : at + tile, :],
                held_weight[...],
                preferred_element_type=jnp.float32,
            )

    for i, stream in enumerate(streams):

        @pl.when(table[step, stream] >= 0)
        def _(i=i):
            pltpu.make_async_copy(outs[i], outs[i], sem.at[i]).wait()


def pick(step, lo, size, streams, table, down_pool, up_pool, got, piece, tokens, key_weight):
    many = tokens.shape[0]
    columns = up_pool.shape[2]
    wide = down_pool.shape[2] + columns
    held = [len(arrays) for arrays in got]
    operands = [in_hbm(down_pool), in_hbm(up_pool)] + [a for arrays in got for a in arrays]
    in_specs = [ANY] * len(operands)
    out_specs = [ANY] * len(streams)
    out_shape = [pltpu.VMEM((size, wide), down_pool.dtype)] * len(streams)
    scratch = [pltpu.SemaphoreType.DMA((len(streams),))]
    if piece is not None:
        operands += [in_vmem(tokens), in_hbm(key_weight)]
        in_specs += [VMEM, ANY]
        out_specs.append(VMEM)
        out_shape.append(jax.ShapeDtypeStruct((many, columns // 2), jnp.float32))
        scratch += [
            pltpu.VMEM((tokens.shape[1], columns // 2), key_weight.dtype),
            pltpu.SemaphoreType.DMA,
        ]
    outs = pl.pallas_call(
        functools.partial(pick_kernel, step, size, lo, streams, held, piece),
        grid_spec=pltpu.PrefetchScalarGridSpec(
            num_scalar_prefetch=1,
            grid=(),
            in_specs=in_specs,
            out_specs=out_specs,
            scratch_shapes=scratch,
        ),
        out_shape=out_shape,
        compiler_params=pltpu.CompilerParams(vmem_limit_bytes=(4 if piece is None else 16) * MIB),
        name="pick",
    )(table, *operands)
    return outs[: len(streams)], outs[len(streams) :]


def dense_kernel(index, down, up, out):
    width = down.shape[2]
    out[:, :, :width] = down[...]
    out[:, :, width:] = up[...]


def dense(adapter_ids, owner_map, down_pool, up_pool):
    held, rank, width = down_pool.shape
    columns = up_pool.shape[2]
    slots = owner_map[adapter_ids] - lax.axis_index("dp") * held
    here = (slots >= 0) & (slots < held)
    index = jnp.sum(jnp.where(here, slots, 0), axis=1).astype(jnp.int32)
    many = index.shape[0]
    send = pl.pallas_call(
        dense_kernel,
        grid_spec=pltpu.PrefetchScalarGridSpec(
            num_scalar_prefetch=1,
            grid=(many,),
            in_specs=[
                pl.BlockSpec((1, rank, width), lambda j, index: (index[j], 0, 0)),
                pl.BlockSpec((1, rank, columns), lambda j, index: (index[j], 0, 0)),
            ],
            out_specs=pl.BlockSpec((1, rank, width + columns), lambda j, index: (j, 0, 0)),
        ),
        out_shape=jax.ShapeDtypeStruct((many, rank, width + columns), down_pool.dtype),
        name="pick_all",
    )(index, in_hbm(down_pool), in_hbm(up_pool))
    return lax.all_to_all(send, "dp", split_axis=0, concat_axis=0, tiled=True)


def request_of_rows(lengths, count, first, rows):
    at = first + lax.broadcasted_iota(jnp.int32, (rows, 1), 0)
    which = jnp.zeros((rows, 1), jnp.int32)
    end = 0
    for r in range(count - 1):
        end = end + lengths[0, r]
        which += (at >= end).astype(jnp.int32)
    return which


def code_kernel(count, kinds, routed, index, others, lengths, tokens, *refs):
    n = sum(many for _, many in kinds)
    arrays, refs = refs[:n], refs[n:]
    out, up, flag, down, sem, up_sem = refs
    rank, columns = out.shape[1] // 2, up.shape[1]
    features = tokens.shape[1]
    flag[0] = 0
    if routed:
        flag[0] = jnp.maximum(index[0, MISFIT], others[0, MISFIT])

    def source(r):
        return index[r, PLACE] if routed else index[r, 0]

    def load(r, kind, held):
        if kind == "pool":
            slot = source(r)
            parts = [(held[0].at[slot], held[1].at[slot])]
        elif kind == "several":
            block = held[0].at[source(r)]
            parts = [(block.at[:, pl.ds(0, features)], block.at[:, pl.ds(features, columns)])]
        else:
            parts = [
                (ref.at[:, pl.ds(0, features)], ref.at[:, pl.ds(features, columns)])
                for ref in held
            ]
        size = rank // len(parts)
        for p, (down_part, up_part) in enumerate(parts):
            mine = pl.ds(r * rank + p * size, size)
            pltpu.make_async_copy(down_part, down.at[mine, :], sem).start()
            pltpu.make_async_copy(up_part, up.at[mine, :], up_sem).start()

    for r in range(count):
        at, number = 0, 0
        for kind, many in kinds:
            held = arrays[at : at + many]
            at += many
            if kind == "several":
                load(r, kind, held)
            elif kind == "pool":
                number = held[0].shape[0]

                @pl.when(source(r) < number)
                def _(r=r, kind=kind, held=held):
                    load(r, kind, held)

            else:

                @pl.when(source(r) == number)
                def _(r=r, kind=kind, held=held):
                    load(r, kind, held)

                number += 1

    pltpu.make_async_copy(down, down, sem).wait()
    half = out.shape[0]
    tile = min(256, half)
    for i in range(half // tile):
        parts = []
        for side in range(2):
            first = side * half + i * tile
            full = lax.dot_general(
                tokens[first : first + tile, :],
                down[...],
                (((1,), (1,)), ((), ())),
                preferred_element_type=jnp.float32,
            )
            which = request_of_rows(lengths, count, first, tile)
            code = full[:, :rank]
            for r in range(1, count):
                code = jnp.where(which == r, full[:, r * rank : (r + 1) * rank], code)
            parts.append(code)
        out[i * tile : (i + 1) * tile, :] = jnp.concatenate(parts, axis=1)
    pltpu.make_async_copy(up, up, up_sem).wait()


def codes(index, others, lengths, tokens, sources, rank, columns):
    many, features = tokens.shape
    count = lengths.shape[1]
    routed = others is not None
    kinds = [(kind, len(held)) for kind, held in sources]
    arrays = [array for _, held in sources for array in held]
    return pl.pallas_call(
        functools.partial(code_kernel, count, kinds, routed),
        grid_spec=pltpu.PrefetchScalarGridSpec(
            num_scalar_prefetch=3,
            grid=(),
            in_specs=[VMEM] + [ANY] * len(arrays),
            out_specs=[VMEM, VMEM, pl.BlockSpec(memory_space=pltpu.SMEM)],
            scratch_shapes=[
                pltpu.VMEM((count * rank, features), tokens.dtype),
                pltpu.SemaphoreType.DMA,
                pltpu.SemaphoreType.DMA,
            ],
        ),
        out_shape=[
            jax.ShapeDtypeStruct((many // 2, 2 * rank), jnp.float32),
            jax.ShapeDtypeStruct((count * rank, columns), tokens.dtype),
            jax.ShapeDtypeStruct((1,), jnp.int32),
        ],
        compiler_params=pltpu.CompilerParams(vmem_limit_bytes=(16 if routed else 40) * MIB),
        name="codes",
    )(index, others if routed else index, lengths, in_vmem(tokens) if routed else tokens, *arrays)


def finish_kernel(count, parts, shares, tile, lengths, *refs):
    code_parts, base_parts = refs[:parts], refs[parts : parts + sum(shares)]
    up, out, hold, sem = refs[parts + sum(shares) :]
    rank = up.shape[0] // count
    code = code_parts[0][...]
    for p in range(1, parts):
        code = code + code_parts[p][...]
    half = code.shape[0]
    copies = []
    for i in range(out.shape[0] // tile):
        first = i * tile
        side, at = first // half, first % half
        mine = code[at : at + tile, side * rank : (side + 1) * rank]
        which = request_of_rows(lengths, count, first, tile)
        zero = jnp.zeros_like(mine)
        wide = jnp.concatenate([jnp.where(which == r, mine, zero) for r in range(count)], axis=1)
        delta = None
        for _ in range(3):
            part = wide.astype(jnp.bfloat16)
            wide = wide - part.astype(jnp.float32)
            term = jnp.dot(part, up[...], preferred_element_type=jnp.float32)
            delta = term if delta is None else delta + term
        rows = pl.ds(first, tile)
        left, number = 0, 0
        for share in shares:
            base = base_parts[number][rows, :]
            for p in range(1, share):
                base = base + base_parts[number + p][rows, :]
            number += share
            right = left + base.shape[1]
            total = base + ADAPTER_SCALE * delta[:, left:right]
            hold[rows, left:right] = total.astype(hold.dtype)
            left = right
        copies.append(pltpu.make_async_copy(hold.at[rows, :], out.at[rows, :], sem.at[i]))
        copies[-1].start()
    for copy in copies:
        copy.wait()


def finish(lengths, code_parts, base, up):
    many = base[0][0].shape[0]
    columns = up.shape[1]
    count = lengths.shape[1]
    parts = len(code_parts)
    tile = min(256, many // 2)
    shares = [len(share) for share in base]
    return pl.pallas_call(
        functools.partial(finish_kernel, count, parts, shares, tile),
        grid_spec=pltpu.PrefetchScalarGridSpec(
            num_scalar_prefetch=1,
            grid=(),
            in_specs=[VMEM] * (parts + sum(shares) + 1),
            out_specs=ANY,
            scratch_shapes=[
                pltpu.VMEM((many, columns), jnp.bfloat16),
                pltpu.SemaphoreType.DMA((many // tile,)),
            ],
        ),
        out_shape=jax.ShapeDtypeStruct((many, columns), jnp.bfloat16),
        compiler_params=pltpu.CompilerParams(vmem_limit_bytes=24 * MIB),
        name="finish",
    )(lengths, *code_parts, *[part for share in base for part in share], up)


def gathered(part, axis, size):
    held = [part]
    for step in range(1, size):
        held.append(lax.ppermute(part, axis, [(i, (i + step) % size) for i in range(size)]))
    return held


def route(table, down_pool, up_pool, n_dp, tokens, key_weight):
    rank = down_pool.shape[1]
    size = rank // 2
    half = up_pool.shape[2] // 2
    outer = [(i, i ^ 2) for i in range(n_dp)]
    middle = [(i, i + 2) for i in (2, 3)] + [(i, i - 2) for i in (4, 5)]
    over_x = [(i, i ^ 1) for i in range(n_dp)]
    got = [([], [], []), ([], [], [])]
    pieces = [(1, 0), (1, half), (0, 0), (0, half)]
    done = []
    for step in range(Z_STEPS):
        streams = [E_TABLE, O_TABLE] + ([X_TABLE] if step < X_STEPS else [])
        for part in range(2):
            known = [list(arrays) for arrays in got[part]]
            piece = pieces[step - 1] if part == 1 and 1 <= step <= len(pieces) else None
            sends, product = pick(
                step, part * size, size, streams, table, down_pool, up_pool, known, piece,
                tokens, key_weight,
            )
            done += product
            for stream, send in zip(streams, sends):
                pairs = (outer, middle, over_x)[stream]
                got[part][stream].append(lax.ppermute(send, "dp", pairs))
    return got, done


def shards(sizes, tokens, key_weight, down_pool, up_pool, adapter_ids, lengths, owner_map):
    n_groups, n_dp, n_tensor = sizes
    held, rank, width = down_pool.shape
    columns = up_pool.shape[2]

    def sent_on(part, step):
        pairs = [(i, (i + step) % n_tensor) for i in range(n_tensor)]
        return lax.ppermute(part, "tensor", pairs)

    def by_all_to_all():
        me = lax.axis_index("tensor")
        parts = []
        for step in range(n_tensor):
            first = lax.rem(me + step, n_tensor) * columns
            weight = lax.dynamic_slice_in_dim(key_weight, first, columns, 1)
            part = jnp.dot(tokens, weight, preferred_element_type=jnp.float32)
            parts.append(sent_on(part, step) if step else part)
        blocks = dense(adapter_ids, owner_map, down_pool, up_pool)
        member = lax.axis_index("dp")
        my_ids = lax.dynamic_index_in_dim(adapter_ids, member, 0, keepdims=False)
        index = (owner_map[my_ids] // held)[:, None]
        code, up, _ = codes(index, None, lengths, tokens, [("several", (blocks,))], rank, columns)
        return finish(lengths, gathered(code, "tensor", n_tensor), [parts], up)

    routable = n_dp == 8 and n_tensor == 2 and n_groups <= 2
    if not (routable and rank % 32 == 0 and adapter_ids.shape[1] == 4):
        return by_all_to_all()
    table = plan(held, adapter_ids, owner_map)
    got, done = route(table, down_pool, up_pool, n_dp, tokens, key_weight)
    base = [[here, sent_on(there, 1)] for there, here in zip(done[:2], done[2:])]
    others = gathered(table, "groups", n_groups)[-1]
    sources = [("pool", (in_hbm(down_pool), in_hbm(up_pool)))]
    for stream in (2, 0, 1):
        sources += [("block", pair) for pair in zip(got[0][stream], got[1][stream])]
    code, up, misfit = codes(table, others, lengths, tokens, sources, rank, columns)
    keys = finish(lengths, gathered(code, "tensor", n_tensor), base, up)
    return lax.cond(misfit[0] == 0, lambda: keys, by_all_to_all)


def solution(mesh):
    placed = (
        P(("groups", "dp"), "tensor"),
        P("tensor", None),
        P("dp", None, "tensor"),
        P("dp", None, "tensor"),
        P("groups", None),
        P(("groups", "dp"), None),
        P("groups"),
    )
    sizes = tuple(mesh.shape[name] for name in ("groups", "dp", "tensor"))
    return jax.shard_map(
        functools.partial(shards, sizes),
        mesh=mesh,
        in_specs=placed,
        out_specs=P(("groups", "dp"), "tensor"),
        check_vma=False,
    )
```

profile of v0, /device:TPU:9, one launch (start us, length us, event | category | flops | bytes accessed | tf_op | source)
XLA Modules:
  0.0 129.0 jit_solution(11193113915514341875)
XLA Ops:
  0.0 1.8 %plan.1.table.index = s32[8,128]{1,0:T(8,128)S(1)} custom-call(s32[4,8]{1,0:T(4,128)} %bitcast.20, s32[80]{0:T(128)} %owner_map.1), custom_call_target="tpu_custom_call" | custom-call | tf_op jit(solution)/shard_map/plan/pallas_call | solution.py:170
  1.8 1.7 %pick.12 = (bf16[32,4608]{1,0:T(8,128)(2,1)S(1)}, bf16[32,4608]{1,0:T(8,128)(2,1)S(1)}, bf16[32,4608]{1,0:T(8,128)(2,1)S(1)}) custom-call(s32[8,128]{1,0:T(8,128)S(1)} %plan.1.table.index, bf16[10,64,4096]{2,1,0:T(8,128)(2,1)} %refs_0_.1, bf16[10,64,512]{2,1,0:T(8,128)(2,1)} %refs_1_.1), custom_call_target="tpu_custom_call" | custom-call | tf_op jit(solution)/shard_map/pick/pallas_call | solution.py:260
  5.0 4.3 %collective-permute-start.6 = (bf16[32,4608]{1,0:T(8,128)(2,1)S(1)}, bf16[32,4608]{1,0:T(8,128)(2,1)S(1)}, u32[]{:S(2)}, u32[]{:S(2)}) collective-permute-start(bf16[32,4608]{1,0:T(8,128)(2,1)S(1)} %get-tuple-element.74), channel_id=1, source_target_pairs={{4,8},{6,10},{8,4},{10,6},{5,9},{7,11},{9,5},{11,7},{20,24},{22,26... | collective-permute-start | bytes 884744 | tf_op jit(solution)/shard_map/ppermute | solution.py:513
  9.3 1.7 %pick.13 = (bf16[32,4608]{1,0:T(8,128)(2,1)S(1)}, bf16[32,4608]{1,0:T(8,128)(2,1)S(1)}, bf16[32,4608]{1,0:T(8,128)(2,1)S(1)}) custom-call(s32[8,128]{1,0:T(8,128)S(1)} %plan.1.table.index, bf16[10,64,4096]{2,1,0:T(8,128)(2,1)} %refs_0_.1, bf16[10,64,512]{2,1,0:T(8,128)(2,1)} %refs_1_.1), custom_call_target="tpu_custom_call" | custom-call | tf_op jit(solution)/shard_map/pick/pallas_call | solution.py:260
  11.5 3.1 %collective-permute-start.9 = (bf16[32,4608]{1,0:T(8,128)(2,1)S(1)}, bf16[32,4608]{1,0:T(8,128)(2,1)S(1)}, u32[]{:S(2)}, u32[]{:S(2)}) collective-permute-start(bf16[32,4608]{1,0:T(8,128)(2,1)S(1)} %get-tuple-element.77), channel_id=1, source_target_pairs={{4,8},{6,10},{8,4},{10,6},{5,9},{7,11},{9,5},{11,7},{20,24},{22,26... | collective-permute-start | bytes 884744 | tf_op jit(solution)/shard_map/ppermute | solution.py:513
  15.4 1.7 %pick.14 = (bf16[32,4608]{1,0:T(8,128)(2,1)S(1)}, bf16[32,4608]{1,0:T(8,128)(2,1)S(1)}, bf16[32,4608]{1,0:T(8,128)(2,1)S(1)}) custom-call(s32[8,128]{1,0:T(8,128)S(1)} %plan.1.table.index, bf16[10,64,4096]{2,1,0:T(8,128)(2,1)} %refs_0_.1, bf16[10,64,512]{2,1,0:T(8,128)(2,1)} %refs_1_.1, bf16[32,4608]{1,0:T(8,128)(2,1)S(1)} %collective-permute-done.5.refs_0_.refs_10_, ...), custom_call_target="tpu_custom_call" | custom-call | tf_op jit(solution)/shard_map/pick/pallas_call | solution.py:260
  18.0 2.4 %collective-permute-start.12 = (bf16[32,4608]{1,0:T(8,128)(2,1)S(1)}, bf16[32,4608]{1,0:T(8,128)(2,1)S(1)}, u32[]{:S(2)}, u32[]{:S(2)}) collective-permute-start(bf16[32,4608]{1,0:T(8,128)(2,1)S(1)} %get-tuple-element.80), channel_id=1, source_target_pairs={{4,8},{6,10},{8,4},{10,6},{5,9},{7,11},{9,5},{11,7},{20,24},{22,26... | collective-permute-start | bytes 884744 | tf_op jit(solution)/shard_map/ppermute | solution.py:513
  20.4 1.4 %collective-permute-done.9.refs_1_.refs_2_.refs_3_.refs_4_.refs_5_.refs_23_ = bf16[32,4608]{1,0:T(8,128)(2,1)S(1)} collective-permute-done((bf16[32,4608]{1,0:T(8,128)(2,1)S(1)}, bf16[32,4608]{1,0:T(8,128)(2,1)S(1)}, u32[]{:S(2)}, u32[]{:S(2)}) %collective-permute-start.9) | collective-permute-done | bytes 294944 | tf_op jit(solution)/shard_map/ppermute | solution.py:513
  21.8 7.9 %pick.15 = (bf16[32,4608]{1,0:T(8,128)(2,1)S(1)}, bf16[32,4608]{1,0:T(8,128)(2,1)S(1)}, bf16[32,4608]{1,0:T(8,128)(2,1)S(1)}, f32[1024,256]{1,0:T(8,128)S(1)}) custom-call(s32[8,128]{1,0:T(8,128)S(1)} %plan.1.table.index, bf16[10,64,4096]{2,1,0:T(8,128)(2,1)} %refs_0_.1, bf16[10,64,512]{2,1,0:T(8,128)(2,1)} %refs_1_.1, ...), custom_call_target="tpu_custom_call" | custom-call | tf_op jit(solution)/shard_map/pick/pallas_call | solution.py:260
  30.3 3.1 %collective-permute-start.15 = (bf16[32,4608]{1,0:T(8,128)(2,1)S(1)}, bf16[32,4608]{1,0:T(8,128)(2,1)S(1)}, u32[]{:S(2)}, u32[]{:S(2)}) collective-permute-start(bf16[32,4608]{1,0:T(8,128)(2,1)S(1)} %get-tuple-element.83), channel_id=1, source_target_pairs={{4,8},{6,10},{8,4},{10,6},{5,9},{7,11},{9,5},{11,7},{20,24},{22,26... | collective-permute-start | bytes 884744 | tf_op jit(solution)/shard_map/ppermute | solution.py:513
  34.3 1.4 %collective-permute-start.13 = (bf16[32,4608]{1,0:T(8,128)(2,1)S(1)}, bf16[32,4608]{1,0:T(8,128)(2,1)S(1)}, u32[]{:S(2)}, u32[]{:S(2)}) collective-permute-start(bf16[32,4608]{1,0:T(8,128)(2,1)S(1)} %get-tuple-element.81), channel_id=1, source_target_pairs={{0,2},{2,0},{4,6},{6,4},{8,10},{10,8},{12,14},{14,12},{1,3},{3,1},... | collective-permute-start | bytes 884744 | tf_op jit(solution)/shard_map/ppermute | solution.py:513
  36.0 2.9 %collective-permute-start.18 = (bf16[32,4608]{1,0:T(8,128)(2,1)S(1)}, bf16[32,4608]{1,0:T(8,128)(2,1)S(1)}, u32[]{:S(2)}, u32[]{:S(2)}) collective-permute-start(bf16[32,4608]{1,0:T(8,128)(2,1)S(1)} %get-tuple-element.86), channel_id=1, source_target_pairs={{4,8},{6,10},{8,4},{10,6},{5,9},{7,11},{9,5},{11,7},{20,24},{22,26... | collective-permute-start | bytes 884744 | tf_op jit(solution)/shard_map/ppermute | solution.py:513
  39.0 7.9 %pick.17 = (bf16[32,4608]{1,0:T(8,128)(2,1)S(1)}, bf16[32,4608]{1,0:T(8,128)(2,1)S(1)}, bf16[32,4608]{1,0:T(8,128)(2,1)S(1)}, f32[1024,256]{1,0:T(8,128)S(1)}) custom-call(s32[8,128]{1,0:T(8,128)S(1)} %plan.1.table.index, bf16[10,64,4096]{2,1,0:T(8,128)(2,1)} %refs_0_.1, bf16[10,64,512]{2,1,0:T(8,128)(2,1)} %refs_1_.1, ...), custom_call_target="tpu_custom_call" | custom-call | tf_op jit(solution)/shard_map/pick/pallas_call | solution.py:260
  47.5 3.1 %collective-permute-start.21 = (bf16[32,4608]{1,0:T(8,128)(2,1)S(1)}, bf16[32,4608]{1,0:T(8,128)(2,1)S(1)}, u32[]{:S(2)}, u32[]{:S(2)}) collective-permute-start(bf16[32,4608]{1,0:T(8,128)(2,1)S(1)} %get-tuple-element.89), channel_id=1, source_target_pairs={{4,8},{6,10},{8,4},{10,6},{5,9},{7,11},{9,5},{11,7},{20,24},{22,26... | collective-permute-start | bytes 884744 | tf_op jit(solution)/shard_map/ppermute | solution.py:513
  52.5 2.4 %collective-permute-start.25 = (bf16[32,4608]{1,0:T(8,128)(2,1)S(1)}, bf16[32,4608]{1,0:T(8,128)(2,1)S(1)}, u32[]{:S(2)}, u32[]{:S(2)}) collective-permute-start(bf16[32,4608]{1,0:T(8,128)(2,1)S(1)} %get-tuple-element.93), channel_id=1, source_target_pairs={{4,8},{6,10},{8,4},{10,6},{5,9},{7,11},{9,5},{11,7},{20,24},{22,26... | collective-permute-start | bytes 884744 | tf_op jit(solution)/shard_map/ppermute | solution.py:513
  54.9 7.9 %pick.19 = (bf16[32,4608]{1,0:T(8,128)(2,1)S(1)}, bf16[32,4608]{1,0:T(8,128)(2,1)S(1)}, bf16[32,4608]{1,0:T(8,128)(2,1)S(1)}, f32[1024,256]{1,0:T(8,128)S(1)}) custom-call(s32[8,128]{1,0:T(8,128)S(1)} %plan.1.table.index, bf16[10,64,4096]{2,1,0:T(8,128)(2,1)} %refs_0_.1, bf16[10,64,512]{2,1,0:T(8,128)(2,1)} %refs_1_.1, ...), custom_call_target="tpu_custom_call" | custom-call | tf_op jit(solution)/shard_map/pick/pallas_call | solution.py:260
  62.9 1.3 %collective-permute-start.22 = (bf16[32,4608]{1,0:T(8,128)(2,1)S(1)}, bf16[32,4608]{1,0:T(8,128)(2,1)S(1)}, u32[]{:S(2)}, u32[]{:S(2)}) collective-permute-start(bf16[32,4608]{1,0:T(8,128)(2,1)S(1)} %get-tuple-element.90), channel_id=1, source_target_pairs={{0,2},{2,0},{4,6},{6,4},{8,10},{10,8},{12,14},{14,12},{1,3},{3,1},... | collective-permute-start | bytes 884744 | tf_op jit(solution)/shard_map/ppermute | solution.py:513
  64.2 2.2 %collective-permute-start.27 = (bf16[32,4608]{1,0:T(8,128)(2,1)S(1)}, bf16[32,4608]{1,0:T(8,128)(2,1)S(1)}, u32[]{:S(2)}, u32[]{:S(2)}) collective-permute-start(bf16[32,4608]{1,0:T(8,128)(2,1)S(1)} %get-tuple-element.95), channel_id=1, source_target_pairs={{4,8},{6,10},{8,4},{10,6},{5,9},{7,11},{9,5},{11,7},{20,24},{22,26... | collective-permute-start | bytes 884744 | tf_op jit(solution)/shard_map/ppermute | solution.py:513
  67.3 3.2 %collective-permute-start.29 = (bf16[32,4608]{1,0:T(8,128)(2,1)S(1)}, bf16[32,4608]{1,0:T(8,128)(2,1)S(1)}, u32[]{:S(2)}, u32[]{:S(2)}) collective-permute-start(bf16[32,4608]{1,0:T(8,128)(2,1)S(1)} %get-tuple-element.97), channel_id=1, source_target_pairs={{4,8},{6,10},{8,4},{10,6},{5,9},{7,11},{9,5},{11,7},{20,24},{22,26... | collective-permute-start | bytes 884744 | tf_op jit(solution)/shard_map/ppermute | solution.py:513
  70.5 10.0 %collective-permute-start.36 = (f32[1024,256]{1,0:T(8,128)S(1)}, f32[1024,256]{1,0:T(8,128)S(1)}, u32[]{:S(2)}, u32[]{:S(2)}) collective-permute-start(f32[1024,256]{1,0:T(8,128)S(1)} %get-tuple-element.106), channel_id=1, source_target_pairs={{0,1},{1,0},{2,3},{3,2},{4,5},{5,4},{6,7},{7,6},{8,9},{9,8},{10,11... | collective-permute-start | bytes 3145736 | tf_op jit(solution)/shard_map/ppermute | solution.py:524
  80.6 7.9 %pick.21 = (bf16[32,4608]{1,0:T(8,128)(2,1)S(1)}, bf16[32,4608]{1,0:T(8,128)(2,1)S(1)}, f32[1024,256]{1,0:T(8,128)S(1)}) custom-call(s32[8,128]{1,0:T(8,128)S(1)} %plan.1.table.index, bf16[10,64,4096]{2,1,0:T(8,128)(2,1)} %refs_0_.1, bf16[10,64,512]{2,1,0:T(8,128)(2,1)} %refs_1_.1, bf16[32,4608]{1,0:T(8,128)(2,1)S(1)} %collective-permute-done.8.refs_0_.refs_11_, ...), custom_call_target="tpu_custom_call" | custom-call | tf_op jit(solution)/shard_map/pick/pallas_call | solution.py:260
  88.6 2.1 %collective-permute-start.31 = (bf16[32,4608]{1,0:T(8,128)(2,1)S(1)}, bf16[32,4608]{1,0:T(8,128)(2,1)S(1)}, u32[]{:S(2)}, u32[]{:S(2)}) collective-permute-start(bf16[32,4608]{1,0:T(8,128)(2,1)S(1)} %get-tuple-element.99), channel_id=1, source_target_pairs={{4,8},{6,10},{8,4},{10,6},{5,9},{7,11},{9,5},{11,7},{20,24},{22,26... | collective-permute-start | bytes 884744 | tf_op jit(solution)/shard_map/ppermute | solution.py:513
  91.7 4.5 %collective-permute-done.28.refs_4_.refs_19_ = bf16[32,4608]{1,0:T(8,128)(2,1)S(1)} collective-permute-done((bf16[32,4608]{1,0:T(8,128)(2,1)S(1)}, bf16[32,4608]{1,0:T(8,128)(2,1)S(1)}, u32[]{:S(2)}, u32[]{:S(2)}) %collective-permute-start.28) | collective-permute-done | bytes 294944 | tf_op jit(solution)/shard_map/ppermute | solution.py:513
  96.1 1.9 %collective-permute-done.31.refs_9_.refs_31_ = bf16[32,4608]{1,0:T(8,128)(2,1)S(1)} collective-permute-done((bf16[32,4608]{1,0:T(8,128)(2,1)S(1)}, bf16[32,4608]{1,0:T(8,128)(2,1)S(1)}, u32[]{:S(2)}, u32[]{:S(2)}) %collective-permute-start.31) | collective-permute-done | bytes 294944 | tf_op jit(solution)/shard_map/ppermute | solution.py:513
  98.9 1.9 %collective-permute-start.33 = (bf16[32,4608]{1,0:T(8,128)(2,1)S(1)}, bf16[32,4608]{1,0:T(8,128)(2,1)S(1)}, u32[]{:S(2)}, u32[]{:S(2)}) collective-permute-start(bf16[32,4608]{1,0:T(8,128)(2,1)S(1)} %get-tuple-element.101), channel_id=1, source_target_pairs={{4,8},{6,10},{8,4},{10,6},{5,9},{7,11},{9,5},{11,7},{20,24},{22,26... | collective-permute-start | bytes 884744 | tf_op jit(solution)/shard_map/ppermute | solution.py:513
  100.8 1.6 %collective-permute-done.30.refs_20_ = bf16[32,4608]{1,0:T(8,128)(2,1)S(1)} collective-permute-done((bf16[32,4608]{1,0:T(8,128)(2,1)S(1)}, bf16[32,4608]{1,0:T(8,128)(2,1)S(1)}, u32[]{:S(2)}, u32[]{:S(2)}) %collective-permute-start.30) | collective-permute-done | bytes 294944 | tf_op jit(solution)/shard_map/ppermute | solution.py:513
  102.5 2.0 %collective-permute-start.34 = (bf16[32,4608]{1,0:T(8,128)(2,1)S(1)}, bf16[32,4608]{1,0:T(8,128)(2,1)S(1)}, u32[]{:S(2)}, u32[]{:S(2)}) collective-permute-start(bf16[32,4608]{1,0:T(8,128)(2,1)S(1)} %get-tuple-element.102), channel_id=1, source_target_pairs={{4,8},{6,10},{8,4},{10,6},{5,9},{7,11},{9,5},{11,7},{20,24},{22,26... | collective-permute-start | bytes 884744 | tf_op jit(solution)/shard_map/ppermute | solution.py:513
  104.5 4.3 %collective-permute-done.32.refs_21_ = bf16[32,4608]{1,0:T(8,128)(2,1)S(1)} collective-permute-done((bf16[32,4608]{1,0:T(8,128)(2,1)S(1)}, bf16[32,4608]{1,0:T(8,128)(2,1)S(1)}, u32[]{:S(2)}, u32[]{:S(2)}) %collective-permute-start.32) | collective-permute-done | bytes 294944 | tf_op jit(solution)/shard_map/ppermute | solution.py:513
  108.8 3.8 %collective-permute-done.34.refs_33_ = bf16[32,4608]{1,0:T(8,128)(2,1)S(1)} collective-permute-done((bf16[32,4608]{1,0:T(8,128)(2,1)S(1)}, bf16[32,4608]{1,0:T(8,128)(2,1)S(1)}, u32[]{:S(2)}, u32[]{:S(2)}) %collective-permute-start.34) | collective-permute-done | bytes 294944 | tf_op jit(solution)/shard_map/ppermute | solution.py:513
  112.6 8.0 %codes.3 = (f32[512,128]{1,0:T(8,128)S(1)}, bf16[256,512]{1,0:T(8,128)(2,1)S(1)}, s32[1]{0:T(128)}) custom-call(s32[8,128]{1,0:T(8,128)S(1)} %plan.1.table.index, s32[8,128]{1,0:T(8,128)S(1)} %collective-permute-done.2.others, s32[1,4]{1,0:T(1,128)S(1)} %copy-done.1, bf16[1024,4096]{1,0:T(8,128)(2,1)} %tokens.1, bf16[10,64,4096]{2,1,0:T(8,128)(2,1)} %refs_0_.1, ...), custom_call_target="tpu_custom_call" | custom-call | tf_op jit(solution)/shard_map/codes/pallas_call | solution.py:397
  120.6 4.6 %collective-permute-start.35 = (f32[512,128]{1,0:T(8,128)S(1)}, f32[512,128]{1,0:T(8,128)S(1)}, u32[]{:S(2)}, u32[]{:S(2)}) collective-permute-start(f32[512,128]{1,0:T(8,128)S(1)} %get-tuple-element.104.refs_0_), channel_id=1, source_target_pairs={{0,1},{1,0},{2,3},{3,2},{4,5},{5,4},{6,7},{7,6},{8,9},{9,8},{10,11... | collective-permute-start | bytes 786440 | tf_op jit(solution)/shard_map/ppermute | solution.py:487
  126.3 2.5 %finish.3 = bf16[1024,512]{1,0:T(8,128)(2,1)} custom-call(s32[1,4]{1,0:T(1,128)S(1)} %copy-done.1, f32[512,128]{1,0:T(8,128)S(1)} %get-tuple-element.104.refs_0_, f32[512,128]{1,0:T(8,128)S(1)} %collective-permute-done.35.refs_1_, f32[1024,256]{1,0:T(8,128)S(1)} %get-tuple-element.105.refs_2_, f32[1024,256]{1,0:T(8,128)S(1)} %collective-permute-done.36.refs_3_, ...), custom_call_target="tpu_custom_call" | custom-call | tf_op jit(solution)/shard_map/finish/pallas_call | solution.py:466
  (62 shorter events, 11.3 us)
Async XLA Ops:
  3.5 7.9 %collective-permute-start.3 = (bf16[32,4608]{1,0:T(8,128)(2,1)S(1)}, bf16[32,4608]{1,0:T(8,128)(2,1)S(1)}, u32[]{:S(2)}, u32[]{:S(2)}) collective-permute-start(bf16[32,4608]{1,0:T(8,128)(2,1)S(1)} %get-tuple-element.71), channel_id=1, source_target_pairs={{0,2},{2,0},{4,6},{6,4},{8,10},{10,8},{12,14},{14,12},{1,3},{3,1},... | collective-permute-start | bytes 884744 | tf_op jit(solution)/shard_map/ppermute | solution.py:513
  4.8 9.8 %collective-permute-start.5 = (bf16[32,4608]{1,0:T(8,128)(2,1)S(1)}, bf16[32,4608]{1,0:T(8,128)(2,1)S(1)}, u32[]{:S(2)}, u32[]{:S(2)}) collective-permute-start(bf16[32,4608]{1,0:T(8,128)(2,1)S(1)} %get-tuple-element.73), channel_id=1, source_target_pairs={{0,4},{2,6},{4,0},{6,2},{8,12},{10,14},{12,8},{14,10},{1,5},{3,7},... | collective-permute-start | bytes 884744 | tf_op jit(solution)/shard_map/ppermute | solution.py:513
  5.0 10.4 %collective-permute-start.6 = (bf16[32,4608]{1,0:T(8,128)(2,1)S(1)}, bf16[32,4608]{1,0:T(8,128)(2,1)S(1)}, u32[]{:S(2)}, u32[]{:S(2)}) collective-permute-start(bf16[32,4608]{1,0:T(8,128)(2,1)S(1)} %get-tuple-element.74), channel_id=1, source_target_pairs={{4,8},{6,10},{8,4},{10,6},{5,9},{7,11},{9,5},{11,7},{20,24},{22,26... | collective-permute-start | bytes 884744 | tf_op jit(solution)/shard_map/ppermute | solution.py:513
  11.0 7.0 %collective-permute-start.4 = (bf16[32,4608]{1,0:T(8,128)(2,1)S(1)}, bf16[32,4608]{1,0:T(8,128)(2,1)S(1)}, u32[]{:S(2)}, u32[]{:S(2)}) collective-permute-start(bf16[32,4608]{1,0:T(8,128)(2,1)S(1)} %get-tuple-element.72), channel_id=1, source_target_pairs={{0,2},{2,0},{4,6},{6,4},{8,10},{10,8},{12,14},{14,12},{1,3},{3,1},... | collective-permute-start | bytes 884744 | tf_op jit(solution)/shard_map/ppermute | solution.py:513
  11.3 9.1 %collective-permute-start.8 = (bf16[32,4608]{1,0:T(8,128)(2,1)S(1)}, bf16[32,4608]{1,0:T(8,128)(2,1)S(1)}, u32[]{:S(2)}, u32[]{:S(2)}) collective-permute-start(bf16[32,4608]{1,0:T(8,128)(2,1)S(1)} %get-tuple-element.76), channel_id=1, source_target_pairs={{0,4},{2,6},{4,0},{6,2},{8,12},{10,14},{12,8},{14,10},{1,5},{3,7},... | collective-permute-start | bytes 884744 | tf_op jit(solution)/shard_map/ppermute | solution.py:513
  11.5 10.3 %collective-permute-start.9 = (bf16[32,4608]{1,0:T(8,128)(2,1)S(1)}, bf16[32,4608]{1,0:T(8,128)(2,1)S(1)}, u32[]{:S(2)}, u32[]{:S(2)}) collective-permute-start(bf16[32,4608]{1,0:T(8,128)(2,1)S(1)} %get-tuple-element.77), channel_id=1, source_target_pairs={{4,8},{6,10},{8,4},{10,6},{5,9},{7,11},{9,5},{11,7},{20,24},{22,26... | collective-permute-start | bytes 884744 | tf_op jit(solution)/shard_map/ppermute | solution.py:513
  17.0 13.3 %collective-permute-start.7 = (bf16[32,4608]{1,0:T(8,128)(2,1)S(1)}, bf16[32,4608]{1,0:T(8,128)(2,1)S(1)}, u32[]{:S(2)}, u32[]{:S(2)}) collective-permute-start(bf16[32,4608]{1,0:T(8,128)(2,1)S(1)} %get-tuple-element.75), channel_id=1, source_target_pairs={{0,2},{2,0},{4,6},{6,4},{8,10},{10,8},{12,14},{14,12},{1,3},{3,1},... | collective-permute-start | bytes 884744 | tf_op jit(solution)/shard_map/ppermute | solution.py:513
  17.7 15.8 %collective-permute-start.11 = (bf16[32,4608]{1,0:T(8,128)(2,1)S(1)}, bf16[32,4608]{1,0:T(8,128)(2,1)S(1)}, u32[]{:S(2)}, u32[]{:S(2)}) collective-permute-start(bf16[32,4608]{1,0:T(8,128)(2,1)S(1)} %get-tuple-element.79), channel_id=1, source_target_pairs={{0,4},{2,6},{4,0},{6,2},{8,12},{10,14},{12,8},{14,10},{1,5},{3,7},... | collective-permute-start | bytes 884744 | tf_op jit(solution)/shard_map/ppermute | solution.py:513
  18.0 15.5 %collective-permute-start.12 = (bf16[32,4608]{1,0:T(8,128)(2,1)S(1)}, bf16[32,4608]{1,0:T(8,128)(2,1)S(1)}, u32[]{:S(2)}, u32[]{:S(2)}) collective-permute-start(bf16[32,4608]{1,0:T(8,128)(2,1)S(1)} %get-tuple-element.80), channel_id=1, source_target_pairs={{4,8},{6,10},{8,4},{10,6},{5,9},{7,11},{9,5},{11,7},{20,24},{22,26... | collective-permute-start | bytes 884744 | tf_op jit(solution)/shard_map/ppermute | solution.py:513
  30.3 8.6 %collective-permute-start.14 = (bf16[32,4608]{1,0:T(8,128)(2,1)S(1)}, bf16[32,4608]{1,0:T(8,128)(2,1)S(1)}, u32[]{:S(2)}, u32[]{:S(2)}) collective-permute-start(bf16[32,4608]{1,0:T(8,128)(2,1)S(1)} %get-tuple-element.82), channel_id=1, source_target_pairs={{0,4},{2,6},{4,0},{6,2},{8,12},{10,14},{12,8},{14,10},{1,5},{3,7},... | collective-permute-start | bytes 884744 | tf_op jit(solution)/shard_map/ppermute | solution.py:513
  30.3 8.6 %collective-permute-start.15 = (bf16[32,4608]{1,0:T(8,128)(2,1)S(1)}, bf16[32,4608]{1,0:T(8,128)(2,1)S(1)}, u32[]{:S(2)}, u32[]{:S(2)}) collective-permute-start(bf16[32,4608]{1,0:T(8,128)(2,1)S(1)} %get-tuple-element.83), channel_id=1, source_target_pairs={{4,8},{6,10},{8,4},{10,6},{5,9},{7,11},{9,5},{11,7},{20,24},{22,26... | collective-permute-start | bytes 884744 | tf_op jit(solution)/shard_map/ppermute | solution.py:513
  34.3 13.2 %collective-permute-start.13 = (bf16[32,4608]{1,0:T(8,128)(2,1)S(1)}, bf16[32,4608]{1,0:T(8,128)(2,1)S(1)}, u32[]{:S(2)}, u32[]{:S(2)}) collective-permute-start(bf16[32,4608]{1,0:T(8,128)(2,1)S(1)} %get-tuple-element.81), channel_id=1, source_target_pairs={{0,2},{2,0},{4,6},{6,4},{8,10},{10,8},{12,14},{14,12},{1,3},{3,1},... | collective-permute-start | bytes 884744 | tf_op jit(solution)/shard_map/ppermute | solution.py:513
  35.7 14.9 %collective-permute-start.17 = (bf16[32,4608]{1,0:T(8,128)(2,1)S(1)}, bf16[32,4608]{1,0:T(8,128)(2,1)S(1)}, u32[]{:S(2)}, u32[]{:S(2)}) collective-permute-start(bf16[32,4608]{1,0:T(8,128)(2,1)S(1)} %get-tuple-element.85), channel_id=1, source_target_pairs={{0,4},{2,6},{4,0},{6,2},{8,12},{10,14},{12,8},{14,10},{1,5},{3,7},... | collective-permute-start | bytes 884744 | tf_op jit(solution)/shard_map/ppermute | solution.py:513
  36.0 14.6 %collective-permute-start.18 = (bf16[32,4608]{1,0:T(8,128)(2,1)S(1)}, bf16[32,4608]{1,0:T(8,128)(2,1)S(1)}, u32[]{:S(2)}, u32[]{:S(2)}) collective-permute-start(bf16[32,4608]{1,0:T(8,128)(2,1)S(1)} %get-tuple-element.86), channel_id=1, source_target_pairs={{4,8},{6,10},{8,4},{10,6},{5,9},{7,11},{9,5},{11,7},{20,24},{22,26... | collective-permute-start | bytes 884744 | tf_op jit(solution)/shard_map/ppermute | solution.py:513
  47.5 7.5 %collective-permute-start.20 = (bf16[32,4608]{1,0:T(8,128)(2,1)S(1)}, bf16[32,4608]{1,0:T(8,128)(2,1)S(1)}, u32[]{:S(2)}, u32[]{:S(2)}) collective-permute-start(bf16[32,4608]{1,0:T(8,128)(2,1)S(1)} %get-tuple-element.88), channel_id=1, source_target_pairs={{0,4},{2,6},{4,0},{6,2},{8,12},{10,14},{12,8},{14,10},{1,5},{3,7},... | collective-permute-start | bytes 884744 | tf_op jit(solution)/shard_map/ppermute | solution.py:513
  47.5 7.5 %collective-permute-start.21 = (bf16[32,4608]{1,0:T(8,128)(2,1)S(1)}, bf16[32,4608]{1,0:T(8,128)(2,1)S(1)}, u32[]{:S(2)}, u32[]{:S(2)}) collective-permute-start(bf16[32,4608]{1,0:T(8,128)(2,1)S(1)} %get-tuple-element.89), channel_id=1, source_target_pairs={{4,8},{6,10},{8,4},{10,6},{5,9},{7,11},{9,5},{11,7},{20,24},{22,26... | collective-permute-start | bytes 884744 | tf_op jit(solution)/shard_map/ppermute | solution.py:513
  51.5 12.7 %collective-permute-start.19 = (bf16[32,4608]{1,0:T(8,128)(2,1)S(1)}, bf16[32,4608]{1,0:T(8,128)(2,1)S(1)}, u32[]{:S(2)}, u32[]{:S(2)}) collective-permute-start(bf16[32,4608]{1,0:T(8,128)(2,1)S(1)} %get-tuple-element.87), channel_id=1, source_target_pairs={{0,2},{2,0},{4,6},{6,4},{8,10},{10,8},{12,14},{14,12},{1,3},{3,1},... | collective-permute-start | bytes 884744 | tf_op jit(solution)/shard_map/ppermute | solution.py:513
  51.7 14.6 %collective-permute-start.23 = (bf16[32,4608]{1,0:T(8,128)(2,1)S(1)}, bf16[32,4608]{1,0:T(8,128)(2,1)S(1)}, u32[]{:S(2)}, u32[]{:S(2)}) collective-permute-start(bf16[32,4608]{1,0:T(8,128)(2,1)S(1)} %get-tuple-element.91), channel_id=1, source_target_pairs={{0,4},{2,6},{4,0},{6,2},{8,12},{10,14},{12,8},{14,10},{1,5},{3,7},... | collective-permute-start | bytes 884744 | tf_op jit(solution)/shard_map/ppermute | solution.py:513
  52.5 13.8 %collective-permute-start.25 = (bf16[32,4608]{1,0:T(8,128)(2,1)S(1)}, bf16[32,4608]{1,0:T(8,128)(2,1)S(1)}, u32[]{:S(2)}, u32[]{:S(2)}) collective-permute-start(bf16[32,4608]{1,0:T(8,128)(2,1)S(1)} %get-tuple-element.93), channel_id=1, source_target_pairs={{4,8},{6,10},{8,4},{10,6},{5,9},{7,11},{9,5},{11,7},{20,24},{22,26... | collective-permute-start | bytes 884744 | tf_op jit(solution)/shard_map/ppermute | solution.py:513
  62.9 7.6 %collective-permute-start.22 = (bf16[32,4608]{1,0:T(8,128)(2,1)S(1)}, bf16[32,4608]{1,0:T(8,128)(2,1)S(1)}, u32[]{:S(2)}, u32[]{:S(2)}) collective-permute-start(bf16[32,4608]{1,0:T(8,128)(2,1)S(1)} %get-tuple-element.90), channel_id=1, source_target_pairs={{0,2},{2,0},{4,6},{6,4},{8,10},{10,8},{12,14},{14,12},{1,3},{3,1},... | collective-permute-start | bytes 884744 | tf_op jit(solution)/shard_map/ppermute | solution.py:513
  64.2 16.3 %collective-permute-start.24 = (bf16[32,4608]{1,0:T(8,128)(2,1)S(1)}, bf16[32,4608]{1,0:T(8,128)(2,1)S(1)}, u32[]{:S(2)}, u32[]{:S(2)}) collective-permute-start(bf16[32,4608]{1,0:T(8,128)(2,1)S(1)} %get-tuple-element.92), channel_id=1, source_target_pairs={{0,4},{2,6},{4,0},{6,2},{8,12},{10,14},{12,8},{14,10},{1,5},{3,7},... | collective-permute-start | bytes 884744 | tf_op jit(solution)/shard_map/ppermute | solution.py:513
  64.2 16.4 %collective-permute-start.27 = (bf16[32,4608]{1,0:T(8,128)(2,1)S(1)}, bf16[32,4608]{1,0:T(8,128)(2,1)S(1)}, u32[]{:S(2)}, u32[]{:S(2)}) collective-permute-start(bf16[32,4608]{1,0:T(8,128)(2,1)S(1)} %get-tuple-element.95), channel_id=1, source_target_pairs={{4,8},{6,10},{8,4},{10,6},{5,9},{7,11},{9,5},{11,7},{20,24},{22,26... | collective-permute-start | bytes 884744 | tf_op jit(solution)/shard_map/ppermute | solution.py:513
  67.2 21.4 %collective-permute-start.26 = (bf16[32,4608]{1,0:T(8,128)(2,1)S(1)}, bf16[32,4608]{1,0:T(8,128)(2,1)S(1)}, u32[]{:S(2)}, u32[]{:S(2)}) collective-permute-start(bf16[32,4608]{1,0:T(8,128)(2,1)S(1)} %get-tuple-element.94), channel_id=1, source_target_pairs={{0,4},{2,6},{4,0},{6,2},{8,12},{10,14},{12,8},{14,10},{1,5},{3,7},... | collective-permute-start | bytes 884744 | tf_op jit(solution)/shard_map/ppermute | solution.py:513
  67.3 23.5 %collective-permute-start.29 = (bf16[32,4608]{1,0:T(8,128)(2,1)S(1)}, bf16[32,4608]{1,0:T(8,128)(2,1)S(1)}, u32[]{:S(2)}, u32[]{:S(2)}) collective-permute-start(bf16[32,4608]{1,0:T(8,128)(2,1)S(1)} %get-tuple-element.97), channel_id=1, source_target_pairs={{4,8},{6,10},{8,4},{10,6},{5,9},{7,11},{9,5},{11,7},{20,24},{22,26... | collective-permute-start | bytes 884744 | tf_op jit(solution)/shard_map/ppermute | solution.py:513
  70.5 55.3 %collective-permute-start.36 = (f32[1024,256]{1,0:T(8,128)S(1)}, f32[1024,256]{1,0:T(8,128)S(1)}, u32[]{:S(2)}, u32[]{:S(2)}) collective-permute-start(f32[1024,256]{1,0:T(8,128)S(1)} %get-tuple-element.106), channel_id=1, source_target_pairs={{0,1},{1,0},{2,3},{3,2},{4,5},{5,4},{6,7},{7,6},{8,9},{9,8},{10,11... | collective-permute-start | bytes 3145736 | tf_op jit(solution)/shard_map/ppermute | solution.py:524
  80.5 45.3 %collective-permute-start.37 = (f32[1024,256]{1,0:T(8,128)S(1)}, f32[1024,256]{1,0:T(8,128)S(1)}, u32[]{:S(2)}, u32[]{:S(2)}) collective-permute-start(f32[1024,256]{1,0:T(8,128)S(1)} %get-tuple-element.108), channel_id=1, source_target_pairs={{0,1},{1,0},{2,3},{3,2},{4,5},{5,4},{6,7},{7,6},{8,9},{9,8},{10,11... | collective-permute-start | bytes 3145736 | tf_op jit(solution)/shard_map/ppermute | solution.py:524
  88.5 7.6 %collective-permute-start.28 = (bf16[32,4608]{1,0:T(8,128)(2,1)S(1)}, bf16[32,4608]{1,0:T(8,128)(2,1)S(1)}, u32[]{:S(2)}, u32[]{:S(2)}) collective-permute-start(bf16[32,4608]{1,0:T(8,128)(2,1)S(1)} %get-tuple-element.96), channel_id=1, source_target_pairs={{0,4},{2,6},{4,0},{6,2},{8,12},{10,14},{12,8},{14,10},{1,5},{3,7},... | collective-permute-start | bytes 884744 | tf_op jit(solution)/shard_map/ppermute | solution.py:513
  88.6 9.5 %collective-permute-start.31 = (bf16[32,4608]{1,0:T(8,128)(2,1)S(1)}, bf16[32,4608]{1,0:T(8,128)(2,1)S(1)}, u32[]{:S(2)}, u32[]{:S(2)}) collective-permute-start(bf16[32,4608]{1,0:T(8,128)(2,1)S(1)} %get-tuple-element.99), channel_id=1, source_target_pairs={{4,8},{6,10},{8,4},{10,6},{5,9},{7,11},{9,5},{11,7},{20,24},{22,26... | collective-permute-start | bytes 884744 | tf_op jit(solution)/shard_map/ppermute | solution.py:513
  91.5 11.0 %collective-permute-start.30 = (bf16[32,4608]{1,0:T(8,128)(2,1)S(1)}, bf16[32,4608]{1,0:T(8,128)(2,1)S(1)}, u32[]{:S(2)}, u32[]{:S(2)}) collective-permute-start(bf16[32,4608]{1,0:T(8,128)(2,1)S(1)} %get-tuple-element.98), channel_id=1, source_target_pairs={{0,4},{2,6},{4,0},{6,2},{8,12},{10,14},{12,8},{14,10},{1,5},{3,7},... | collective-permute-start | bytes 884744 | tf_op jit(solution)/shard_map/ppermute | solution.py:513
  98.8 10.0 %collective-permute-start.32 = (bf16[32,4608]{1,0:T(8,128)(2,1)S(1)}, bf16[32,4608]{1,0:T(8,128)(2,1)S(1)}, u32[]{:S(2)}, u32[]{:S(2)}) collective-permute-start(bf16[32,4608]{1,0:T(8,128)(2,1)S(1)} %get-tuple-element.100), channel_id=1, source_target_pairs={{0,4},{2,6},{4,0},{6,2},{8,12},{10,14},{12,8},{14,10},{1,5},{3,7},... | collective-permute-start | bytes 884744 | tf_op jit(solution)/shard_map/ppermute | solution.py:513
  98.9 9.9 %collective-permute-start.33 = (bf16[32,4608]{1,0:T(8,128)(2,1)S(1)}, bf16[32,4608]{1,0:T(8,128)(2,1)S(1)}, u32[]{:S(2)}, u32[]{:S(2)}) collective-permute-start(bf16[32,4608]{1,0:T(8,128)(2,1)S(1)} %get-tuple-element.101), channel_id=1, source_target_pairs={{4,8},{6,10},{8,4},{10,6},{5,9},{7,11},{9,5},{11,7},{20,24},{22,26... | collective-permute-start | bytes 884744 | tf_op jit(solution)/shard_map/ppermute | solution.py:513
  102.5 10.1 %collective-permute-start.34 = (bf16[32,4608]{1,0:T(8,128)(2,1)S(1)}, bf16[32,4608]{1,0:T(8,128)(2,1)S(1)}, u32[]{:S(2)}, u32[]{:S(2)}) collective-permute-start(bf16[32,4608]{1,0:T(8,128)(2,1)S(1)} %get-tuple-element.102), channel_id=1, source_target_pairs={{4,8},{6,10},{8,4},{10,6},{5,9},{7,11},{9,5},{11,7},{20,24},{22,26... | collective-permute-start | bytes 884744 | tf_op jit(solution)/shard_map/ppermute | solution.py:513
  (7 other events, 97.1 us)
where the time goes:
time: 129 us
  starting transfers between devices  54.4 us (42%)
  Pallas kernels  53 us (41%)
  waiting for transfers between devices  20.3 us (16%)
    pallas_call x12, Pallas kernels, pick(): pl.pallas_call(functools.partial(pick_kernel, step, size, lo, streams, he...  40.7 us
    ppermute x32, starting transfers between devices, route(): got[part][stream].append(lax.ppermute(send, 'dp', pairs))  39.7 us
    ppermute x32, waiting for transfers between devices, route(): got[part][stream].append(lax.ppermute(send, 'dp', pairs))  19.8 us
    ppermute x2, starting transfers between devices, sent_on(): return lax.ppermute(part, 'tensor', pairs)  10.1 us
    pallas_call x1, Pallas kernels, codes(): pl.pallas_call(functools.partial(code_kernel, count, kinds, routed), grid...  7.99 us
    ppermute x2, starting transfers between devices, gathered(): lax.ppermute(part, axis, [(i, (i + step) % size) for i in range(size)])  4.55 us
  transfers between devices with their start and end apart: 36, of which 12 were waited for; matrix products, arithmetic and copies ran while one was open for 0% of the time, Pallas kernels for 36%

commit v1 on v0

--- a/solution.py
+++ b/solution.py
@@ -301,6 +301,24 @@
         name="pick_all",
     )(index, in_hbm(down_pool), in_hbm(up_pool))
     return lax.all_to_all(send, "dp", split_axis=0, concat_axis=0, tiled=True)
+
+
+def stage_kernel(source, out, sem):
+    copy = pltpu.make_async_copy(source, out, sem)
+    copy.start()
+    copy.wait()
+
+
+def stage(x):
+    return pl.pallas_call(
+        stage_kernel,
+        in_specs=[ANY],
+        out_specs=VMEM,
+        out_shape=pltpu.VMEM(x.shape, x.dtype),
+        scratch_shapes=[pltpu.SemaphoreType.DMA],
+        compiler_params=pltpu.CompilerParams(vmem_limit_bytes=4 * MIB),
+        name="stage",
+    )(in_hbm(x))
 
 
 def request_of_rows(lengths, count, first, rows):
@@ -542,13 +560,14 @@
     if not (routable and rank % 32 == 0 and adapter_ids.shape[1] == 4):
         return by_all_to_all()
     table = plan(held, adapter_ids, owner_map)
-    got, done = route(table, down_pool, up_pool, n_dp, tokens, key_weight)
+    at_hand = stage(tokens)
+    got, done = route(table, down_pool, up_pool, n_dp, at_hand, key_weight)
     base = [[here, sent_on(there, 1)] for there, here in zip(done[:2], done[2:])]
     others = gathered(table, "groups", n_groups)[-1]
     sources = [("pool", (in_hbm(down_pool), in_hbm(up_pool)))]
     for stream in (2, 0, 1):
         sources += [("block", pair) for pair in zip(got[0][stream], got[1][stream])]
-    code, up, misfit = codes(table, others, lengths, tokens, sources, rank, columns)
+    code, up, misfit = codes(table, others, lengths, at_hand, sources, rank, columns)
     keys = finish(lengths, gathered(code, "tensor", n_tensor), base, up)
     return lax.cond(misfit[0] == 0, lambda: keys, by_all_to_all)
 

time: 129 us -> 115 us (0.89)
  Pallas kernels: 53 us -> 40.7 us
  waiting for transfers between devices: 20.3 us -> 15.3 us
  starting transfers between devices: 54.4 us -> 56.6 us
    pallas_call x12, Pallas kernels: 40.7 us -> 28.3 us  [pick(): pl.pallas_call(functools.partial(pick_kernel, step, size, lo, streams, he...]
    ppermute x32, waiting for transfers between devices: 19.8 us -> 14.8 us  [route(): got[part][stream].append(lax.ppermute(send, 'dp', pairs))]
    pallas_call x0 -> x1, Pallas kernels: none -> 3.39 us  [stage(): pl.pallas_call(stage_kernel, in_specs=[ANY], out_specs=VMEM, out_shape=pl...]
    pallas_call x1, Pallas kernels: 7.99 us -> 4.69 us  [codes(): pl.pallas_call(functools.partial(code_kernel, count, kinds, routed), grid...]
    ppermute x32, starting transfers between devices: 39.7 us -> 42 us  [route(): got[part][stream].append(lax.ppermute(send, 'dp', pairs))]
    ppermute x2, starting transfers between devices: 10.1 us -> 8.27 us  [sent_on(): return lax.ppermute(part, 'tensor', pairs)]
    ppermute x2, starting transfers between devices: 4.55 us -> 6.3 us  [gathered(): lax.ppermute(part, axis, [(i, (i + step) % size) for i in range(size)])]
  transfers between devices with their start and end apart: 36 -> 36, of which waited for: 12 -> 13; matrix products, arithmetic and copies ran while one was open for 0% -> 0% of each run, Pallas kernels for 36% -> 31%
where the time goes in v1:
time: 115 us; the launch traced here: 114 us
  starting transfers between devices  56.6 us (49%)
  Pallas kernels  40.7 us (35%)
  waiting for transfers between devices  15.3 us (13%)
  between operations  1.23 us (1%)
    ppermute x32, starting transfers between devices, route(): got[part][stream].append(lax.ppermute(send, 'dp', pairs))  42 us
    pallas_call x12, Pallas kernels, pick(): pl.pallas_call(functools.partial(pick_kernel, step, size, lo, streams, he...  28.3 us
    ppermute x32, waiting for transfers between devices, route(): got[part][stream].append(lax.ppermute(send, 'dp', pairs))  14.8 us
    ppermute x2, starting transfers between devices, sent_on(): return lax.ppermute(part, 'tensor', pairs)  8.27 us
    ppermute x2, starting transfers between devices, gathered(): lax.ppermute(part, axis, [(i, (i + step) % size) for i in range(size)])  6.3 us
    pallas_call x1, Pallas kernels, codes(): pl.pallas_call(functools.partial(code_kernel, count, kinds, routed), grid...  4.69 us
    pallas_call x1, Pallas kernels, stage(): pl.pallas_call(stage_kernel, in_specs=[ANY], out_specs=VMEM, out_shape=pl...  3.39 us
    pallas_call x1, Pallas kernels, finish(): pl.pallas_call(functools.partial(finish_kernel, count, parts, shares, til...  2.51 us
  transfers between devices with their start and end apart: 36, of which 13 were waited for; matrix products, arithmetic and copies ran while one was open for 0% of the time, Pallas kernels for 31%

profile of v1, /device:TPU:9, one launch (start us, length us, event | category | flops | bytes accessed | tf_op | source)
XLA Modules:
  0.0 113.8 jit_solution(15992918394242515498)
XLA Ops:
  0.0 1.8 %plan.1.table.index = s32[8,128]{1,0:T(8,128)S(1)} custom-call(s32[4,8]{1,0:T(4,128)} %bitcast.20, s32[80]{0:T(128)} %owner_map.1), custom_call_target="tpu_custom_call" | custom-call | tf_op jit(solution)/shard_map/plan/pallas_call | solution.py:170
  1.8 1.7 %pick.12 = (bf16[32,4608]{1,0:T(8,128)(2,1)S(1)}, bf16[32,4608]{1,0:T(8,128)(2,1)S(1)}, bf16[32,4608]{1,0:T(8,128)(2,1)S(1)}) custom-call(s32[8,128]{1,0:T(8,128)S(1)} %plan.1.table.index, bf16[10,64,4096]{2,1,0:T(8,128)(2,1)} %refs_0_.1, bf16[10,64,512]{2,1,0:T(8,128)(2,1)} %refs_1_.1), custom_call_target="tpu_custom_call" | custom-call | tf_op jit(solution)/shard_map/pick/pallas_call | solution.py:260
  5.0 4.3 %collective-permute-start.6 = (bf16[32,4608]{1,0:T(8,128)(2,1)S(1)}, bf16[32,4608]{1,0:T(8,128)(2,1)S(1)}, u32[]{:S(2)}, u32[]{:S(2)}) collective-permute-start(bf16[32,4608]{1,0:T(8,128)(2,1)S(1)} %get-tuple-element.74), channel_id=1, source_target_pairs={{4,8},{6,10},{8,4},{10,6},{5,9},{7,11},{9,5},{11,7},{20,24},{22,26... | collective-permute-start | bytes 884744 | tf_op jit(solution)/shard_map/ppermute | solution.py:531
  9.3 1.7 %pick.13 = (bf16[32,4608]{1,0:T(8,128)(2,1)S(1)}, bf16[32,4608]{1,0:T(8,128)(2,1)S(1)}, bf16[32,4608]{1,0:T(8,128)(2,1)S(1)}) custom-call(s32[8,128]{1,0:T(8,128)S(1)} %plan.1.table.index, bf16[10,64,4096]{2,1,0:T(8,128)(2,1)} %refs_0_.1, bf16[10,64,512]{2,1,0:T(8,128)(2,1)} %refs_1_.1), custom_call_target="tpu_custom_call" | custom-call | tf_op jit(solution)/shard_map/pick/pallas_call | solution.py:260
  11.5 3.2 %collective-permute-start.9 = (bf16[32,4608]{1,0:T(8,128)(2,1)S(1)}, bf16[32,4608]{1,0:T(8,128)(2,1)S(1)}, u32[]{:S(2)}, u32[]{:S(2)}) collective-permute-start(bf16[32,4608]{1,0:T(8,128)(2,1)S(1)} %get-tuple-element.77), channel_id=1, source_target_pairs={{4,8},{6,10},{8,4},{10,6},{5,9},{7,11},{9,5},{11,7},{20,24},{22,26... | collective-permute-start | bytes 884744 | tf_op jit(solution)/shard_map/ppermute | solution.py:531
  15.4 1.7 %pick.14 = (bf16[32,4608]{1,0:T(8,128)(2,1)S(1)}, bf16[32,4608]{1,0:T(8,128)(2,1)S(1)}, bf16[32,4608]{1,0:T(8,128)(2,1)S(1)}) custom-call(s32[8,128]{1,0:T(8,128)S(1)} %plan.1.table.index, bf16[10,64,4096]{2,1,0:T(8,128)(2,1)} %refs_0_.1, bf16[10,64,512]{2,1,0:T(8,128)(2,1)} %refs_1_.1, bf16[32,4608]{1,0:T(8,128)(2,1)S(1)} %collective-permute-done.5.refs_0_.refs_10_, ...), custom_call_target="tpu_custom_call" | custom-call | tf_op jit(solution)/shard_map/pick/pallas_call | solution.py:260
  18.0 2.5 %collective-permute-start.12 = (bf16[32,4608]{1,0:T(8,128)(2,1)S(1)}, bf16[32,4608]{1,0:T(8,128)(2,1)S(1)}, u32[]{:S(2)}, u32[]{:S(2)}) collective-permute-start(bf16[32,4608]{1,0:T(8,128)(2,1)S(1)} %get-tuple-element.80), channel_id=1, source_target_pairs={{4,8},{6,10},{8,4},{10,6},{5,9},{7,11},{9,5},{11,7},{20,24},{22,26... | collective-permute-start | bytes 884744 | tf_op jit(solution)/shard_map/ppermute | solution.py:531
  20.5 3.4 %stage.1.refs_3_.refs_6_.refs_9_.refs_12_.tokens = bf16[1024,4096]{1,0:T(8,128)(2,1)S(1)} custom-call(bf16[1024,4096]{1,0:T(8,128)(2,1)} %source.1), custom_call_target="tpu_custom_call" | custom-call | tf_op jit(solution)/shard_map/stage/pallas_call | solution.py:313
  23.9 4.6 %pick.15 = (bf16[32,4608]{1,0:T(8,128)(2,1)S(1)}, bf16[32,4608]{1,0:T(8,128)(2,1)S(1)}, bf16[32,4608]{1,0:T(8,128)(2,1)S(1)}, f32[1024,256]{1,0:T(8,128)S(1)}) custom-call(s32[8,128]{1,0:T(8,128)S(1)} %plan.1.table.index, bf16[10,64,4096]{2,1,0:T(8,128)(2,1)} %refs_0_.1, bf16[10,64,512]{2,1,0:T(8,128)(2,1)} %refs_1_.1, ...), custom_call_target="tpu_custom_call" | custom-call | tf_op jit(solution)/shard_map/pick/pallas_call | solution.py:260
  28.5 1.9 %collective-permute-start.10 = (bf16[32,4608]{1,0:T(8,128)(2,1)S(1)}, bf16[32,4608]{1,0:T(8,128)(2,1)S(1)}, u32[]{:S(2)}, u32[]{:S(2)}) collective-permute-start(bf16[32,4608]{1,0:T(8,128)(2,1)S(1)} %get-tuple-element.78), channel_id=1, source_target_pairs={{0,2},{2,0},{4,6},{6,4},{8,10},{10,8},{12,14},{14,12},{1,3},{3,1},... | collective-permute-start | bytes 884744 | tf_op jit(solution)/shard_map/ppermute | solution.py:531
  30.4 1.9 %collective-permute-start.15 = (bf16[32,4608]{1,0:T(8,128)(2,1)S(1)}, bf16[32,4608]{1,0:T(8,128)(2,1)S(1)}, u32[]{:S(2)}, u32[]{:S(2)}) collective-permute-start(bf16[32,4608]{1,0:T(8,128)(2,1)S(1)} %get-tuple-element.83), channel_id=1, source_target_pairs={{4,8},{6,10},{8,4},{10,6},{5,9},{7,11},{9,5},{11,7},{20,24},{22,26... | collective-permute-start | bytes 884744 | tf_op jit(solution)/shard_map/ppermute | solution.py:531
  35.0 2.0 %collective-permute-start.18 = (bf16[32,4608]{1,0:T(8,128)(2,1)S(1)}, bf16[32,4608]{1,0:T(8,128)(2,1)S(1)}, u32[]{:S(2)}, u32[]{:S(2)}) collective-permute-start(bf16[32,4608]{1,0:T(8,128)(2,1)S(1)} %get-tuple-element.86), channel_id=1, source_target_pairs={{4,8},{6,10},{8,4},{10,6},{5,9},{7,11},{9,5},{11,7},{20,24},{22,26... | collective-permute-start | bytes 884744 | tf_op jit(solution)/shard_map/ppermute | solution.py:531
  38.2 4.6 %pick.17 = (bf16[32,4608]{1,0:T(8,128)(2,1)S(1)}, bf16[32,4608]{1,0:T(8,128)(2,1)S(1)}, bf16[32,4608]{1,0:T(8,128)(2,1)S(1)}, f32[1024,256]{1,0:T(8,128)S(1)}) custom-call(s32[8,128]{1,0:T(8,128)S(1)} %plan.1.table.index, bf16[10,64,4096]{2,1,0:T(8,128)(2,1)} %refs_0_.1, bf16[10,64,512]{2,1,0:T(8,128)(2,1)} %refs_1_.1, ...), custom_call_target="tpu_custom_call" | custom-call | tf_op jit(solution)/shard_map/pick/pallas_call | solution.py:260
  43.0 3.0 %collective-permute-start.21 = (bf16[32,4608]{1,0:T(8,128)(2,1)S(1)}, bf16[32,4608]{1,0:T(8,128)(2,1)S(1)}, u32[]{:S(2)}, u32[]{:S(2)}) collective-permute-start(bf16[32,4608]{1,0:T(8,128)(2,1)S(1)} %get-tuple-element.89), channel_id=1, source_target_pairs={{4,8},{6,10},{8,4},{10,6},{5,9},{7,11},{9,5},{11,7},{20,24},{22,26... | collective-permute-start | bytes 884744 | tf_op jit(solution)/shard_map/ppermute | solution.py:531
  48.7 2.1 %collective-permute-start.25 = (bf16[32,4608]{1,0:T(8,128)(2,1)S(1)}, bf16[32,4608]{1,0:T(8,128)(2,1)S(1)}, u32[]{:S(2)}, u32[]{:S(2)}) collective-permute-start(bf16[32,4608]{1,0:T(8,128)(2,1)S(1)} %get-tuple-element.93), channel_id=1, source_target_pairs={{4,8},{6,10},{8,4},{10,6},{5,9},{7,11},{9,5},{11,7},{20,24},{22,26... | collective-permute-start | bytes 884744 | tf_op jit(solution)/shard_map/ppermute | solution.py:531
  51.4 4.6 %pick.19 = (bf16[32,4608]{1,0:T(8,128)(2,1)S(1)}, bf16[32,4608]{1,0:T(8,128)(2,1)S(1)}, bf16[32,4608]{1,0:T(8,128)(2,1)S(1)}, f32[1024,256]{1,0:T(8,128)S(1)}) custom-call(s32[8,128]{1,0:T(8,128)S(1)} %plan.1.table.index, bf16[10,64,4096]{2,1,0:T(8,128)(2,1)} %refs_0_.1, bf16[10,64,512]{2,1,0:T(8,128)(2,1)} %refs_1_.1, ...), custom_call_target="tpu_custom_call" | custom-call | tf_op jit(solution)/shard_map/pick/pallas_call | solution.py:260
  56.0 2.0 %collective-permute-start.22 = (bf16[32,4608]{1,0:T(8,128)(2,1)S(1)}, bf16[32,4608]{1,0:T(8,128)(2,1)S(1)}, u32[]{:S(2)}, u32[]{:S(2)}) collective-permute-start(bf16[32,4608]{1,0:T(8,128)(2,1)S(1)} %get-tuple-element.90), channel_id=1, source_target_pairs={{0,2},{2,0},{4,6},{6,4},{8,10},{10,8},{12,14},{14,12},{1,3},{3,1},... | collective-permute-start | bytes 884744 | tf_op jit(solution)/shard_map/ppermute | solution.py:531
  58.0 1.9 %collective-permute-start.27 = (bf16[32,4608]{1,0:T(8,128)(2,1)S(1)}, bf16[32,4608]{1,0:T(8,128)(2,1)S(1)}, u32[]{:S(2)}, u32[]{:S(2)}) collective-permute-start(bf16[32,4608]{1,0:T(8,128)(2,1)S(1)} %get-tuple-element.95), channel_id=1, source_target_pairs={{4,8},{6,10},{8,4},{10,6},{5,9},{7,11},{9,5},{11,7},{20,24},{22,26... | collective-permute-start | bytes 884744 | tf_op jit(solution)/shard_map/ppermute | solution.py:531
  59.9 1.7 %pick.20 = (bf16[32,4608]{1,0:T(8,128)(2,1)S(1)}, bf16[32,4608]{1,0:T(8,128)(2,1)S(1)}) custom-call(s32[8,128]{1,0:T(8,128)S(1)} %plan.1.table.index, bf16[10,64,4096]{2,1,0:T(8,128)(2,1)} %refs_0_.1, bf16[10,64,512]{2,1,0:T(8,128)(2,1)} %refs_1_.1, bf16[32,4608]{1,0:T(8,128)(2,1)S(1)} %collective-permute-done.5.refs_0_.refs_10_, ...), custom_call_target="tpu_custom_call" | custom-call | tf_op jit(solution)/shard_map/pick/pallas_call | solution.py:260
  61.7 2.5 %collective-permute-start.29 = (bf16[32,4608]{1,0:T(8,128)(2,1)S(1)}, bf16[32,4608]{1,0:T(8,128)(2,1)S(1)}, u32[]{:S(2)}, u32[]{:S(2)}) collective-permute-start(bf16[32,4608]{1,0:T(8,128)(2,1)S(1)} %get-tuple-element.97), channel_id=1, source_target_pairs={{4,8},{6,10},{8,4},{10,6},{5,9},{7,11},{9,5},{11,7},{20,24},{22,26... | collective-permute-start | bytes 884744 | tf_op jit(solution)/shard_map/ppermute | solution.py:531
  64.2 8.2 %collective-permute-start.36 = (f32[1024,256]{1,0:T(8,128)S(1)}, f32[1024,256]{1,0:T(8,128)S(1)}, u32[]{:S(2)}, u32[]{:S(2)}) collective-permute-start(f32[1024,256]{1,0:T(8,128)S(1)} %get-tuple-element.106), channel_id=1, source_target_pairs={{0,1},{1,0},{2,3},{3,2},{4,5},{5,4},{6,7},{7,6},{8,9},{9,8},{10,11... | collective-permute-start | bytes 3145736 | tf_op jit(solution)/shard_map/ppermute | solution.py:542
  72.5 4.6 %pick.21 = (bf16[32,4608]{1,0:T(8,128)(2,1)S(1)}, bf16[32,4608]{1,0:T(8,128)(2,1)S(1)}, f32[1024,256]{1,0:T(8,128)S(1)}) custom-call(s32[8,128]{1,0:T(8,128)S(1)} %plan.1.table.index, bf16[10,64,4096]{2,1,0:T(8,128)(2,1)} %refs_0_.1, bf16[10,64,512]{2,1,0:T(8,128)(2,1)} %refs_1_.1, bf16[32,4608]{1,0:T(8,128)(2,1)S(1)} %collective-permute-done.8.refs_0_.refs_11_, ...), custom_call_target="tpu_custom_call" | custom-call | tf_op jit(solution)/shard_map/pick/pallas_call | solution.py:260
  77.4 3.2 %collective-permute-start.31 = (bf16[32,4608]{1,0:T(8,128)(2,1)S(1)}, bf16[32,4608]{1,0:T(8,128)(2,1)S(1)}, u32[]{:S(2)}, u32[]{:S(2)}) collective-permute-start(bf16[32,4608]{1,0:T(8,128)(2,1)S(1)} %get-tuple-element.99), channel_id=1, source_target_pairs={{4,8},{6,10},{8,4},{10,6},{5,9},{7,11},{9,5},{11,7},{20,24},{22,26... | collective-permute-start | bytes 884744 | tf_op jit(solution)/shard_map/ppermute | solution.py:531
  81.5 2.2 %collective-permute-done.28.refs_4_.refs_19_ = bf16[32,4608]{1,0:T(8,128)(2,1)S(1)} collective-permute-done((bf16[32,4608]{1,0:T(8,128)(2,1)S(1)}, bf16[32,4608]{1,0:T(8,128)(2,1)S(1)}, u32[]{:S(2)}, u32[]{:S(2)}) %collective-permute-start.28) | collective-permute-done | bytes 294944 | tf_op jit(solution)/shard_map/ppermute | solution.py:531
  83.7 2.1 %collective-permute-start.2 = (s32[8,128]{1,0:T(8,128)S(1)}, s32[8,128]{1,0:T(8,128)S(1)}, u32[]{:S(2)}, u32[]{:S(2)}) collective-permute-start(s32[8,128]{1,0:T(8,128)S(1)} %plan.1.table.index), channel_id=1, source_target_pairs={{0,16},{16,0},{1,17},{17,1},{2,18},{18,2},{3,19},{19,3},{4,20},{20... | collective-permute-start | bytes 12296 | tf_op jit(solution)/shard_map/ppermute | solution.py:505
  86.4 3.0 %collective-permute-start.33 = (bf16[32,4608]{1,0:T(8,128)(2,1)S(1)}, bf16[32,4608]{1,0:T(8,128)(2,1)S(1)}, u32[]{:S(2)}, u32[]{:S(2)}) collective-permute-start(bf16[32,4608]{1,0:T(8,128)(2,1)S(1)} %get-tuple-element.101), channel_id=1, source_target_pairs={{4,8},{6,10},{8,4},{10,6},{5,9},{7,11},{9,5},{11,7},{20,24},{22,26... | collective-permute-start | bytes 884744 | tf_op jit(solution)/shard_map/ppermute | solution.py:531
  90.6 3.4 %collective-permute-start.34 = (bf16[32,4608]{1,0:T(8,128)(2,1)S(1)}, bf16[32,4608]{1,0:T(8,128)(2,1)S(1)}, u32[]{:S(2)}, u32[]{:S(2)}) collective-permute-start(bf16[32,4608]{1,0:T(8,128)(2,1)S(1)} %get-tuple-element.102), channel_id=1, source_target_pairs={{4,8},{6,10},{8,4},{10,6},{5,9},{7,11},{9,5},{11,7},{20,24},{22,26... | collective-permute-start | bytes 884744 | tf_op jit(solution)/shard_map/ppermute | solution.py:531
  93.9 2.2 %collective-permute-done.32.refs_21_ = bf16[32,4608]{1,0:T(8,128)(2,1)S(1)} collective-permute-done((bf16[32,4608]{1,0:T(8,128)(2,1)S(1)}, bf16[32,4608]{1,0:T(8,128)(2,1)S(1)}, u32[]{:S(2)}, u32[]{:S(2)}) %collective-permute-start.32) | collective-permute-done | bytes 294944 | tf_op jit(solution)/shard_map/ppermute | solution.py:531
  96.1 4.9 %collective-permute-done.34.refs_33_ = bf16[32,4608]{1,0:T(8,128)(2,1)S(1)} collective-permute-done((bf16[32,4608]{1,0:T(8,128)(2,1)S(1)}, bf16[32,4608]{1,0:T(8,128)(2,1)S(1)}, u32[]{:S(2)}, u32[]{:S(2)}) %collective-permute-start.34) | collective-permute-done | bytes 294944 | tf_op jit(solution)/shard_map/ppermute | solution.py:531
  101.0 4.7 %codes.3 = (f32[512,128]{1,0:T(8,128)S(1)}, bf16[256,512]{1,0:T(8,128)(2,1)S(1)}, s32[1]{0:T(128)}) custom-call(s32[8,128]{1,0:T(8,128)S(1)} %plan.1.table.index, s32[8,128]{1,0:T(8,128)S(1)} %collective-permute-done.2.others, s32[1,4]{1,0:T(1,128)S(1)} %copy-done.1, bf16[1024,4096]{1,0:T(8,128)(2,1)S(1)} %stage.1.refs_3_.refs_6_.refs_9_.refs_12_.tokens, ...), custom_call_target="tpu_custom_call" | custom-call | tf_op jit(solution)/shard_map/codes/pallas_call | solution.py:415
  105.7 4.3 %collective-permute-start.35 = (f32[512,128]{1,0:T(8,128)S(1)}, f32[512,128]{1,0:T(8,128)S(1)}, u32[]{:S(2)}, u32[]{:S(2)}) collective-permute-start(f32[512,128]{1,0:T(8,128)S(1)} %get-tuple-element.104.refs_0_), channel_id=1, source_target_pairs={{0,1},{1,0},{2,3},{3,2},{4,5},{5,4},{6,7},{7,6},{8,9},{9,8},{10,11... | collective-permute-start | bytes 786440 | tf_op jit(solution)/shard_map/ppermute | solution.py:505
  111.1 2.5 %finish.3 = bf16[1024,512]{1,0:T(8,128)(2,1)} custom-call(s32[1,4]{1,0:T(1,128)S(1)} %copy-done.1, f32[512,128]{1,0:T(8,128)S(1)} %get-tuple-element.104.refs_0_, f32[512,128]{1,0:T(8,128)S(1)} %collective-permute-done.35.refs_1_, f32[1024,256]{1,0:T(8,128)S(1)} %get-tuple-element.105.refs_2_, f32[1024,256]{1,0:T(8,128)S(1)} %collective-permute-done.36.refs_3_, ...), custom_call_target="tpu_custom_call" | custom-call | tf_op jit(solution)/shard_map/finish/pallas_call | solution.py:484
  (63 shorter events, 14.4 us)
Async XLA Ops:
  3.5 7.9 %collective-permute-start.3 = (bf16[32,4608]{1,0:T(8,128)(2,1)S(1)}, bf16[32,4608]{1,0:T(8,128)(2,1)S(1)}, u32[]{:S(2)}, u32[]{:S(2)}) collective-permute-start(bf16[32,4608]{1,0:T(8,128)(2,1)S(1)} %get-tuple-element.71), channel_id=1, source_target_pairs={{0,2},{2,0},{4,6},{6,4},{8,10},{10,8},{12,14},{14,12},{1,3},{3,1},... | collective-permute-start | bytes 884744 | tf_op jit(solution)/shard_map/ppermute | solution.py:531
  4.9 9.8 %collective-permute-start.5 = (bf16[32,4608]{1,0:T(8,128)(2,1)S(1)}, bf16[32,4608]{1,0:T(8,128)(2,1)S(1)}, u32[]{:S(2)}, u32[]{:S(2)}) collective-permute-start(bf16[32,4608]{1,0:T(8,128)(2,1)S(1)} %get-tuple-element.73), channel_id=1, source_target_pairs={{0,4},{2,6},{4,0},{6,2},{8,12},{10,14},{12,8},{14,10},{1,5},{3,7},... | collective-permute-start | bytes 884744 | tf_op jit(solution)/shard_map/ppermute | solution.py:531
  5.0 10.4 %collective-permute-start.6 = (bf16[32,4608]{1,0:T(8,128)(2,1)S(1)}, bf16[32,4608]{1,0:T(8,128)(2,1)S(1)}, u32[]{:S(2)}, u32[]{:S(2)}) collective-permute-start(bf16[32,4608]{1,0:T(8,128)(2,1)S(1)} %get-tuple-element.74), channel_id=1, source_target_pairs={{4,8},{6,10},{8,4},{10,6},{5,9},{7,11},{9,5},{11,7},{20,24},{22,26... | collective-permute-start | bytes 884744 | tf_op jit(solution)/shard_map/ppermute | solution.py:531
  11.0 7.0 %collective-permute-start.4 = (bf16[32,4608]{1,0:T(8,128)(2,1)S(1)}, bf16[32,4608]{1,0:T(8,128)(2,1)S(1)}, u32[]{:S(2)}, u32[]{:S(2)}) collective-permute-start(bf16[32,4608]{1,0:T(8,128)(2,1)S(1)} %get-tuple-element.72), channel_id=1, source_target_pairs={{0,2},{2,0},{4,6},{6,4},{8,10},{10,8},{12,14},{14,12},{1,3},{3,1},... | collective-permute-start | bytes 884744 | tf_op jit(solution)/shard_map/ppermute | solution.py:531
  11.4 12.5 %collective-permute-start.8 = (bf16[32,4608]{1,0:T(8,128)(2,1)S(1)}, bf16[32,4608]{1,0:T(8,128)(2,1)S(1)}, u32[]{:S(2)}, u32[]{:S(2)}) collective-permute-start(bf16[32,4608]{1,0:T(8,128)(2,1)S(1)} %get-tuple-element.76), channel_id=1, source_target_pairs={{0,4},{2,6},{4,0},{6,2},{8,12},{10,14},{12,8},{14,10},{1,5},{3,7},... | collective-permute-start | bytes 884744 | tf_op jit(solution)/shard_map/ppermute | solution.py:531
  11.5 12.5 %collective-permute-start.9 = (bf16[32,4608]{1,0:T(8,128)(2,1)S(1)}, bf16[32,4608]{1,0:T(8,128)(2,1)S(1)}, u32[]{:S(2)}, u32[]{:S(2)}) collective-permute-start(bf16[32,4608]{1,0:T(8,128)(2,1)S(1)} %get-tuple-element.77), channel_id=1, source_target_pairs={{4,8},{6,10},{8,4},{10,6},{5,9},{7,11},{9,5},{11,7},{20,24},{22,26... | collective-permute-start | bytes 884744 | tf_op jit(solution)/shard_map/ppermute | solution.py:531
  17.1 13.3 %collective-permute-start.7 = (bf16[32,4608]{1,0:T(8,128)(2,1)S(1)}, bf16[32,4608]{1,0:T(8,128)(2,1)S(1)}, u32[]{:S(2)}, u32[]{:S(2)}) collective-permute-start(bf16[32,4608]{1,0:T(8,128)(2,1)S(1)} %get-tuple-element.75), channel_id=1, source_target_pairs={{0,2},{2,0},{4,6},{6,4},{8,10},{10,8},{12,14},{14,12},{1,3},{3,1},... | collective-permute-start | bytes 884744 | tf_op jit(solution)/shard_map/ppermute | solution.py:531
  17.6 14.7 %collective-permute-start.11 = (bf16[32,4608]{1,0:T(8,128)(2,1)S(1)}, bf16[32,4608]{1,0:T(8,128)(2,1)S(1)}, u32[]{:S(2)}, u32[]{:S(2)}) collective-permute-start(bf16[32,4608]{1,0:T(8,128)(2,1)S(1)} %get-tuple-element.79), channel_id=1, source_target_pairs={{0,4},{2,6},{4,0},{6,2},{8,12},{10,14},{12,8},{14,10},{1,5},{3,7},... | collective-permute-start | bytes 884744 | tf_op jit(solution)/shard_map/ppermute | solution.py:531
  18.0 14.3 %collective-permute-start.12 = (bf16[32,4608]{1,0:T(8,128)(2,1)S(1)}, bf16[32,4608]{1,0:T(8,128)(2,1)S(1)}, u32[]{:S(2)}, u32[]{:S(2)}) collective-permute-start(bf16[32,4608]{1,0:T(8,128)(2,1)S(1)} %get-tuple-element.80), channel_id=1, source_target_pairs={{4,8},{6,10},{8,4},{10,6},{5,9},{7,11},{9,5},{11,7},{20,24},{22,26... | collective-permute-start | bytes 884744 | tf_op jit(solution)/shard_map/ppermute | solution.py:531
  30.4 6.6 %collective-permute-start.14 = (bf16[32,4608]{1,0:T(8,128)(2,1)S(1)}, bf16[32,4608]{1,0:T(8,128)(2,1)S(1)}, u32[]{:S(2)}, u32[]{:S(2)}) collective-permute-start(bf16[32,4608]{1,0:T(8,128)(2,1)S(1)} %get-tuple-element.82), channel_id=1, source_target_pairs={{0,4},{2,6},{4,0},{6,2},{8,12},{10,14},{12,8},{14,10},{1,5},{3,7},... | collective-permute-start | bytes 884744 | tf_op jit(solution)/shard_map/ppermute | solution.py:531
  30.4 7.8 %collective-permute-start.15 = (bf16[32,4608]{1,0:T(8,128)(2,1)S(1)}, bf16[32,4608]{1,0:T(8,128)(2,1)S(1)}, u32[]{:S(2)}, u32[]{:S(2)}) collective-permute-start(bf16[32,4608]{1,0:T(8,128)(2,1)S(1)} %get-tuple-element.83), channel_id=1, source_target_pairs={{4,8},{6,10},{8,4},{10,6},{5,9},{7,11},{9,5},{11,7},{20,24},{22,26... | collective-permute-start | bytes 884744 | tf_op jit(solution)/shard_map/ppermute | solution.py:531
  33.2 9.8 %collective-permute-start.13 = (bf16[32,4608]{1,0:T(8,128)(2,1)S(1)}, bf16[32,4608]{1,0:T(8,128)(2,1)S(1)}, u32[]{:S(2)}, u32[]{:S(2)}) collective-permute-start(bf16[32,4608]{1,0:T(8,128)(2,1)S(1)} %get-tuple-element.81), channel_id=1, source_target_pairs={{0,2},{2,0},{4,6},{6,4},{8,10},{10,8},{12,14},{14,12},{1,3},{3,1},... | collective-permute-start | bytes 884744 | tf_op jit(solution)/shard_map/ppermute | solution.py:531
  34.7 11.3 %collective-permute-start.17 = (bf16[32,4608]{1,0:T(8,128)(2,1)S(1)}, bf16[32,4608]{1,0:T(8,128)(2,1)S(1)}, u32[]{:S(2)}, u32[]{:S(2)}) collective-permute-start(bf16[32,4608]{1,0:T(8,128)(2,1)S(1)} %get-tuple-element.85), channel_id=1, source_target_pairs={{0,4},{2,6},{4,0},{6,2},{8,12},{10,14},{12,8},{14,10},{1,5},{3,7},... | collective-permute-start | bytes 884744 | tf_op jit(solution)/shard_map/ppermute | solution.py:531
  35.0 11.0 %collective-permute-start.18 = (bf16[32,4608]{1,0:T(8,128)(2,1)S(1)}, bf16[32,4608]{1,0:T(8,128)(2,1)S(1)}, u32[]{:S(2)}, u32[]{:S(2)}) collective-permute-start(bf16[32,4608]{1,0:T(8,128)(2,1)S(1)} %get-tuple-element.86), channel_id=1, source_target_pairs={{4,8},{6,10},{8,4},{10,6},{5,9},{7,11},{9,5},{11,7},{20,24},{22,26... | collective-permute-start | bytes 884744 | tf_op jit(solution)/shard_map/ppermute | solution.py:531
  43.0 7.9 %collective-permute-start.20 = (bf16[32,4608]{1,0:T(8,128)(2,1)S(1)}, bf16[32,4608]{1,0:T(8,128)(2,1)S(1)}, u32[]{:S(2)}, u32[]{:S(2)}) collective-permute-start(bf16[32,4608]{1,0:T(8,128)(2,1)S(1)} %get-tuple-element.88), channel_id=1, source_target_pairs={{0,4},{2,6},{4,0},{6,2},{8,12},{10,14},{12,8},{14,10},{1,5},{3,7},... | collective-permute-start | bytes 884744 | tf_op jit(solution)/shard_map/ppermute | solution.py:531
  43.0 8.5 %collective-permute-start.21 = (bf16[32,4608]{1,0:T(8,128)(2,1)S(1)}, bf16[32,4608]{1,0:T(8,128)(2,1)S(1)}, u32[]{:S(2)}, u32[]{:S(2)}) collective-permute-start(bf16[32,4608]{1,0:T(8,128)(2,1)S(1)} %get-tuple-element.89), channel_id=1, source_target_pairs={{4,8},{6,10},{8,4},{10,6},{5,9},{7,11},{9,5},{11,7},{20,24},{22,26... | collective-permute-start | bytes 884744 | tf_op jit(solution)/shard_map/ppermute | solution.py:531
  46.8 11.2 %collective-permute-start.19 = (bf16[32,4608]{1,0:T(8,128)(2,1)S(1)}, bf16[32,4608]{1,0:T(8,128)(2,1)S(1)}, u32[]{:S(2)}, u32[]{:S(2)}) collective-permute-start(bf16[32,4608]{1,0:T(8,128)(2,1)S(1)} %get-tuple-element.87), channel_id=1, source_target_pairs={{0,2},{2,0},{4,6},{6,4},{8,10},{10,8},{12,14},{14,12},{1,3},{3,1},... | collective-permute-start | bytes 884744 | tf_op jit(solution)/shard_map/ppermute | solution.py:531
  47.4 12.5 %collective-permute-start.23 = (bf16[32,4608]{1,0:T(8,128)(2,1)S(1)}, bf16[32,4608]{1,0:T(8,128)(2,1)S(1)}, u32[]{:S(2)}, u32[]{:S(2)}) collective-permute-start(bf16[32,4608]{1,0:T(8,128)(2,1)S(1)} %get-tuple-element.91), channel_id=1, source_target_pairs={{0,4},{2,6},{4,0},{6,2},{8,12},{10,14},{12,8},{14,10},{1,5},{3,7},... | collective-permute-start | bytes 884744 | tf_op jit(solution)/shard_map/ppermute | solution.py:531
  48.7 11.2 %collective-permute-start.25 = (bf16[32,4608]{1,0:T(8,128)(2,1)S(1)}, bf16[32,4608]{1,0:T(8,128)(2,1)S(1)}, u32[]{:S(2)}, u32[]{:S(2)}) collective-permute-start(bf16[32,4608]{1,0:T(8,128)(2,1)S(1)} %get-tuple-element.93), channel_id=1, source_target_pairs={{4,8},{6,10},{8,4},{10,6},{5,9},{7,11},{9,5},{11,7},{20,24},{22,26... | collective-permute-start | bytes 884744 | tf_op jit(solution)/shard_map/ppermute | solution.py:531
  56.0 8.2 %collective-permute-start.22 = (bf16[32,4608]{1,0:T(8,128)(2,1)S(1)}, bf16[32,4608]{1,0:T(8,128)(2,1)S(1)}, u32[]{:S(2)}, u32[]{:S(2)}) collective-permute-start(bf16[32,4608]{1,0:T(8,128)(2,1)S(1)} %get-tuple-element.90), channel_id=1, source_target_pairs={{0,2},{2,0},{4,6},{6,4},{8,10},{10,8},{12,14},{14,12},{1,3},{3,1},... | collective-permute-start | bytes 884744 | tf_op jit(solution)/shard_map/ppermute | solution.py:531
  58.0 14.4 %collective-permute-start.24 = (bf16[32,4608]{1,0:T(8,128)(2,1)S(1)}, bf16[32,4608]{1,0:T(8,128)(2,1)S(1)}, u32[]{:S(2)}, u32[]{:S(2)}) collective-permute-start(bf16[32,4608]{1,0:T(8,128)(2,1)S(1)} %get-tuple-element.92), channel_id=1, source_target_pairs={{0,4},{2,6},{4,0},{6,2},{8,12},{10,14},{12,8},{14,10},{1,5},{3,7},... | collective-permute-start | bytes 884744 | tf_op jit(solution)/shard_map/ppermute | solution.py:531
  58.0 14.5 %collective-permute-start.27 = (bf16[32,4608]{1,0:T(8,128)(2,1)S(1)}, bf16[32,4608]{1,0:T(8,128)(2,1)S(1)}, u32[]{:S(2)}, u32[]{:S(2)}) collective-permute-start(bf16[32,4608]{1,0:T(8,128)(2,1)S(1)} %get-tuple-element.95), channel_id=1, source_target_pairs={{4,8},{6,10},{8,4},{10,6},{5,9},{7,11},{9,5},{11,7},{20,24},{22,26... | collective-permute-start | bytes 884744 | tf_op jit(solution)/shard_map/ppermute | solution.py:531
  61.6 15.8 %collective-permute-start.26 = (bf16[32,4608]{1,0:T(8,128)(2,1)S(1)}, bf16[32,4608]{1,0:T(8,128)(2,1)S(1)}, u32[]{:S(2)}, u32[]{:S(2)}) collective-permute-start(bf16[32,4608]{1,0:T(8,128)(2,1)S(1)} %get-tuple-element.94), channel_id=1, source_target_pairs={{0,4},{2,6},{4,0},{6,2},{8,12},{10,14},{12,8},{14,10},{1,5},{3,7},... | collective-permute-start | bytes 884744 | tf_op jit(solution)/shard_map/ppermute | solution.py:531
  61.7 18.9 %collective-permute-start.29 = (bf16[32,4608]{1,0:T(8,128)(2,1)S(1)}, bf16[32,4608]{1,0:T(8,128)(2,1)S(1)}, u32[]{:S(2)}, u32[]{:S(2)}) collective-permute-start(bf16[32,4608]{1,0:T(8,128)(2,1)S(1)} %get-tuple-element.97), channel_id=1, source_target_pairs={{4,8},{6,10},{8,4},{10,6},{5,9},{7,11},{9,5},{11,7},{20,24},{22,26... | collective-permute-start | bytes 884744 | tf_op jit(solution)/shard_map/ppermute | solution.py:531
  64.2 46.4 %collective-permute-start.36 = (f32[1024,256]{1,0:T(8,128)S(1)}, f32[1024,256]{1,0:T(8,128)S(1)}, u32[]{:S(2)}, u32[]{:S(2)}) collective-permute-start(f32[1024,256]{1,0:T(8,128)S(1)} %get-tuple-element.106), channel_id=1, source_target_pairs={{0,1},{1,0},{2,3},{3,2},{4,5},{5,4},{6,7},{7,6},{8,9},{9,8},{10,11... | collective-permute-start | bytes 3145736 | tf_op jit(solution)/shard_map/ppermute | solution.py:542
  72.4 38.2 %collective-permute-start.37 = (f32[1024,256]{1,0:T(8,128)S(1)}, f32[1024,256]{1,0:T(8,128)S(1)}, u32[]{:S(2)}, u32[]{:S(2)}) collective-permute-start(f32[1024,256]{1,0:T(8,128)S(1)} %get-tuple-element.108), channel_id=1, source_target_pairs={{0,1},{1,0},{2,3},{3,2},{4,5},{5,4},{6,7},{7,6},{8,9},{9,8},{10,11... | collective-permute-start | bytes 3145736 | tf_op jit(solution)/shard_map/ppermute | solution.py:542
  77.1 6.6 %collective-permute-start.28 = (bf16[32,4608]{1,0:T(8,128)(2,1)S(1)}, bf16[32,4608]{1,0:T(8,128)(2,1)S(1)}, u32[]{:S(2)}, u32[]{:S(2)}) collective-permute-start(bf16[32,4608]{1,0:T(8,128)(2,1)S(1)} %get-tuple-element.96), channel_id=1, source_target_pairs={{0,4},{2,6},{4,0},{6,2},{8,12},{10,14},{12,8},{14,10},{1,5},{3,7},... | collective-permute-start | bytes 884744 | tf_op jit(solution)/shard_map/ppermute | solution.py:531
  77.4 8.9 %collective-permute-start.31 = (bf16[32,4608]{1,0:T(8,128)(2,1)S(1)}, bf16[32,4608]{1,0:T(8,128)(2,1)S(1)}, u32[]{:S(2)}, u32[]{:S(2)}) collective-permute-start(bf16[32,4608]{1,0:T(8,128)(2,1)S(1)} %get-tuple-element.99), channel_id=1, source_target_pairs={{4,8},{6,10},{8,4},{10,6},{5,9},{7,11},{9,5},{11,7},{20,24},{22,26... | collective-permute-start | bytes 884744 | tf_op jit(solution)/shard_map/ppermute | solution.py:531
  81.4 9.2 %collective-permute-start.30 = (bf16[32,4608]{1,0:T(8,128)(2,1)S(1)}, bf16[32,4608]{1,0:T(8,128)(2,1)S(1)}, u32[]{:S(2)}, u32[]{:S(2)}) collective-permute-start(bf16[32,4608]{1,0:T(8,128)(2,1)S(1)} %get-tuple-element.98), channel_id=1, source_target_pairs={{0,4},{2,6},{4,0},{6,2},{8,12},{10,14},{12,8},{14,10},{1,5},{3,7},... | collective-permute-start | bytes 884744 | tf_op jit(solution)/shard_map/ppermute | solution.py:531
  83.7 6.5 %collective-permute-start.2 = (s32[8,128]{1,0:T(8,128)S(1)}, s32[8,128]{1,0:T(8,128)S(1)}, u32[]{:S(2)}, u32[]{:S(2)}) collective-permute-start(s32[8,128]{1,0:T(8,128)S(1)} %plan.1.table.index), channel_id=1, source_target_pairs={{0,16},{16,0},{1,17},{17,1},{2,18},{18,2},{3,19},{19,3},{4,20},{20... | collective-permute-start | bytes 12296 | tf_op jit(solution)/shard_map/ppermute | solution.py:505
  86.4 7.6 %collective-permute-start.33 = (bf16[32,4608]{1,0:T(8,128)(2,1)S(1)}, bf16[32,4608]{1,0:T(8,128)(2,1)S(1)}, u32[]{:S(2)}, u32[]{:S(2)}) collective-permute-start(bf16[32,4608]{1,0:T(8,128)(2,1)S(1)} %get-tuple-element.101), channel_id=1, source_target_pairs={{4,8},{6,10},{8,4},{10,6},{5,9},{7,11},{9,5},{11,7},{20,24},{22,26... | collective-permute-start | bytes 884744 | tf_op jit(solution)/shard_map/ppermute | solution.py:531
  90.6 10.4 %collective-permute-start.34 = (bf16[32,4608]{1,0:T(8,128)(2,1)S(1)}, bf16[32,4608]{1,0:T(8,128)(2,1)S(1)}, u32[]{:S(2)}, u32[]{:S(2)}) collective-permute-start(bf16[32,4608]{1,0:T(8,128)(2,1)S(1)} %get-tuple-element.102), channel_id=1, source_target_pairs={{4,8},{6,10},{8,4},{10,6},{5,9},{7,11},{9,5},{11,7},{20,24},{22,26... | collective-permute-start | bytes 884744 | tf_op jit(solution)/shard_map/ppermute | solution.py:531
  (7 other events, 93.4 us)

commit v2 on v0

--- a/solution.py
+++ b/solution.py
@@ -178,7 +178,7 @@
     )(adapter_ids.T, owner_map)
 
 
-def pick_kernel(step, size, lo, streams, held, piece, table, down, up, *refs):
+def pick_kernel(step, size, lo, streams, held, piece, staging, table, down, up, *refs):
     at = 0
     got = []
     for many in held:
@@ -187,6 +187,7 @@
     refs = list(refs[at:])
     if piece is not None:
         tokens, weight = refs.pop(0), refs.pop(0)
+        row_sem = refs.pop(-1) if staging else None
         held_weight, weight_sem = refs.pop(-2), refs.pop(-1)
         distance, shift = piece
         columns, wide = up.shape[2], held_weight.shape[1]
@@ -194,6 +195,18 @@
         first = pl.multiple_of(to * columns + shift, 128)
         load = pltpu.make_async_copy(weight.at[:, pl.ds(first, wide)], held_weight, weight_sem)
         load.start()
+        if staging:
+            at_hand, brought = refs[len(streams) + 1], []
+            tile = min(256, tokens.shape[0])
+            for at in range(0, tokens.shape[0], tile):
+                some = pl.ds(at, tile)
+                brought.append(
+                    pltpu.make_async_copy(
+                        tokens.at[some, :], at_hand.at[some, :], row_sem.at[at // tile]
+                    )
+                )
+                brought[-1].start()
+            tokens = at_hand
     outs, sem = refs[: len(streams)], refs[-1]
     slots, _, width = down.shape
     from_x, from_e, from_o = slots, slots + X_STEPS, slots + X_STEPS + Z_STEPS
@@ -225,6 +238,8 @@
         product = refs[len(streams)]
         tile = min(256, product.shape[0])
         for at in range(0, product.shape[0], tile):
+            if staging:
+                brought[at // tile].wait()
             product[at : at + tile, :] = jnp.dot(
                 tokens[at : at + tile, :],
                 held_weight[...],
@@ -238,7 +253,9 @@
             pltpu.make_async_copy(outs[i], outs[i], sem.at[i]).wait()
 
 
-def pick(step, lo, size, streams, table, down_pool, up_pool, got, piece, tokens, key_weight):
+def pick(
+    step, lo, size, streams, table, down_pool, up_pool, got, piece, staging, tokens, key_weight
+):
     many = tokens.shape[0]
     columns = up_pool.shape[2]
     wide = down_pool.shape[2] + columns
@@ -249,16 +266,20 @@
     out_shape = [pltpu.VMEM((size, wide), down_pool.dtype)] * len(streams)
     scratch = [pltpu.SemaphoreType.DMA((len(streams),))]
     if piece is not None:
-        operands += [in_vmem(tokens), in_hbm(key_weight)]
-        in_specs += [VMEM, ANY]
+        operands += [in_hbm(tokens) if staging else in_vmem(tokens), in_hbm(key_weight)]
+        in_specs += [ANY if staging else VMEM, ANY]
         out_specs.append(VMEM)
         out_shape.append(jax.ShapeDtypeStruct((many, columns // 2), jnp.float32))
         scratch += [
             pltpu.VMEM((tokens.shape[1], columns // 2), key_weight.dtype),
             pltpu.SemaphoreType.DMA,
         ]
+        if staging:
+            out_specs.append(VMEM)
+            out_shape.append(pltpu.VMEM(tokens.shape, tokens.dtype))
+            scratch.append(pltpu.SemaphoreType.DMA((-(-many // min(256, many)),)))
     outs = pl.pallas_call(
-        functools.partial(pick_kernel, step, size, lo, streams, held, piece),
+        functools.partial(pick_kernel, step, size, lo, streams, held, piece, staging),
         grid_spec=pltpu.PrefetchScalarGridSpec(
             num_scalar_prefetch=1,
             grid=(),
@@ -268,9 +289,10 @@
         ),
         out_shape=out_shape,
         compiler_params=pltpu.CompilerParams(vmem_limit_bytes=(4 if piece is None else 16) * MIB),
+        cost_estimate=pl.CostEstimate(flops=0, bytes_accessed=1024, transcendentals=0),
         name="pick",
     )(table, *operands)
-    return outs[: len(streams)], outs[len(streams) :]
+    return outs[: len(streams)], list(outs[len(streams) :])
 
 
 def dense_kernel(index, down, up, out):
@@ -488,7 +510,7 @@
     return held
 
 
-def route(table, down_pool, up_pool, n_dp, tokens, key_weight):
+def route(table, down_pool, up_pool, n_dp, tokens, key_weight, swap_plans):
     rank = down_pool.shape[1]
     size = rank // 2
     half = up_pool.shape[2] // 2
@@ -500,18 +522,24 @@
     done = []
     for step in range(Z_STEPS):
         streams = [E_TABLE, O_TABLE] + ([X_TABLE] if step < X_STEPS else [])
+        if step == Z_STEPS - 2:
+            table, others = lax.optimization_barrier((table, swap_plans(table)))
         for part in range(2):
             known = [list(arrays) for arrays in got[part]]
             piece = pieces[step - 1] if part == 1 and 1 <= step <= len(pieces) else None
+            staging = piece is not None and not done
             sends, product = pick(
                 step, part * size, size, streams, table, down_pool, up_pool, known, piece,
-                tokens, key_weight,
+                staging, tokens, key_weight,
             )
+            if staging:
+                tokens = product.pop()
             done += product
             for stream, send in zip(streams, sends):
                 pairs = (outer, middle, over_x)[stream]
                 got[part][stream].append(lax.ppermute(send, "dp", pairs))
-    return got, done
+    *theirs, got[1][0][-2] = lax.optimization_barrier((*done[:2], got[1][0][-2]))
+    return got, theirs, done[2:], others, tokens
 
 
 def shards(sizes, tokens, key_weight, down_pool, up_pool, adapter_ids, lengths, owner_map):
@@ -542,13 +570,18 @@
     if not (routable and rank % 32 == 0 and adapter_ids.shape[1] == 4):
         return by_all_to_all()
     table = plan(held, adapter_ids, owner_map)
-    got, done = route(table, down_pool, up_pool, n_dp, tokens, key_weight)
-    base = [[here, sent_on(there, 1)] for there, here in zip(done[:2], done[2:])]
-    others = gathered(table, "groups", n_groups)[-1]
+
+    def swap_plans(table):
+        return gathered(table, "groups", n_groups)[-1]
+
+    got, theirs, mine, others, at_hand = route(
+        table, down_pool, up_pool, n_dp, tokens, key_weight, swap_plans
+    )
+    base = [[here, sent_on(there, 1)] for here, there in zip(mine, theirs)]
     sources = [("pool", (in_hbm(down_pool), in_hbm(up_pool)))]
     for stream in (2, 0, 1):
         sources += [("block", pair) for pair in zip(got[0][stream], got[1][stream])]
-    code, up, misfit = codes(table, others, lengths, tokens, sources, rank, columns)
+    code, up, misfit = codes(table, others, lengths, at_hand, sources, rank, columns)
     keys = finish(lengths, gathered(code, "tensor", n_tensor), base, up)
     return lax.cond(misfit[0] == 0, lambda: keys, by_all_to_all)
 

time: 129 us -> 120 us (0.930)
  Pallas kernels: 53 us -> 42.6 us
  starting transfers between devices: 54.4 us -> 47 us
  waiting for transfers between devices: 20.3 us -> 27.3 us
    pallas_call x12, Pallas kernels: 40.7 us -> 33.4 us  [pick(): pl.pallas_call(functools.partial(pick_kernel, step, size, lo, streams, he...]
    ppermute x32, waiting for transfers between devices: 19.8 us -> 26.5 us  [route(): got[part][stream].append(lax.ppermute(send, 'dp', pairs))]
    ppermute x2, starting transfers between devices: 10.1 us -> 7.01 us  [sent_on(): return lax.ppermute(part, 'tensor', pairs)]
    pallas_call x1, Pallas kernels: 7.99 us -> 4.99 us  [codes(): pl.pallas_call(functools.partial(code_kernel, count, kinds, routed), grid...]
    ppermute x32, starting transfers between devices: 39.7 us -> 37 us  [route(): got[part][stream].append(lax.ppermute(send, 'dp', pairs))]
    ppermute x2, starting transfers between devices: 4.55 us -> 2.98 us  [gathered(): lax.ppermute(part, axis, [(i, (i + step) % size) for i in range(size)])]
  transfers between devices with their start and end apart: 36 -> 36, of which waited for: 12 -> 17; matrix products, arithmetic and copies ran while one was open for 0% -> 0% of each run, Pallas kernels for 36% -> 31%
where the time goes in v2:
time: 120 us; the launch traced here: 119 us
  starting transfers between devices  47 us (39%)
  Pallas kernels  42.6 us (36%)
  waiting for transfers between devices  27.3 us (23%)
    ppermute x32, starting transfers between devices, route(): got[part][stream].append(lax.ppermute(send, 'dp', pairs))  37 us
    pallas_call x12, Pallas kernels, pick(): pl.pallas_call(functools.partial(pick_kernel, step, size, lo, streams, he...  33.4 us
    ppermute x32, waiting for transfers between devices, route(): got[part][stream].append(lax.ppermute(send, 'dp', pairs))  26.5 us
    ppermute x2, starting transfers between devices, sent_on(): return lax.ppermute(part, 'tensor', pairs)  7.01 us
    pallas_call x1, Pallas kernels, codes(): pl.pallas_call(functools.partial(code_kernel, count, kinds, routed), grid...  4.99 us
    ppermute x2, starting transfers between devices, gathered(): lax.ppermute(part, axis, [(i, (i + step) % size) for i in range(size)])  2.98 us
    pallas_call x1, Pallas kernels, finish(): pl.pallas_call(functools.partial(finish_kernel, count, parts, shares, til...  2.44 us
  transfers between devices with their start and end apart: 36, of which 17 were waited for; matrix products, arithmetic and copies ran while one was open for 0% of the time, Pallas kernels for 31%

profile of v2, /device:TPU:9, one launch (start us, length us, event | category | flops | bytes accessed | tf_op | source)
XLA Modules:
  0.0 119.0 jit_solution(3485583880947457116)
XLA Ops:
  0.0 1.8 %plan.1.table.index = s32[8,128]{1,0:T(8,128)S(1)} custom-call(s32[4,8]{1,0:T(4,128)} %bitcast.20, s32[80]{0:T(128)} %owner_map.1), custom_call_target="tpu_custom_call" | custom-call | tf_op jit(solution)/shard_map/plan/pallas_call | solution.py:170
  1.8 1.7 %pick.12 = (bf16[32,4608]{1,0:T(8,128)(2,1)S(1)}, bf16[32,4608]{1,0:T(8,128)(2,1)S(1)}, bf16[32,4608]{1,0:T(8,128)(2,1)S(1)}) custom-call(s32[8,128]{1,0:T(8,128)S(1)} %plan.1.table.index, bf16[10,64,4096]{2,1,0:T(8,128)(2,1)} %refs_0_.1, bf16[10,64,512]{2,1,0:T(8,128)(2,1)} %refs_1_.1), custom_call_target="tpu_custom_call" | custom-call | bytes 1024 | tf_op jit(solution)/shard_map/pick/pallas_call | solution.py:281
  3.6 4.5 %collective-permute-start.4 = (bf16[32,4608]{1,0:T(8,128)(2,1)S(1)}, bf16[32,4608]{1,0:T(8,128)(2,1)S(1)}, u32[]{:S(2)}, u32[]{:S(2)}) collective-permute-start(bf16[32,4608]{1,0:T(8,128)(2,1)S(1)} %get-tuple-element.79), channel_id=1, source_target_pairs={{4,8},{6,10},{8,4},{10,6},{5,9},{7,11},{9,5},{11,7},{20,24},{22,26... | collective-permute-start | bytes 884744 | tf_op jit(solution)/shard_map/ppermute | solution.py:540
  9.2 1.7 %pick.14 = (bf16[32,4608]{1,0:T(8,128)(2,1)S(1)}, bf16[32,4608]{1,0:T(8,128)(2,1)S(1)}, bf16[32,4608]{1,0:T(8,128)(2,1)S(1)}) custom-call(s32[8,128]{1,0:T(8,128)S(1)} %plan.1.table.index, bf16[10,64,4096]{2,1,0:T(8,128)(2,1)} %refs_0_.1, bf16[10,64,512]{2,1,0:T(8,128)(2,1)} %refs_1_.1), custom_call_target="tpu_custom_call" | custom-call | bytes 1024 | tf_op jit(solution)/shard_map/pick/pallas_call | solution.py:281
  11.5 3.2 %collective-permute-start.8 = (bf16[32,4608]{1,0:T(8,128)(2,1)S(1)}, bf16[32,4608]{1,0:T(8,128)(2,1)S(1)}, u32[]{:S(2)}, u32[]{:S(2)}) collective-permute-start(bf16[32,4608]{1,0:T(8,128)(2,1)S(1)} %get-tuple-element.84), channel_id=1, source_target_pairs={{4,8},{6,10},{8,4},{10,6},{5,9},{7,11},{9,5},{11,7},{20,24},{22,26... | collective-permute-start | bytes 884744 | tf_op jit(solution)/shard_map/ppermute | solution.py:540
  15.4 9.6 %pick.13 = (bf16[32,4608]{1,0:T(8,128)(2,1)S(1)}, bf16[32,4608]{1,0:T(8,128)(2,1)S(1)}, bf16[32,4608]{1,0:T(8,128)(2,1)S(1)}, f32[1024,256]{1,0:T(8,128)S(1)}, bf16[1024,4096]{1,0:T(8,128)(2,1)S(1)}) custom-call(s32[8,128]{1,0:T(8,128)S(1)} %plan.1.table.index, bf16[10,64,4096]{2,1,0:T(8,128)(2,1)} %refs_0_.1, bf16[10,64,512]{2,1,0:T(8,128)(2,1)} %refs_1_.1, ...), custom_call_target="tpu_custom_call" | custom-call | bytes 1024 | tf_op jit(solution)/shard_map/pick/pallas_call | solution.py:281
  26.2 2.2 %collective-permute-start.15 = (bf16[32,4608]{1,0:T(8,128)(2,1)S(1)}, bf16[32,4608]{1,0:T(8,128)(2,1)S(1)}, u32[]{:S(2)}, u32[]{:S(2)}) collective-permute-start(bf16[32,4608]{1,0:T(8,128)(2,1)S(1)} %get-tuple-element.91), channel_id=1, source_target_pairs={{4,8},{6,10},{8,4},{10,6},{5,9},{7,11},{9,5},{11,7},{20,24},{22,26... | collective-permute-start | bytes 884744 | tf_op jit(solution)/shard_map/ppermute | solution.py:540
  28.5 1.7 %pick.15 = (bf16[32,4608]{1,0:T(8,128)(2,1)S(1)}, bf16[32,4608]{1,0:T(8,128)(2,1)S(1)}, bf16[32,4608]{1,0:T(8,128)(2,1)S(1)}) custom-call(s32[8,128]{1,0:T(8,128)S(1)} %plan.1.table.index, bf16[10,64,4096]{2,1,0:T(8,128)(2,1)} %refs_0_.1, bf16[10,64,512]{2,1,0:T(8,128)(2,1)} %refs_1_.1, bf16[32,4608]{1,0:T(8,128)(2,1)S(1)} %collective-permute-done.7.refs_0_.refs_10_, ...), custom_call_target="tpu_custom_call" | custom-call | bytes 1024 | tf_op jit(solution)/shard_map/pick/pallas_call | solution.py:281
  30.7 2.2 %collective-permute-start.12 = (bf16[32,4608]{1,0:T(8,128)(2,1)S(1)}, bf16[32,4608]{1,0:T(8,128)(2,1)S(1)}, u32[]{:S(2)}, u32[]{:S(2)}) collective-permute-start(bf16[32,4608]{1,0:T(8,128)(2,1)S(1)} %get-tuple-element.88), channel_id=1, source_target_pairs={{4,8},{6,10},{8,4},{10,6},{5,9},{7,11},{9,5},{11,7},{20,24},{22,26... | collective-permute-start | bytes 884744 | tf_op jit(solution)/shard_map/ppermute | solution.py:540
  34.0 4.6 %pick.17 = (bf16[32,4608]{1,0:T(8,128)(2,1)S(1)}, bf16[32,4608]{1,0:T(8,128)(2,1)S(1)}, bf16[32,4608]{1,0:T(8,128)(2,1)S(1)}, f32[1024,256]{1,0:T(8,128)S(1)}) custom-call(s32[8,128]{1,0:T(8,128)S(1)} %plan.1.table.index, bf16[10,64,4096]{2,1,0:T(8,128)(2,1)} %refs_0_.1, bf16[10,64,512]{2,1,0:T(8,128)(2,1)} %refs_1_.1, ...), custom_call_target="tpu_custom_call" | custom-call | bytes 1024 | tf_op jit(solution)/shard_map/pick/pallas_call | solution.py:281
  39.3 2.5 %collective-permute-start.21 = (bf16[32,4608]{1,0:T(8,128)(2,1)S(1)}, bf16[32,4608]{1,0:T(8,128)(2,1)S(1)}, u32[]{:S(2)}, u32[]{:S(2)}) collective-permute-start(bf16[32,4608]{1,0:T(8,128)(2,1)S(1)} %get-tuple-element.97), channel_id=1, source_target_pairs={{4,8},{6,10},{8,4},{10,6},{5,9},{7,11},{9,5},{11,7},{20,24},{22,26... | collective-permute-start | bytes 884744 | tf_op jit(solution)/shard_map/ppermute | solution.py:540
  41.8 1.8 %pick.16 = (bf16[32,4608]{1,0:T(8,128)(2,1)S(1)}, bf16[32,4608]{1,0:T(8,128)(2,1)S(1)}, bf16[32,4608]{1,0:T(8,128)(2,1)S(1)}) custom-call(s32[8,128]{1,0:T(8,128)S(1)} %plan.1.table.index, bf16[10,64,4096]{2,1,0:T(8,128)(2,1)} %refs_0_.1, bf16[10,64,512]{2,1,0:T(8,128)(2,1)} %refs_1_.1, bf16[32,4608]{1,0:T(8,128)(2,1)S(1)} %collective-permute-done.7.refs_0_.refs_10_, ...), custom_call_target="tpu_custom_call" | custom-call | bytes 1024 | tf_op jit(solution)/shard_map/pick/pallas_call | solution.py:281
  44.8 1.9 %collective-permute-start.18 = (bf16[32,4608]{1,0:T(8,128)(2,1)S(1)}, bf16[32,4608]{1,0:T(8,128)(2,1)S(1)}, u32[]{:S(2)}, u32[]{:S(2)}) collective-permute-start(bf16[32,4608]{1,0:T(8,128)(2,1)S(1)} %get-tuple-element.94), channel_id=1, source_target_pairs={{4,8},{6,10},{8,4},{10,6},{5,9},{7,11},{9,5},{11,7},{20,24},{22,26... | collective-permute-start | bytes 884744 | tf_op jit(solution)/shard_map/ppermute | solution.py:540
  46.8 2.5 %collective-permute-done.21.refs_5_.refs_6_.refs_7_.refs_27_ = bf16[32,4608]{1,0:T(8,128)(2,1)S(1)} collective-permute-done((bf16[32,4608]{1,0:T(8,128)(2,1)S(1)}, bf16[32,4608]{1,0:T(8,128)(2,1)S(1)}, u32[]{:S(2)}, u32[]{:S(2)}) %collective-permute-start.21) | collective-permute-done | bytes 294944 | tf_op jit(solution)/shard_map/ppermute | solution.py:540
  49.3 4.6 %pick.19 = (bf16[32,4608]{1,0:T(8,128)(2,1)S(1)}, bf16[32,4608]{1,0:T(8,128)(2,1)S(1)}, bf16[32,4608]{1,0:T(8,128)(2,1)S(1)}, f32[1024,256]{1,0:T(8,128)S(1)}) custom-call(s32[8,128]{1,0:T(8,128)S(1)} %plan.1.table.index, bf16[10,64,4096]{2,1,0:T(8,128)(2,1)} %refs_0_.1, bf16[10,64,512]{2,1,0:T(8,128)(2,1)} %refs_1_.1, ...), custom_call_target="tpu_custom_call" | custom-call | bytes 1024 | tf_op jit(solution)/shard_map/pick/pallas_call | solution.py:281
  55.4 2.1 %collective-permute-start.27 = (bf16[32,4608]{1,0:T(8,128)(2,1)S(1)}, bf16[32,4608]{1,0:T(8,128)(2,1)S(1)}, u32[]{:S(2)}, u32[]{:S(2)}) collective-permute-start(bf16[32,4608]{1,0:T(8,128)(2,1)S(1)} %get-tuple-element.106), channel_id=1, source_target_pairs={{4,8},{6,10},{8,4},{10,6},{5,9},{7,11},{9,5},{11,7},{20,24},{22,26... | collective-permute-start | bytes 884744 | tf_op jit(solution)/shard_map/ppermute | solution.py:540
  57.5 1.6 %collective-permute-start.2 = (s32[8,128]{1,0:T(8,128)S(1)}, s32[8,128]{1,0:T(8,128)S(1)}, u32[]{:S(2)}, u32[]{:S(2)}) collective-permute-start(s32[8,128]{1,0:T(8,128)S(1)} %plan.1.table.index), channel_id=1, source_target_pairs={{0,16},{16,0},{1,17},{17,1},{2,18},{18,2},{3,19},{19,3},{4,20},{20... | collective-permute-start | bytes 12296 | tf_op jit(solution)/shard_map/ppermute | solution.py:509
  60.6 1.6 %collective-permute-done.22.refs_11_.refs_13_.refs_9_ = bf16[32,4608]{1,0:T(8,128)(2,1)S(1)} collective-permute-done((bf16[32,4608]{1,0:T(8,128)(2,1)S(1)}, bf16[32,4608]{1,0:T(8,128)(2,1)S(1)}, u32[]{:S(2)}, u32[]{:S(2)}) %collective-permute-start.22) | collective-permute-done | bytes 294944 | tf_op jit(solution)/shard_map/ppermute | solution.py:540
  62.2 1.9 %collective-permute-start.25 = (bf16[32,4608]{1,0:T(8,128)(2,1)S(1)}, bf16[32,4608]{1,0:T(8,128)(2,1)S(1)}, u32[]{:S(2)}, u32[]{:S(2)}) collective-permute-start(bf16[32,4608]{1,0:T(8,128)(2,1)S(1)} %get-tuple-element.102), channel_id=1, source_target_pairs={{4,8},{6,10},{8,4},{10,6},{5,9},{7,11},{9,5},{11,7},{20,24},{22,26... | collective-permute-start | bytes 884744 | tf_op jit(solution)/shard_map/ppermute | solution.py:540
  65.2 4.6 %pick.21 = (bf16[32,4608]{1,0:T(8,128)(2,1)S(1)}, bf16[32,4608]{1,0:T(8,128)(2,1)S(1)}, f32[1024,256]{1,0:T(8,128)S(1)}) custom-call(s32[8,128]{1,0:T(8,128)S(1)} %plan.1.table.index, bf16[10,64,4096]{2,1,0:T(8,128)(2,1)} %refs_0_.1, bf16[10,64,512]{2,1,0:T(8,128)(2,1)} %refs_1_.1, bf16[32,4608]{1,0:T(8,128)(2,1)S(1)} %collective-permute-done.3.refs_0_.refs_11_, ...), custom_call_target="tpu_custom_call" | custom-call | bytes 1024 | tf_op jit(solution)/shard_map/pick/pallas_call | solution.py:281
  69.9 2.2 %collective-permute-done.25.refs_7_.refs_8_.refs_28_ = bf16[32,4608]{1,0:T(8,128)(2,1)S(1)} collective-permute-done((bf16[32,4608]{1,0:T(8,128)(2,1)S(1)}, bf16[32,4608]{1,0:T(8,128)(2,1)S(1)}, u32[]{:S(2)}, u32[]{:S(2)}) %collective-permute-start.25) | collective-permute-done | bytes 294944 | tf_op jit(solution)/shard_map/ppermute | solution.py:540
  73.0 1.9 %collective-permute-start.29 = (bf16[32,4608]{1,0:T(8,128)(2,1)S(1)}, bf16[32,4608]{1,0:T(8,128)(2,1)S(1)}, u32[]{:S(2)}, u32[]{:S(2)}) collective-permute-start(bf16[32,4608]{1,0:T(8,128)(2,1)S(1)} %get-tuple-element.109), channel_id=1, source_target_pairs={{4,8},{6,10},{8,4},{10,6},{5,9},{7,11},{9,5},{11,7},{20,24},{22,26... | collective-permute-start | bytes 884744 | tf_op jit(solution)/shard_map/ppermute | solution.py:540
  74.9 3.3 %collective-permute-done.28.refs_4_.refs_19_ = bf16[32,4608]{1,0:T(8,128)(2,1)S(1)} collective-permute-done((bf16[32,4608]{1,0:T(8,128)(2,1)S(1)}, bf16[32,4608]{1,0:T(8,128)(2,1)S(1)}, u32[]{:S(2)}, u32[]{:S(2)}) %collective-permute-start.28) | collective-permute-done | bytes 294944 | tf_op jit(solution)/shard_map/ppermute | solution.py:540
  78.2 7.0 %collective-permute-start.36 = (f32[1024,256]{1,0:T(8,128)S(1)}, f32[1024,256]{1,0:T(8,128)S(1)}, u32[]{:S(2)}, u32[]{:S(2)}) collective-permute-start(f32[1024,256]{1,0:T(8,128)S(1)} %get-tuple-element.118), channel_id=1, source_target_pairs={{0,1},{1,0},{2,3},{3,2},{4,5},{5,4},{6,7},{7,6},{8,9},{9,8},{10,11... | collective-permute-start | bytes 3145736 | tf_op jit(solution)/shard_map/ppermute | solution.py:552
  85.2 2.9 %collective-permute-start.31 = (bf16[32,4608]{1,0:T(8,128)(2,1)S(1)}, bf16[32,4608]{1,0:T(8,128)(2,1)S(1)}, u32[]{:S(2)}, u32[]{:S(2)}) collective-permute-start(bf16[32,4608]{1,0:T(8,128)(2,1)S(1)} %get-tuple-element.111), channel_id=1, source_target_pairs={{4,8},{6,10},{8,4},{10,6},{5,9},{7,11},{9,5},{11,7},{20,24},{22,26... | collective-permute-start | bytes 884744 | tf_op jit(solution)/shard_map/ppermute | solution.py:540
  88.9 2.5 %collective-permute-start.33 = (bf16[32,4608]{1,0:T(8,128)(2,1)S(1)}, bf16[32,4608]{1,0:T(8,128)(2,1)S(1)}, u32[]{:S(2)}, u32[]{:S(2)}) collective-permute-start(bf16[32,4608]{1,0:T(8,128)(2,1)S(1)} %get-tuple-element.113), channel_id=1, source_target_pairs={{4,8},{6,10},{8,4},{10,6},{5,9},{7,11},{9,5},{11,7},{20,24},{22,26... | collective-permute-start | bytes 884744 | tf_op jit(solution)/shard_map/ppermute | solution.py:540
  91.5 3.8 %collective-permute-done.31.refs_9_.refs_31_ = bf16[32,4608]{1,0:T(8,128)(2,1)S(1)} collective-permute-done((bf16[32,4608]{1,0:T(8,128)(2,1)S(1)}, bf16[32,4608]{1,0:T(8,128)(2,1)S(1)}, u32[]{:S(2)}, u32[]{:S(2)}) %collective-permute-start.31) | collective-permute-done | bytes 294944 | tf_op jit(solution)/shard_map/ppermute | solution.py:540
  96.1 2.7 %collective-permute-start.34 = (bf16[32,4608]{1,0:T(8,128)(2,1)S(1)}, bf16[32,4608]{1,0:T(8,128)(2,1)S(1)}, u32[]{:S(2)}, u32[]{:S(2)}) collective-permute-start(bf16[32,4608]{1,0:T(8,128)(2,1)S(1)} %get-tuple-element.114), channel_id=1, source_target_pairs={{4,8},{6,10},{8,4},{10,6},{5,9},{7,11},{9,5},{11,7},{20,24},{22,26... | collective-permute-start | bytes 884744 | tf_op jit(solution)/shard_map/ppermute | solution.py:540
  98.9 2.7 %collective-permute-done.33.refs_32_ = bf16[32,4608]{1,0:T(8,128)(2,1)S(1)} collective-permute-done((bf16[32,4608]{1,0:T(8,128)(2,1)S(1)}, bf16[32,4608]{1,0:T(8,128)(2,1)S(1)}, u32[]{:S(2)}, u32[]{:S(2)}) %collective-permute-start.33) | collective-permute-done | bytes 294944 | tf_op jit(solution)/shard_map/ppermute | solution.py:540
  102.2 5.7 %collective-permute-done.34.refs_33_ = bf16[32,4608]{1,0:T(8,128)(2,1)S(1)} collective-permute-done((bf16[32,4608]{1,0:T(8,128)(2,1)S(1)}, bf16[32,4608]{1,0:T(8,128)(2,1)S(1)}, u32[]{:S(2)}, u32[]{:S(2)}) %collective-permute-start.34) | collective-permute-done | bytes 294944 | tf_op jit(solution)/shard_map/ppermute | solution.py:540
  107.9 5.0 %codes.3 = (f32[512,128]{1,0:T(8,128)S(1)}, bf16[256,512]{1,0:T(8,128)(2,1)S(1)}, s32[1]{0:T(128)}) custom-call(s32[8,128]{1,0:T(8,128)S(1)} %plan.1.table.index, s32[8,128]{1,0:T(8,128)S(1)} %collective-permute-done.2.others, s32[1,4]{1,0:T(1,128)S(1)} %copy-done.2, bf16[1024,4096]{1,0:T(8,128)(2,1)S(1)} %get-tuple-element.81.refs_6_.refs_9_.refs_12_.tokens, ...), custom_call_target="tpu_custom_call" | custom-call | tf_op jit(solution)/shard_map/codes/pallas_call | solution.py:419
  115.5 2.4 %finish.3 = bf16[1024,512]{1,0:T(8,128)(2,1)S(1)} custom-call(s32[1,4]{1,0:T(1,128)S(1)} %copy-done.2, f32[512,128]{1,0:T(8,128)S(1)} %get-tuple-element.116.refs_0_, f32[512,128]{1,0:T(8,128)S(1)} %collective-permute-done.35.refs_1_, f32[1024,256]{1,0:T(8,128)S(1)} %get-tuple-element.117.refs_2_, f32[1024,256]{1,0:T(8,128)S(1)} %collective-permute-done.36.refs_3_, ...), custom_call_target="tpu_custom_call" | custom-call | tf_op jit(solution)/shard_map/finish/pallas_call | solution.py:488
  (64 shorter events, 17.4 us)
Async XLA Ops:
  3.5 7.9 %collective-permute-start.3 = (bf16[32,4608]{1,0:T(8,128)(2,1)S(1)}, bf16[32,4608]{1,0:T(8,128)(2,1)S(1)}, u32[]{:S(2)}, u32[]{:S(2)}) collective-permute-start(bf16[32,4608]{1,0:T(8,128)(2,1)S(1)} %get-tuple-element.78), channel_id=1, source_target_pairs={{0,4},{2,6},{4,0},{6,2},{8,12},{10,14},{12,8},{14,10},{1,5},{3,7},... | collective-permute-start | bytes 884744 | tf_op jit(solution)/shard_map/ppermute | solution.py:540
  3.6 11.1 %collective-permute-start.4 = (bf16[32,4608]{1,0:T(8,128)(2,1)S(1)}, bf16[32,4608]{1,0:T(8,128)(2,1)S(1)}, u32[]{:S(2)}, u32[]{:S(2)}) collective-permute-start(bf16[32,4608]{1,0:T(8,128)(2,1)S(1)} %get-tuple-element.79), channel_id=1, source_target_pairs={{4,8},{6,10},{8,4},{10,6},{5,9},{7,11},{9,5},{11,7},{20,24},{22,26... | collective-permute-start | bytes 884744 | tf_op jit(solution)/shard_map/ppermute | solution.py:540
  8.1 7.3 %collective-permute-start.5 = (bf16[32,4608]{1,0:T(8,128)(2,1)S(1)}, bf16[32,4608]{1,0:T(8,128)(2,1)S(1)}, u32[]{:S(2)}, u32[]{:S(2)}) collective-permute-start(bf16[32,4608]{1,0:T(8,128)(2,1)S(1)} %get-tuple-element.80), channel_id=1, source_target_pairs={{0,2},{2,0},{4,6},{6,4},{8,10},{10,8},{12,14},{14,12},{1,3},{3,1},... | collective-permute-start | bytes 884744 | tf_op jit(solution)/shard_map/ppermute | solution.py:540
  10.9 15.3 %collective-permute-start.6 = (bf16[32,4608]{1,0:T(8,128)(2,1)S(1)}, bf16[32,4608]{1,0:T(8,128)(2,1)S(1)}, u32[]{:S(2)}, u32[]{:S(2)}) collective-permute-start(bf16[32,4608]{1,0:T(8,128)(2,1)S(1)} %get-tuple-element.82), channel_id=1, source_target_pairs={{0,2},{2,0},{4,6},{6,4},{8,10},{10,8},{12,14},{14,12},{1,3},{3,1},... | collective-permute-start | bytes 884744 | tf_op jit(solution)/shard_map/ppermute | solution.py:540
  11.4 17.1 %collective-permute-start.7 = (bf16[32,4608]{1,0:T(8,128)(2,1)S(1)}, bf16[32,4608]{1,0:T(8,128)(2,1)S(1)}, u32[]{:S(2)}, u32[]{:S(2)}) collective-permute-start(bf16[32,4608]{1,0:T(8,128)(2,1)S(1)} %get-tuple-element.83), channel_id=1, source_target_pairs={{0,4},{2,6},{4,0},{6,2},{8,12},{10,14},{12,8},{14,10},{1,5},{3,7},... | collective-permute-start | bytes 884744 | tf_op jit(solution)/shard_map/ppermute | solution.py:540
  11.5 17.0 %collective-permute-start.8 = (bf16[32,4608]{1,0:T(8,128)(2,1)S(1)}, bf16[32,4608]{1,0:T(8,128)(2,1)S(1)}, u32[]{:S(2)}, u32[]{:S(2)}) collective-permute-start(bf16[32,4608]{1,0:T(8,128)(2,1)S(1)} %get-tuple-element.84), channel_id=1, source_target_pairs={{4,8},{6,10},{8,4},{10,6},{5,9},{7,11},{9,5},{11,7},{20,24},{22,26... | collective-permute-start | bytes 884744 | tf_op jit(solution)/shard_map/ppermute | solution.py:540
  26.2 6.7 %collective-permute-start.14 = (bf16[32,4608]{1,0:T(8,128)(2,1)S(1)}, bf16[32,4608]{1,0:T(8,128)(2,1)S(1)}, u32[]{:S(2)}, u32[]{:S(2)}) collective-permute-start(bf16[32,4608]{1,0:T(8,128)(2,1)S(1)} %get-tuple-element.90), channel_id=1, source_target_pairs={{0,4},{2,6},{4,0},{6,2},{8,12},{10,14},{12,8},{14,10},{1,5},{3,7},... | collective-permute-start | bytes 884744 | tf_op jit(solution)/shard_map/ppermute | solution.py:540
  26.2 7.8 %collective-permute-start.15 = (bf16[32,4608]{1,0:T(8,128)(2,1)S(1)}, bf16[32,4608]{1,0:T(8,128)(2,1)S(1)}, u32[]{:S(2)}, u32[]{:S(2)}) collective-permute-start(bf16[32,4608]{1,0:T(8,128)(2,1)S(1)} %get-tuple-element.91), channel_id=1, source_target_pairs={{4,8},{6,10},{8,4},{10,6},{5,9},{7,11},{9,5},{11,7},{20,24},{22,26... | collective-permute-start | bytes 884744 | tf_op jit(solution)/shard_map/ppermute | solution.py:540
  30.2 9.1 %collective-permute-start.9 = (bf16[32,4608]{1,0:T(8,128)(2,1)S(1)}, bf16[32,4608]{1,0:T(8,128)(2,1)S(1)}, u32[]{:S(2)}, u32[]{:S(2)}) collective-permute-start(bf16[32,4608]{1,0:T(8,128)(2,1)S(1)} %get-tuple-element.85), channel_id=1, source_target_pairs={{0,2},{2,0},{4,6},{6,4},{8,10},{10,8},{12,14},{14,12},{1,3},{3,1},... | collective-permute-start | bytes 884744 | tf_op jit(solution)/shard_map/ppermute | solution.py:540
  30.6 11.2 %collective-permute-start.11 = (bf16[32,4608]{1,0:T(8,128)(2,1)S(1)}, bf16[32,4608]{1,0:T(8,128)(2,1)S(1)}, u32[]{:S(2)}, u32[]{:S(2)}) collective-permute-start(bf16[32,4608]{1,0:T(8,128)(2,1)S(1)} %get-tuple-element.87), channel_id=1, source_target_pairs={{0,4},{2,6},{4,0},{6,2},{8,12},{10,14},{12,8},{14,10},{1,5},{3,7},... | collective-permute-start | bytes 884744 | tf_op jit(solution)/shard_map/ppermute | solution.py:540
  30.7 11.1 %collective-permute-start.12 = (bf16[32,4608]{1,0:T(8,128)(2,1)S(1)}, bf16[32,4608]{1,0:T(8,128)(2,1)S(1)}, u32[]{:S(2)}, u32[]{:S(2)}) collective-permute-start(bf16[32,4608]{1,0:T(8,128)(2,1)S(1)} %get-tuple-element.88), channel_id=1, source_target_pairs={{4,8},{6,10},{8,4},{10,6},{5,9},{7,11},{9,5},{11,7},{20,24},{22,26... | collective-permute-start | bytes 884744 | tf_op jit(solution)/shard_map/ppermute | solution.py:540
  38.6 6.3 %collective-permute-start.16 = (bf16[32,4608]{1,0:T(8,128)(2,1)S(1)}, bf16[32,4608]{1,0:T(8,128)(2,1)S(1)}, u32[]{:S(2)}, u32[]{:S(2)}) collective-permute-start(bf16[32,4608]{1,0:T(8,128)(2,1)S(1)} %get-tuple-element.92), channel_id=1, source_target_pairs={{0,2},{2,0},{4,6},{6,4},{8,10},{10,8},{12,14},{14,12},{1,3},{3,1},... | collective-permute-start | bytes 884744 | tf_op jit(solution)/shard_map/ppermute | solution.py:540
  39.0 7.8 %collective-permute-start.20 = (bf16[32,4608]{1,0:T(8,128)(2,1)S(1)}, bf16[32,4608]{1,0:T(8,128)(2,1)S(1)}, u32[]{:S(2)}, u32[]{:S(2)}) collective-permute-start(bf16[32,4608]{1,0:T(8,128)(2,1)S(1)} %get-tuple-element.96), channel_id=1, source_target_pairs={{0,4},{2,6},{4,0},{6,2},{8,12},{10,14},{12,8},{14,10},{1,5},{3,7},... | collective-permute-start | bytes 884744 | tf_op jit(solution)/shard_map/ppermute | solution.py:540
  39.3 10.0 %collective-permute-start.21 = (bf16[32,4608]{1,0:T(8,128)(2,1)S(1)}, bf16[32,4608]{1,0:T(8,128)(2,1)S(1)}, u32[]{:S(2)}, u32[]{:S(2)}) collective-permute-start(bf16[32,4608]{1,0:T(8,128)(2,1)S(1)} %get-tuple-element.97), channel_id=1, source_target_pairs={{4,8},{6,10},{8,4},{10,6},{5,9},{7,11},{9,5},{11,7},{20,24},{22,26... | collective-permute-start | bytes 884744 | tf_op jit(solution)/shard_map/ppermute | solution.py:540
  43.6 11.8 %collective-permute-start.13 = (bf16[32,4608]{1,0:T(8,128)(2,1)S(1)}, bf16[32,4608]{1,0:T(8,128)(2,1)S(1)}, u32[]{:S(2)}, u32[]{:S(2)}) collective-permute-start(bf16[32,4608]{1,0:T(8,128)(2,1)S(1)} %get-tuple-element.89), channel_id=1, source_target_pairs={{0,2},{2,0},{4,6},{6,4},{8,10},{10,8},{12,14},{14,12},{1,3},{3,1},... | collective-permute-start | bytes 884744 | tf_op jit(solution)/shard_map/ppermute | solution.py:540
  44.1 13.3 %collective-permute-start.17 = (bf16[32,4608]{1,0:T(8,128)(2,1)S(1)}, bf16[32,4608]{1,0:T(8,128)(2,1)S(1)}, u32[]{:S(2)}, u32[]{:S(2)}) collective-permute-start(bf16[32,4608]{1,0:T(8,128)(2,1)S(1)} %get-tuple-element.93), channel_id=1, source_target_pairs={{0,4},{2,6},{4,0},{6,2},{8,12},{10,14},{12,8},{14,10},{1,5},{3,7},... | collective-permute-start | bytes 884744 | tf_op jit(solution)/shard_map/ppermute | solution.py:540
  44.8 14.2 %collective-permute-start.18 = (bf16[32,4608]{1,0:T(8,128)(2,1)S(1)}, bf16[32,4608]{1,0:T(8,128)(2,1)S(1)}, u32[]{:S(2)}, u32[]{:S(2)}) collective-permute-start(bf16[32,4608]{1,0:T(8,128)(2,1)S(1)} %get-tuple-element.94), channel_id=1, source_target_pairs={{4,8},{6,10},{8,4},{10,6},{5,9},{7,11},{9,5},{11,7},{20,24},{22,26... | collective-permute-start | bytes 884744 | tf_op jit(solution)/shard_map/ppermute | solution.py:540
  53.9 8.3 %collective-permute-start.22 = (bf16[32,4608]{1,0:T(8,128)(2,1)S(1)}, bf16[32,4608]{1,0:T(8,128)(2,1)S(1)}, u32[]{:S(2)}, u32[]{:S(2)}) collective-permute-start(bf16[32,4608]{1,0:T(8,128)(2,1)S(1)} %get-tuple-element.98), channel_id=1, source_target_pairs={{0,2},{2,0},{4,6},{6,4},{8,10},{10,8},{12,14},{14,12},{1,3},{3,1},... | collective-permute-start | bytes 884744 | tf_op jit(solution)/shard_map/ppermute | solution.py:540
  55.4 8.7 %collective-permute-start.24 = (bf16[32,4608]{1,0:T(8,128)(2,1)S(1)}, bf16[32,4608]{1,0:T(8,128)(2,1)S(1)}, u32[]{:S(2)}, u32[]{:S(2)}) collective-permute-start(bf16[32,4608]{1,0:T(8,128)(2,1)S(1)} %get-tuple-element.100), channel_id=1, source_target_pairs={{0,4},{2,6},{4,0},{6,2},{8,12},{10,14},{12,8},{14,10},{1,5},{3,7},... | collective-permute-start | bytes 884744 | tf_op jit(solution)/shard_map/ppermute | solution.py:540
  55.4 9.8 %collective-permute-start.27 = (bf16[32,4608]{1,0:T(8,128)(2,1)S(1)}, bf16[32,4608]{1,0:T(8,128)(2,1)S(1)}, u32[]{:S(2)}, u32[]{:S(2)}) collective-permute-start(bf16[32,4608]{1,0:T(8,128)(2,1)S(1)} %get-tuple-element.106), channel_id=1, source_target_pairs={{4,8},{6,10},{8,4},{10,6},{5,9},{7,11},{9,5},{11,7},{20,24},{22,26... | collective-permute-start | bytes 884744 | tf_op jit(solution)/shard_map/ppermute | solution.py:540
  59.9 10.0 %collective-permute-start.19 = (bf16[32,4608]{1,0:T(8,128)(2,1)S(1)}, bf16[32,4608]{1,0:T(8,128)(2,1)S(1)}, u32[]{:S(2)}, u32[]{:S(2)}) collective-permute-start(bf16[32,4608]{1,0:T(8,128)(2,1)S(1)} %get-tuple-element.95), channel_id=1, source_target_pairs={{0,2},{2,0},{4,6},{6,4},{8,10},{10,8},{12,14},{14,12},{1,3},{3,1},... | collective-permute-start | bytes 884744 | tf_op jit(solution)/shard_map/ppermute | solution.py:540
  60.3 9.5 %collective-permute-start.23 = (bf16[32,4608]{1,0:T(8,128)(2,1)S(1)}, bf16[32,4608]{1,0:T(8,128)(2,1)S(1)}, u32[]{:S(2)}, u32[]{:S(2)}) collective-permute-start(bf16[32,4608]{1,0:T(8,128)(2,1)S(1)} %get-tuple-element.99), channel_id=1, source_target_pairs={{0,4},{2,6},{4,0},{6,2},{8,12},{10,14},{12,8},{14,10},{1,5},{3,7},... | collective-permute-start | bytes 884744 | tf_op jit(solution)/shard_map/ppermute | solution.py:540
  62.2 9.9 %collective-permute-start.25 = (bf16[32,4608]{1,0:T(8,128)(2,1)S(1)}, bf16[32,4608]{1,0:T(8,128)(2,1)S(1)}, u32[]{:S(2)}, u32[]{:S(2)}) collective-permute-start(bf16[32,4608]{1,0:T(8,128)(2,1)S(1)} %get-tuple-element.102), channel_id=1, source_target_pairs={{4,8},{6,10},{8,4},{10,6},{5,9},{7,11},{9,5},{11,7},{20,24},{22,26... | collective-permute-start | bytes 884744 | tf_op jit(solution)/shard_map/ppermute | solution.py:540
  69.8 8.4 %collective-permute-start.28 = (bf16[32,4608]{1,0:T(8,128)(2,1)S(1)}, bf16[32,4608]{1,0:T(8,128)(2,1)S(1)}, u32[]{:S(2)}, u32[]{:S(2)}) collective-permute-start(bf16[32,4608]{1,0:T(8,128)(2,1)S(1)} %get-tuple-element.107), channel_id=1, source_target_pairs={{0,4},{2,6},{4,0},{6,2},{8,12},{10,14},{12,8},{14,10},{1,5},{3,7},... | collective-permute-start | bytes 884744 | tf_op jit(solution)/shard_map/ppermute | solution.py:540
  72.9 15.1 %collective-permute-start.26 = (bf16[32,4608]{1,0:T(8,128)(2,1)S(1)}, bf16[32,4608]{1,0:T(8,128)(2,1)S(1)}, u32[]{:S(2)}, u32[]{:S(2)}) collective-permute-start(bf16[32,4608]{1,0:T(8,128)(2,1)S(1)} %get-tuple-element.103), channel_id=1, source_target_pairs={{0,4},{2,6},{4,0},{6,2},{8,12},{10,14},{12,8},{14,10},{1,5},{3,7},... | collective-permute-start | bytes 884744 | tf_op jit(solution)/shard_map/ppermute | solution.py:540
  73.0 15.1 %collective-permute-start.29 = (bf16[32,4608]{1,0:T(8,128)(2,1)S(1)}, bf16[32,4608]{1,0:T(8,128)(2,1)S(1)}, u32[]{:S(2)}, u32[]{:S(2)}) collective-permute-start(bf16[32,4608]{1,0:T(8,128)(2,1)S(1)} %get-tuple-element.109), channel_id=1, source_target_pairs={{4,8},{6,10},{8,4},{10,6},{5,9},{7,11},{9,5},{11,7},{20,24},{22,26... | collective-permute-start | bytes 884744 | tf_op jit(solution)/shard_map/ppermute | solution.py:540
  78.2 37.3 %collective-permute-start.36 = (f32[1024,256]{1,0:T(8,128)S(1)}, f32[1024,256]{1,0:T(8,128)S(1)}, u32[]{:S(2)}, u32[]{:S(2)}) collective-permute-start(f32[1024,256]{1,0:T(8,128)S(1)} %get-tuple-element.118), channel_id=1, source_target_pairs={{0,1},{1,0},{2,3},{3,2},{4,5},{5,4},{6,7},{7,6},{8,9},{9,8},{10,11... | collective-permute-start | bytes 3145736 | tf_op jit(solution)/shard_map/ppermute | solution.py:552
  85.2 30.3 %collective-permute-start.37 = (f32[1024,256]{1,0:T(8,128)S(1)}, f32[1024,256]{1,0:T(8,128)S(1)}, u32[]{:S(2)}, u32[]{:S(2)}) collective-permute-start(f32[1024,256]{1,0:T(8,128)S(1)} %get-tuple-element.120), channel_id=1, source_target_pairs={{0,1},{1,0},{2,3},{3,2},{4,5},{5,4},{6,7},{7,6},{8,9},{9,8},{10,11... | collective-permute-start | bytes 3145736 | tf_op jit(solution)/shard_map/ppermute | solution.py:552
  85.2 10.1 %collective-permute-start.31 = (bf16[32,4608]{1,0:T(8,128)(2,1)S(1)}, bf16[32,4608]{1,0:T(8,128)(2,1)S(1)}, u32[]{:S(2)}, u32[]{:S(2)}) collective-permute-start(bf16[32,4608]{1,0:T(8,128)(2,1)S(1)} %get-tuple-element.111), channel_id=1, source_target_pairs={{4,8},{6,10},{8,4},{10,6},{5,9},{7,11},{9,5},{11,7},{20,24},{22,26... | collective-permute-start | bytes 884744 | tf_op jit(solution)/shard_map/ppermute | solution.py:540
  88.8 7.3 %collective-permute-start.30 = (bf16[32,4608]{1,0:T(8,128)(2,1)S(1)}, bf16[32,4608]{1,0:T(8,128)(2,1)S(1)}, u32[]{:S(2)}, u32[]{:S(2)}) collective-permute-start(bf16[32,4608]{1,0:T(8,128)(2,1)S(1)} %get-tuple-element.110), channel_id=1, source_target_pairs={{0,4},{2,6},{4,0},{6,2},{8,12},{10,14},{12,8},{14,10},{1,5},{3,7},... | collective-permute-start | bytes 884744 | tf_op jit(solution)/shard_map/ppermute | solution.py:540
  88.9 12.7 %collective-permute-start.33 = (bf16[32,4608]{1,0:T(8,128)(2,1)S(1)}, bf16[32,4608]{1,0:T(8,128)(2,1)S(1)}, u32[]{:S(2)}, u32[]{:S(2)}) collective-permute-start(bf16[32,4608]{1,0:T(8,128)(2,1)S(1)} %get-tuple-element.113), channel_id=1, source_target_pairs={{4,8},{6,10},{8,4},{10,6},{5,9},{7,11},{9,5},{11,7},{20,24},{22,26... | collective-permute-start | bytes 884744 | tf_op jit(solution)/shard_map/ppermute | solution.py:540
  96.1 11.8 %collective-permute-start.34 = (bf16[32,4608]{1,0:T(8,128)(2,1)S(1)}, bf16[32,4608]{1,0:T(8,128)(2,1)S(1)}, u32[]{:S(2)}, u32[]{:S(2)}) collective-permute-start(bf16[32,4608]{1,0:T(8,128)(2,1)S(1)} %get-tuple-element.114), channel_id=1, source_target_pairs={{4,8},{6,10},{8,4},{10,6},{5,9},{7,11},{9,5},{11,7},{20,24},{22,26... | collective-permute-start | bytes 884744 | tf_op jit(solution)/shard_map/ppermute | solution.py:540
  (8 other events, 84.7 us)

commit v3 on v1

--- a/solution.py
+++ b/solution.py
@@ -506,7 +506,7 @@
     return held
 
 
-def route(table, down_pool, up_pool, n_dp, tokens, key_weight):
+def route(table, down_pool, up_pool, n_dp, tokens, key_weight, swap_plans):
     rank = down_pool.shape[1]
     size = rank // 2
     half = up_pool.shape[2] // 2
@@ -518,6 +518,8 @@
     done = []
     for step in range(Z_STEPS):
         streams = [E_TABLE, O_TABLE] + ([X_TABLE] if step < X_STEPS else [])
+        if step == Z_STEPS - 2:
+            table, others = lax.optimization_barrier((table, swap_plans(table)))
         for part in range(2):
             known = [list(arrays) for arrays in got[part]]
             piece = pieces[step - 1] if part == 1 and 1 <= step <= len(pieces) else None
@@ -529,7 +531,7 @@
             for stream, send in zip(streams, sends):
                 pairs = (outer, middle, over_x)[stream]
                 got[part][stream].append(lax.ppermute(send, "dp", pairs))
-    return got, done
+    return got, done, others
 
 
 def shards(sizes, tokens, key_weight, down_pool, up_pool, adapter_ids, lengths, owner_map):
@@ -561,9 +563,14 @@
         return by_all_to_all()
     table = plan(held, adapter_ids, owner_map)
     at_hand = stage(tokens)
-    got, done = route(table, down_pool, up_pool, n_dp, at_hand, key_weight)
+
+    def swap_plans(table):
+        return gathered(table, "groups", n_groups)[-1]
+
+    got, done, others = route(
+        table, down_pool, up_pool, n_dp, at_hand, key_weight, swap_plans
+    )
     base = [[here, sent_on(there, 1)] for there, here in zip(done[:2], done[2:])]
-    others = gathered(table, "groups", n_groups)[-1]
     sources = [("pool", (in_hbm(down_pool), in_hbm(up_pool)))]
     for stream in (2, 0, 1):
         sources += [("block", pair) for pair in zip(got[0][stream], got[1][stream])]

time: 115 us -> 115 us (level)
  waiting for transfers between devices: 15.3 us -> 19.7 us
  starting transfers between devices: 56.6 us -> 54 us
    ppermute x32, waiting for transfers between devices: 14.8 us -> 19.2 us  [route(): got[part][stream].append(lax.ppermute(send, 'dp', pairs))]
    pallas_call x12, Pallas kernels: 28.3 us -> 26.3 us  [pick(): pl.pallas_call(functools.partial(pick_kernel, step, size, lo, streams, he...]
    ppermute x2, starting transfers between devices: 6.3 us -> 4.32 us  [gathered(): lax.ppermute(part, axis, [(i, (i + step) % size) for i in range(size)])]
  transfers between devices with their start and end apart: 36 -> 36, of which waited for: 13 -> 12; matrix products, arithmetic and copies ran while one was open for 0% -> 0% of each run, Pallas kernels for 31% -> 29%
where the time goes in v3:
time: 115 us
  starting transfers between devices  54 us (47%)
  Pallas kernels  39.6 us (34%)
  waiting for transfers between devices  19.7 us (17%)
  between operations  1.23 us (1%)
    ppermute x32, starting transfers between devices, route(): got[part][stream].append(lax.ppermute(send, 'dp', pairs))  41.4 us
    pallas_call x12, Pallas kernels, pick(): pl.pallas_call(functools.partial(pick_kernel, step, size, lo, streams, he...  26.3 us
    ppermute x32, waiting for transfers between devices, route(): got[part][stream].append(lax.ppermute(send, 'dp', pairs))  19.2 us
    ppermute x2, starting transfers between devices, sent_on(): return lax.ppermute(part, 'tensor', pairs)  8.27 us
    pallas_call x1, Pallas kernels, codes(): pl.pallas_call(functools.partial(code_kernel, count, kinds, routed), grid...  5.54 us
    ppermute x2, starting transfers between devices, gathered(): lax.ppermute(part, axis, [(i, (i + step) % size) for i in range(size)])  4.32 us
    pallas_call x1, Pallas kernels, stage(): pl.pallas_call(stage_kernel, in_specs=[ANY], out_specs=VMEM, out_shape=pl...  3.39 us
    pallas_call x1, Pallas kernels, finish(): pl.pallas_call(functools.partial(finish_kernel, count, parts, shares, til...  2.54 us
  transfers between devices with their start and end apart: 36, of which 12 were waited for; matrix products, arithmetic and copies ran while one was open for 0% of the time, Pallas kernels for 29%

profile of v3, /device:TPU:9, one launch (start us, length us, event | category | flops | bytes accessed | tf_op | source)
XLA Modules:
  0.0 114.6 jit_solution(11374975525652695074)
XLA Ops:
  0.0 1.8 %plan.1.table.index = s32[8,128]{1,0:T(8,128)S(1)} custom-call(s32[4,8]{1,0:T(4,128)} %bitcast.20, s32[80]{0:T(128)} %owner_map.1), custom_call_target="tpu_custom_call" | custom-call | tf_op jit(solution)/shard_map/plan/pallas_call | solution.py:170
  1.8 1.7 %pick.12 = (bf16[32,4608]{1,0:T(8,128)(2,1)S(1)}, bf16[32,4608]{1,0:T(8,128)(2,1)S(1)}, bf16[32,4608]{1,0:T(8,128)(2,1)S(1)}) custom-call(s32[8,128]{1,0:T(8,128)S(1)} %plan.1.table.index, bf16[10,64,4096]{2,1,0:T(8,128)(2,1)} %refs_0_.1, bf16[10,64,512]{2,1,0:T(8,128)(2,1)} %refs_1_.1), custom_call_target="tpu_custom_call" | custom-call | tf_op jit(solution)/shard_map/pick/pallas_call | solution.py:260
  3.5 1.3 %collective-permute-start.3 = (bf16[32,4608]{1,0:T(8,128)(2,1)S(1)}, bf16[32,4608]{1,0:T(8,128)(2,1)S(1)}, u32[]{:S(2)}, u32[]{:S(2)}) collective-permute-start(bf16[32,4608]{1,0:T(8,128)(2,1)S(1)} %get-tuple-element.74), channel_id=1, source_target_pairs={{0,2},{2,0},{4,6},{6,4},{8,10},{10,8},{12,14},{14,12},{1,3},{3,1},... | collective-permute-start | bytes 884744 | tf_op jit(solution)/shard_map/ppermute | solution.py:533
  5.0 4.3 %collective-permute-start.6 = (bf16[32,4608]{1,0:T(8,128)(2,1)S(1)}, bf16[32,4608]{1,0:T(8,128)(2,1)S(1)}, u32[]{:S(2)}, u32[]{:S(2)}) collective-permute-start(bf16[32,4608]{1,0:T(8,128)(2,1)S(1)} %get-tuple-element.77), channel_id=1, source_target_pairs={{4,8},{6,10},{8,4},{10,6},{5,9},{7,11},{9,5},{11,7},{20,24},{22,26... | collective-permute-start | bytes 884744 | tf_op jit(solution)/shard_map/ppermute | solution.py:533
  9.3 1.7 %pick.13 = (bf16[32,4608]{1,0:T(8,128)(2,1)S(1)}, bf16[32,4608]{1,0:T(8,128)(2,1)S(1)}, bf16[32,4608]{1,0:T(8,128)(2,1)S(1)}) custom-call(s32[8,128]{1,0:T(8,128)S(1)} %plan.1.table.index, bf16[10,64,4096]{2,1,0:T(8,128)(2,1)} %refs_0_.1, bf16[10,64,512]{2,1,0:T(8,128)(2,1)} %refs_1_.1), custom_call_target="tpu_custom_call" | custom-call | tf_op jit(solution)/shard_map/pick/pallas_call | solution.py:260
  11.5 3.3 %collective-permute-start.9 = (bf16[32,4608]{1,0:T(8,128)(2,1)S(1)}, bf16[32,4608]{1,0:T(8,128)(2,1)S(1)}, u32[]{:S(2)}, u32[]{:S(2)}) collective-permute-start(bf16[32,4608]{1,0:T(8,128)(2,1)S(1)} %get-tuple-element.80), channel_id=1, source_target_pairs={{4,8},{6,10},{8,4},{10,6},{5,9},{7,11},{9,5},{11,7},{20,24},{22,26... | collective-permute-start | bytes 884744 | tf_op jit(solution)/shard_map/ppermute | solution.py:533
  18.0 2.5 %collective-permute-start.12 = (bf16[32,4608]{1,0:T(8,128)(2,1)S(1)}, bf16[32,4608]{1,0:T(8,128)(2,1)S(1)}, u32[]{:S(2)}, u32[]{:S(2)}) collective-permute-start(bf16[32,4608]{1,0:T(8,128)(2,1)S(1)} %get-tuple-element.83), channel_id=1, source_target_pairs={{4,8},{6,10},{8,4},{10,6},{5,9},{7,11},{9,5},{11,7},{20,24},{22,26... | collective-permute-start | bytes 884744 | tf_op jit(solution)/shard_map/ppermute | solution.py:533
  20.6 3.4 %stage.1.refs_3_.refs_6_.refs_9_.refs_12_.tokens = bf16[1024,4096]{1,0:T(8,128)(2,1)S(1)} custom-call(bf16[1024,4096]{1,0:T(8,128)(2,1)} %source.1), custom_call_target="tpu_custom_call" | custom-call | tf_op jit(solution)/shard_map/stage/pallas_call | solution.py:313
  24.0 4.6 %pick.15 = (bf16[32,4608]{1,0:T(8,128)(2,1)S(1)}, bf16[32,4608]{1,0:T(8,128)(2,1)S(1)}, bf16[32,4608]{1,0:T(8,128)(2,1)S(1)}, f32[1024,256]{1,0:T(8,128)S(1)}) custom-call(s32[8,128]{1,0:T(8,128)S(1)} %plan.1.table.index, bf16[10,64,4096]{2,1,0:T(8,128)(2,1)} %refs_0_.1, bf16[10,64,512]{2,1,0:T(8,128)(2,1)} %refs_1_.1, ...), custom_call_target="tpu_custom_call" | custom-call | tf_op jit(solution)/shard_map/pick/pallas_call | solution.py:260
  28.6 1.9 %collective-permute-start.10 = (bf16[32,4608]{1,0:T(8,128)(2,1)S(1)}, bf16[32,4608]{1,0:T(8,128)(2,1)S(1)}, u32[]{:S(2)}, u32[]{:S(2)}) collective-permute-start(bf16[32,4608]{1,0:T(8,128)(2,1)S(1)} %get-tuple-element.81), channel_id=1, source_target_pairs={{0,2},{2,0},{4,6},{6,4},{8,10},{10,8},{12,14},{14,12},{1,3},{3,1},... | collective-permute-start | bytes 884744 | tf_op jit(solution)/shard_map/ppermute | solution.py:533
  30.5 1.9 %collective-permute-start.15 = (bf16[32,4608]{1,0:T(8,128)(2,1)S(1)}, bf16[32,4608]{1,0:T(8,128)(2,1)S(1)}, u32[]{:S(2)}, u32[]{:S(2)}) collective-permute-start(bf16[32,4608]{1,0:T(8,128)(2,1)S(1)} %get-tuple-element.86), channel_id=1, source_target_pairs={{4,8},{6,10},{8,4},{10,6},{5,9},{7,11},{9,5},{11,7},{20,24},{22,26... | collective-permute-start | bytes 884744 | tf_op jit(solution)/shard_map/ppermute | solution.py:533
  34.9 2.8 %collective-permute-start.18 = (bf16[32,4608]{1,0:T(8,128)(2,1)S(1)}, bf16[32,4608]{1,0:T(8,128)(2,1)S(1)}, u32[]{:S(2)}, u32[]{:S(2)}) collective-permute-start(bf16[32,4608]{1,0:T(8,128)(2,1)S(1)} %get-tuple-element.89), channel_id=1, source_target_pairs={{4,8},{6,10},{8,4},{10,6},{5,9},{7,11},{9,5},{11,7},{20,24},{22,26... | collective-permute-start | bytes 884744 | tf_op jit(solution)/shard_map/ppermute | solution.py:533
  38.3 4.6 %pick.17 = (bf16[32,4608]{1,0:T(8,128)(2,1)S(1)}, bf16[32,4608]{1,0:T(8,128)(2,1)S(1)}, bf16[32,4608]{1,0:T(8,128)(2,1)S(1)}, f32[1024,256]{1,0:T(8,128)S(1)}) custom-call(s32[8,128]{1,0:T(8,128)S(1)} %plan.1.table.index, bf16[10,64,4096]{2,1,0:T(8,128)(2,1)} %refs_0_.1, bf16[10,64,512]{2,1,0:T(8,128)(2,1)} %refs_1_.1, ...), custom_call_target="tpu_custom_call" | custom-call | tf_op jit(solution)/shard_map/pick/pallas_call | solution.py:260
  43.8 2.2 %collective-permute-start.21 = (bf16[32,4608]{1,0:T(8,128)(2,1)S(1)}, bf16[32,4608]{1,0:T(8,128)(2,1)S(1)}, u32[]{:S(2)}, u32[]{:S(2)}) collective-permute-start(bf16[32,4608]{1,0:T(8,128)(2,1)S(1)} %get-tuple-element.92), channel_id=1, source_target_pairs={{4,8},{6,10},{8,4},{10,6},{5,9},{7,11},{9,5},{11,7},{20,24},{22,26... | collective-permute-start | bytes 884744 | tf_op jit(solution)/shard_map/ppermute | solution.py:533
  47.4 1.4 %collective-permute-done.16.refs_8_.refs_10_.refs_12_.refs_7_ = bf16[32,4608]{1,0:T(8,128)(2,1)S(1)} collective-permute-done((bf16[32,4608]{1,0:T(8,128)(2,1)S(1)}, bf16[32,4608]{1,0:T(8,128)(2,1)S(1)}, u32[]{:S(2)}, u32[]{:S(2)}) %collective-permute-start.16) | collective-permute-done | bytes 294944 | tf_op jit(solution)/shard_map/ppermute | solution.py:533
  48.8 2.7 %collective-permute-start.25 = (bf16[32,4608]{1,0:T(8,128)(2,1)S(1)}, bf16[32,4608]{1,0:T(8,128)(2,1)S(1)}, u32[]{:S(2)}, u32[]{:S(2)}) collective-permute-start(bf16[32,4608]{1,0:T(8,128)(2,1)S(1)} %get-tuple-element.97), channel_id=1, source_target_pairs={{4,8},{6,10},{8,4},{10,6},{5,9},{7,11},{9,5},{11,7},{20,24},{22,26... | collective-permute-start | bytes 884744 | tf_op jit(solution)/shard_map/ppermute | solution.py:533
  52.1 4.6 %pick.19 = (bf16[32,4608]{1,0:T(8,128)(2,1)S(1)}, bf16[32,4608]{1,0:T(8,128)(2,1)S(1)}, bf16[32,4608]{1,0:T(8,128)(2,1)S(1)}, f32[1024,256]{1,0:T(8,128)S(1)}) custom-call(s32[8,128]{1,0:T(8,128)S(1)} %plan.1.table.index, bf16[10,64,4096]{2,1,0:T(8,128)(2,1)} %refs_0_.1, bf16[10,64,512]{2,1,0:T(8,128)(2,1)} %refs_1_.1, ...), custom_call_target="tpu_custom_call" | custom-call | tf_op jit(solution)/shard_map/pick/pallas_call | solution.py:260
  56.7 2.6 %collective-permute-start.22 = (bf16[32,4608]{1,0:T(8,128)(2,1)S(1)}, bf16[32,4608]{1,0:T(8,128)(2,1)S(1)}, u32[]{:S(2)}, u32[]{:S(2)}) collective-permute-start(bf16[32,4608]{1,0:T(8,128)(2,1)S(1)} %get-tuple-element.93), channel_id=1, source_target_pairs={{0,2},{2,0},{4,6},{6,4},{8,10},{10,8},{12,14},{14,12},{1,3},{3,1},... | collective-permute-start | bytes 884744 | tf_op jit(solution)/shard_map/ppermute | solution.py:533
  59.2 1.9 %collective-permute-start.27 = (bf16[32,4608]{1,0:T(8,128)(2,1)S(1)}, bf16[32,4608]{1,0:T(8,128)(2,1)S(1)}, u32[]{:S(2)}, u32[]{:S(2)}) collective-permute-start(bf16[32,4608]{1,0:T(8,128)(2,1)S(1)} %get-tuple-element.99), channel_id=1, source_target_pairs={{4,8},{6,10},{8,4},{10,6},{5,9},{7,11},{9,5},{11,7},{20,24},{22,26... | collective-permute-start | bytes 884744 | tf_op jit(solution)/shard_map/ppermute | solution.py:533
  62.2 4.1 %collective-permute-start.29 = (bf16[32,4608]{1,0:T(8,128)(2,1)S(1)}, bf16[32,4608]{1,0:T(8,128)(2,1)S(1)}, u32[]{:S(2)}, u32[]{:S(2)}) collective-permute-start(bf16[32,4608]{1,0:T(8,128)(2,1)S(1)} %get-tuple-element.101), channel_id=1, source_target_pairs={{4,8},{6,10},{8,4},{10,6},{5,9},{7,11},{9,5},{11,7},{20,24},{22,26... | collective-permute-start | bytes 884744 | tf_op jit(solution)/shard_map/ppermute | solution.py:533
  66.3 8.2 %collective-permute-start.36 = (f32[1024,256]{1,0:T(8,128)S(1)}, f32[1024,256]{1,0:T(8,128)S(1)}, u32[]{:S(2)}, u32[]{:S(2)}) collective-permute-start(f32[1024,256]{1,0:T(8,128)S(1)} %get-tuple-element.110), channel_id=1, source_target_pairs={{0,1},{1,0},{2,3},{3,2},{4,5},{5,4},{6,7},{7,6},{8,9},{9,8},{10,11... | collective-permute-start | bytes 3145736 | tf_op jit(solution)/shard_map/ppermute | solution.py:544
  74.6 4.6 %pick.21 = (bf16[32,4608]{1,0:T(8,128)(2,1)S(1)}, bf16[32,4608]{1,0:T(8,128)(2,1)S(1)}, f32[1024,256]{1,0:T(8,128)S(1)}) custom-call(s32[8,128]{1,0:T(8,128)S(1)} %plan.1.table.index, bf16[10,64,4096]{2,1,0:T(8,128)(2,1)} %refs_0_.1, bf16[10,64,512]{2,1,0:T(8,128)(2,1)} %refs_1_.1, bf16[32,4608]{1,0:T(8,128)(2,1)S(1)} %collective-permute-done.8.refs_0_.refs_11_, ...), custom_call_target="tpu_custom_call" | custom-call | tf_op jit(solution)/shard_map/pick/pallas_call | solution.py:260
  79.3 2.2 %collective-permute-start.31 = (bf16[32,4608]{1,0:T(8,128)(2,1)S(1)}, bf16[32,4608]{1,0:T(8,128)(2,1)S(1)}, u32[]{:S(2)}, u32[]{:S(2)}) collective-permute-start(bf16[32,4608]{1,0:T(8,128)(2,1)S(1)} %get-tuple-element.103), channel_id=1, source_target_pairs={{4,8},{6,10},{8,4},{10,6},{5,9},{7,11},{9,5},{11,7},{20,24},{22,26... | collective-permute-start | bytes 884744 | tf_op jit(solution)/shard_map/ppermute | solution.py:533
  82.3 4.6 %collective-permute-done.28.refs_4_.refs_19_ = bf16[32,4608]{1,0:T(8,128)(2,1)S(1)} collective-permute-done((bf16[32,4608]{1,0:T(8,128)(2,1)S(1)}, bf16[32,4608]{1,0:T(8,128)(2,1)S(1)}, u32[]{:S(2)}, u32[]{:S(2)}) %collective-permute-start.28) | collective-permute-done | bytes 294944 | tf_op jit(solution)/shard_map/ppermute | solution.py:533
  86.9 1.9 %collective-permute-start.33 = (bf16[32,4608]{1,0:T(8,128)(2,1)S(1)}, bf16[32,4608]{1,0:T(8,128)(2,1)S(1)}, u32[]{:S(2)}, u32[]{:S(2)}) collective-permute-start(bf16[32,4608]{1,0:T(8,128)(2,1)S(1)} %get-tuple-element.105), channel_id=1, source_target_pairs={{4,8},{6,10},{8,4},{10,6},{5,9},{7,11},{9,5},{11,7},{20,24},{22,26... | collective-permute-start | bytes 884744 | tf_op jit(solution)/shard_map/ppermute | solution.py:533
  89.7 3.6 %collective-permute-done.30.refs_20_ = bf16[32,4608]{1,0:T(8,128)(2,1)S(1)} collective-permute-done((bf16[32,4608]{1,0:T(8,128)(2,1)S(1)}, bf16[32,4608]{1,0:T(8,128)(2,1)S(1)}, u32[]{:S(2)}, u32[]{:S(2)}) %collective-permute-start.30) | collective-permute-done | bytes 294944 | tf_op jit(solution)/shard_map/ppermute | solution.py:533
  93.2 2.0 %collective-permute-start.34 = (bf16[32,4608]{1,0:T(8,128)(2,1)S(1)}, bf16[32,4608]{1,0:T(8,128)(2,1)S(1)}, u32[]{:S(2)}, u32[]{:S(2)}) collective-permute-start(bf16[32,4608]{1,0:T(8,128)(2,1)S(1)} %get-tuple-element.106), channel_id=1, source_target_pairs={{4,8},{6,10},{8,4},{10,6},{5,9},{7,11},{9,5},{11,7},{20,24},{22,26... | collective-permute-start | bytes 884744 | tf_op jit(solution)/shard_map/ppermute | solution.py:533
  95.3 3.9 %collective-permute-done.32.refs_21_ = bf16[32,4608]{1,0:T(8,128)(2,1)S(1)} collective-permute-done((bf16[32,4608]{1,0:T(8,128)(2,1)S(1)}, bf16[32,4608]{1,0:T(8,128)(2,1)S(1)}, u32[]{:S(2)}, u32[]{:S(2)}) %collective-permute-start.32) | collective-permute-done | bytes 294944 | tf_op jit(solution)/shard_map/ppermute | solution.py:533
  99.2 1.9 %collective-permute-done.34.refs_33_ = bf16[32,4608]{1,0:T(8,128)(2,1)S(1)} collective-permute-done((bf16[32,4608]{1,0:T(8,128)(2,1)S(1)}, bf16[32,4608]{1,0:T(8,128)(2,1)S(1)}, u32[]{:S(2)}, u32[]{:S(2)}) %collective-permute-start.34) | collective-permute-done | bytes 294944 | tf_op jit(solution)/shard_map/ppermute | solution.py:533
  101.1 5.5 %codes.3 = (f32[512,128]{1,0:T(8,128)S(1)}, bf16[256,512]{1,0:T(8,128)(2,1)S(1)}, s32[1]{0:T(128)}) custom-call(s32[8,128]{1,0:T(8,128)S(1)} %plan.1.table.index, s32[8,128]{1,0:T(8,128)S(1)} %collective-permute-done.2.others, s32[1,4]{1,0:T(1,128)S(1)} %copy-done.1, bf16[1024,4096]{1,0:T(8,128)(2,1)S(1)} %stage.1.refs_3_.refs_6_.refs_9_.refs_12_.tokens, ...), custom_call_target="tpu_custom_call" | custom-call | tf_op jit(solution)/shard_map/codes/pallas_call | solution.py:415
  106.6 4.1 %collective-permute-start.35 = (f32[512,128]{1,0:T(8,128)S(1)}, f32[512,128]{1,0:T(8,128)S(1)}, u32[]{:S(2)}, u32[]{:S(2)}) collective-permute-start(f32[512,128]{1,0:T(8,128)S(1)} %get-tuple-element.108.refs_0_), channel_id=1, source_target_pairs={{0,1},{1,0},{2,3},{3,2},{4,5},{5,4},{6,7},{7,6},{8,9},{9,8},{10,11... | collective-permute-start | bytes 786440 | tf_op jit(solution)/shard_map/ppermute | solution.py:505
  111.9 2.5 %finish.3 = bf16[1024,512]{1,0:T(8,128)(2,1)} custom-call(s32[1,4]{1,0:T(1,128)S(1)} %copy-done.1, f32[512,128]{1,0:T(8,128)S(1)} %get-tuple-element.108.refs_0_, f32[512,128]{1,0:T(8,128)S(1)} %collective-permute-done.35.refs_1_, f32[1024,256]{1,0:T(8,128)S(1)} %get-tuple-element.109.refs_2_, f32[1024,256]{1,0:T(8,128)S(1)} %collective-permute-done.36.refs_3_, ...), custom_call_target="tpu_custom_call" | custom-call | tf_op jit(solution)/shard_map/finish/pallas_call | solution.py:484
  (63 shorter events, 12.9 us)
Async XLA Ops:
  3.5 7.9 %collective-permute-start.3 = (bf16[32,4608]{1,0:T(8,128)(2,1)S(1)}, bf16[32,4608]{1,0:T(8,128)(2,1)S(1)}, u32[]{:S(2)}, u32[]{:S(2)}) collective-permute-start(bf16[32,4608]{1,0:T(8,128)(2,1)S(1)} %get-tuple-element.74), channel_id=1, source_target_pairs={{0,2},{2,0},{4,6},{6,4},{8,10},{10,8},{12,14},{14,12},{1,3},{3,1},... | collective-permute-start | bytes 884744 | tf_op jit(solution)/shard_map/ppermute | solution.py:533
  4.8 10.0 %collective-permute-start.5 = (bf16[32,4608]{1,0:T(8,128)(2,1)S(1)}, bf16[32,4608]{1,0:T(8,128)(2,1)S(1)}, u32[]{:S(2)}, u32[]{:S(2)}) collective-permute-start(bf16[32,4608]{1,0:T(8,128)(2,1)S(1)} %get-tuple-element.76), channel_id=1, source_target_pairs={{0,4},{2,6},{4,0},{6,2},{8,12},{10,14},{12,8},{14,10},{1,5},{3,7},... | collective-permute-start | bytes 884744 | tf_op jit(solution)/shard_map/ppermute | solution.py:533
  5.0 10.4 %collective-permute-start.6 = (bf16[32,4608]{1,0:T(8,128)(2,1)S(1)}, bf16[32,4608]{1,0:T(8,128)(2,1)S(1)}, u32[]{:S(2)}, u32[]{:S(2)}) collective-permute-start(bf16[32,4608]{1,0:T(8,128)(2,1)S(1)} %get-tuple-element.77), channel_id=1, source_target_pairs={{4,8},{6,10},{8,4},{10,6},{5,9},{7,11},{9,5},{11,7},{20,24},{22,26... | collective-permute-start | bytes 884744 | tf_op jit(solution)/shard_map/ppermute | solution.py:533
  11.3 12.7 %collective-permute-start.8 = (bf16[32,4608]{1,0:T(8,128)(2,1)S(1)}, bf16[32,4608]{1,0:T(8,128)(2,1)S(1)}, u32[]{:S(2)}, u32[]{:S(2)}) collective-permute-start(bf16[32,4608]{1,0:T(8,128)(2,1)S(1)} %get-tuple-element.79), channel_id=1, source_target_pairs={{0,4},{2,6},{4,0},{6,2},{8,12},{10,14},{12,8},{14,10},{1,5},{3,7},... | collective-permute-start | bytes 884744 | tf_op jit(solution)/shard_map/ppermute | solution.py:533
  11.5 12.5 %collective-permute-start.9 = (bf16[32,4608]{1,0:T(8,128)(2,1)S(1)}, bf16[32,4608]{1,0:T(8,128)(2,1)S(1)}, u32[]{:S(2)}, u32[]{:S(2)}) collective-permute-start(bf16[32,4608]{1,0:T(8,128)(2,1)S(1)} %get-tuple-element.80), channel_id=1, source_target_pairs={{4,8},{6,10},{8,4},{10,6},{5,9},{7,11},{9,5},{11,7},{20,24},{22,26... | collective-permute-start | bytes 884744 | tf_op jit(solution)/shard_map/ppermute | solution.py:533
  16.2 14.4 %collective-permute-start.7 = (bf16[32,4608]{1,0:T(8,128)(2,1)S(1)}, bf16[32,4608]{1,0:T(8,128)(2,1)S(1)}, u32[]{:S(2)}, u32[]{:S(2)}) collective-permute-start(bf16[32,4608]{1,0:T(8,128)(2,1)S(1)} %get-tuple-element.78), channel_id=1, source_target_pairs={{0,2},{2,0},{4,6},{6,4},{8,10},{10,8},{12,14},{14,12},{1,3},{3,1},... | collective-permute-start | bytes 884744 | tf_op jit(solution)/shard_map/ppermute | solution.py:533
  16.8 15.6 %collective-permute-start.11 = (bf16[32,4608]{1,0:T(8,128)(2,1)S(1)}, bf16[32,4608]{1,0:T(8,128)(2,1)S(1)}, u32[]{:S(2)}, u32[]{:S(2)}) collective-permute-start(bf16[32,4608]{1,0:T(8,128)(2,1)S(1)} %get-tuple-element.82), channel_id=1, source_target_pairs={{0,4},{2,6},{4,0},{6,2},{8,12},{10,14},{12,8},{14,10},{1,5},{3,7},... | collective-permute-start | bytes 884744 | tf_op jit(solution)/shard_map/ppermute | solution.py:533
  18.0 14.4 %collective-permute-start.12 = (bf16[32,4608]{1,0:T(8,128)(2,1)S(1)}, bf16[32,4608]{1,0:T(8,128)(2,1)S(1)}, u32[]{:S(2)}, u32[]{:S(2)}) collective-permute-start(bf16[32,4608]{1,0:T(8,128)(2,1)S(1)} %get-tuple-element.83), channel_id=1, source_target_pairs={{4,8},{6,10},{8,4},{10,6},{5,9},{7,11},{9,5},{11,7},{20,24},{22,26... | collective-permute-start | bytes 884744 | tf_op jit(solution)/shard_map/ppermute | solution.py:533
  30.5 7.3 %collective-permute-start.14 = (bf16[32,4608]{1,0:T(8,128)(2,1)S(1)}, bf16[32,4608]{1,0:T(8,128)(2,1)S(1)}, u32[]{:S(2)}, u32[]{:S(2)}) collective-permute-start(bf16[32,4608]{1,0:T(8,128)(2,1)S(1)} %get-tuple-element.85), channel_id=1, source_target_pairs={{0,4},{2,6},{4,0},{6,2},{8,12},{10,14},{12,8},{14,10},{1,5},{3,7},... | collective-permute-start | bytes 884744 | tf_op jit(solution)/shard_map/ppermute | solution.py:533
  30.5 7.8 %collective-permute-start.15 = (bf16[32,4608]{1,0:T(8,128)(2,1)S(1)}, bf16[32,4608]{1,0:T(8,128)(2,1)S(1)}, u32[]{:S(2)}, u32[]{:S(2)}) collective-permute-start(bf16[32,4608]{1,0:T(8,128)(2,1)S(1)} %get-tuple-element.86), channel_id=1, source_target_pairs={{4,8},{6,10},{8,4},{10,6},{5,9},{7,11},{9,5},{11,7},{20,24},{22,26... | collective-permute-start | bytes 884744 | tf_op jit(solution)/shard_map/ppermute | solution.py:533
  33.2 10.6 %collective-permute-start.13 = (bf16[32,4608]{1,0:T(8,128)(2,1)S(1)}, bf16[32,4608]{1,0:T(8,128)(2,1)S(1)}, u32[]{:S(2)}, u32[]{:S(2)}) collective-permute-start(bf16[32,4608]{1,0:T(8,128)(2,1)S(1)} %get-tuple-element.84), channel_id=1, source_target_pairs={{0,2},{2,0},{4,6},{6,4},{8,10},{10,8},{12,14},{14,12},{1,3},{3,1},... | collective-permute-start | bytes 884744 | tf_op jit(solution)/shard_map/ppermute | solution.py:533
  33.8 12.3 %collective-permute-start.17 = (bf16[32,4608]{1,0:T(8,128)(2,1)S(1)}, bf16[32,4608]{1,0:T(8,128)(2,1)S(1)}, u32[]{:S(2)}, u32[]{:S(2)}) collective-permute-start(bf16[32,4608]{1,0:T(8,128)(2,1)S(1)} %get-tuple-element.88), channel_id=1, source_target_pairs={{0,4},{2,6},{4,0},{6,2},{8,12},{10,14},{12,8},{14,10},{1,5},{3,7},... | collective-permute-start | bytes 884744 | tf_op jit(solution)/shard_map/ppermute | solution.py:533
  34.9 11.2 %collective-permute-start.18 = (bf16[32,4608]{1,0:T(8,128)(2,1)S(1)}, bf16[32,4608]{1,0:T(8,128)(2,1)S(1)}, u32[]{:S(2)}, u32[]{:S(2)}) collective-permute-start(bf16[32,4608]{1,0:T(8,128)(2,1)S(1)} %get-tuple-element.89), channel_id=1, source_target_pairs={{4,8},{6,10},{8,4},{10,6},{5,9},{7,11},{9,5},{11,7},{20,24},{22,26... | collective-permute-start | bytes 884744 | tf_op jit(solution)/shard_map/ppermute | solution.py:533
  43.8 7.7 %collective-permute-start.20 = (bf16[32,4608]{1,0:T(8,128)(2,1)S(1)}, bf16[32,4608]{1,0:T(8,128)(2,1)S(1)}, u32[]{:S(2)}, u32[]{:S(2)}) collective-permute-start(bf16[32,4608]{1,0:T(8,128)(2,1)S(1)} %get-tuple-element.91), channel_id=1, source_target_pairs={{0,4},{2,6},{4,0},{6,2},{8,12},{10,14},{12,8},{14,10},{1,5},{3,7},... | collective-permute-start | bytes 884744 | tf_op jit(solution)/shard_map/ppermute | solution.py:533
  43.8 8.2 %collective-permute-start.21 = (bf16[32,4608]{1,0:T(8,128)(2,1)S(1)}, bf16[32,4608]{1,0:T(8,128)(2,1)S(1)}, u32[]{:S(2)}, u32[]{:S(2)}) collective-permute-start(bf16[32,4608]{1,0:T(8,128)(2,1)S(1)} %get-tuple-element.92), channel_id=1, source_target_pairs={{4,8},{6,10},{8,4},{10,6},{5,9},{7,11},{9,5},{11,7},{20,24},{22,26... | collective-permute-start | bytes 884744 | tf_op jit(solution)/shard_map/ppermute | solution.py:533
  46.9 12.3 %collective-permute-start.19 = (bf16[32,4608]{1,0:T(8,128)(2,1)S(1)}, bf16[32,4608]{1,0:T(8,128)(2,1)S(1)}, u32[]{:S(2)}, u32[]{:S(2)}) collective-permute-start(bf16[32,4608]{1,0:T(8,128)(2,1)S(1)} %get-tuple-element.90), channel_id=1, source_target_pairs={{0,2},{2,0},{4,6},{6,4},{8,10},{10,8},{12,14},{14,12},{1,3},{3,1},... | collective-permute-start | bytes 884744 | tf_op jit(solution)/shard_map/ppermute | solution.py:533
  47.3 13.9 %collective-permute-start.23 = (bf16[32,4608]{1,0:T(8,128)(2,1)S(1)}, bf16[32,4608]{1,0:T(8,128)(2,1)S(1)}, u32[]{:S(2)}, u32[]{:S(2)}) collective-permute-start(bf16[32,4608]{1,0:T(8,128)(2,1)S(1)} %get-tuple-element.94), channel_id=1, source_target_pairs={{0,4},{2,6},{4,0},{6,2},{8,12},{10,14},{12,8},{14,10},{1,5},{3,7},... | collective-permute-start | bytes 884744 | tf_op jit(solution)/shard_map/ppermute | solution.py:533
  48.8 12.4 %collective-permute-start.25 = (bf16[32,4608]{1,0:T(8,128)(2,1)S(1)}, bf16[32,4608]{1,0:T(8,128)(2,1)S(1)}, u32[]{:S(2)}, u32[]{:S(2)}) collective-permute-start(bf16[32,4608]{1,0:T(8,128)(2,1)S(1)} %get-tuple-element.97), channel_id=1, source_target_pairs={{4,8},{6,10},{8,4},{10,6},{5,9},{7,11},{9,5},{11,7},{20,24},{22,26... | collective-permute-start | bytes 884744 | tf_op jit(solution)/shard_map/ppermute | solution.py:533
  51.6 7.6 %collective-permute-start.2 = (s32[8,128]{1,0:T(8,128)S(1)}, s32[8,128]{1,0:T(8,128)S(1)}, u32[]{:S(2)}, u32[]{:S(2)}) collective-permute-start(s32[8,128]{1,0:T(8,128)S(1)} %plan.1.table.index), channel_id=1, source_target_pairs={{0,16},{16,0},{1,17},{17,1},{2,18},{18,2},{3,19},{19,3},{4,20},{20... | collective-permute-start | bytes 12296 | tf_op jit(solution)/shard_map/ppermute | solution.py:505
  56.7 9.6 %collective-permute-start.22 = (bf16[32,4608]{1,0:T(8,128)(2,1)S(1)}, bf16[32,4608]{1,0:T(8,128)(2,1)S(1)}, u32[]{:S(2)}, u32[]{:S(2)}) collective-permute-start(bf16[32,4608]{1,0:T(8,128)(2,1)S(1)} %get-tuple-element.93), channel_id=1, source_target_pairs={{0,2},{2,0},{4,6},{6,4},{8,10},{10,8},{12,14},{14,12},{1,3},{3,1},... | collective-permute-start | bytes 884744 | tf_op jit(solution)/shard_map/ppermute | solution.py:533
  59.2 15.2 %collective-permute-start.24 = (bf16[32,4608]{1,0:T(8,128)(2,1)S(1)}, bf16[32,4608]{1,0:T(8,128)(2,1)S(1)}, u32[]{:S(2)}, u32[]{:S(2)}) collective-permute-start(bf16[32,4608]{1,0:T(8,128)(2,1)S(1)} %get-tuple-element.95), channel_id=1, source_target_pairs={{0,4},{2,6},{4,0},{6,2},{8,12},{10,14},{12,8},{14,10},{1,5},{3,7},... | collective-permute-start | bytes 884744 | tf_op jit(solution)/shard_map/ppermute | solution.py:533
  59.2 15.3 %collective-permute-start.27 = (bf16[32,4608]{1,0:T(8,128)(2,1)S(1)}, bf16[32,4608]{1,0:T(8,128)(2,1)S(1)}, u32[]{:S(2)}, u32[]{:S(2)}) collective-permute-start(bf16[32,4608]{1,0:T(8,128)(2,1)S(1)} %get-tuple-element.99), channel_id=1, source_target_pairs={{4,8},{6,10},{8,4},{10,6},{5,9},{7,11},{9,5},{11,7},{20,24},{22,26... | collective-permute-start | bytes 884744 | tf_op jit(solution)/shard_map/ppermute | solution.py:533
  61.9 17.3 %collective-permute-start.26 = (bf16[32,4608]{1,0:T(8,128)(2,1)S(1)}, bf16[32,4608]{1,0:T(8,128)(2,1)S(1)}, u32[]{:S(2)}, u32[]{:S(2)}) collective-permute-start(bf16[32,4608]{1,0:T(8,128)(2,1)S(1)} %get-tuple-element.98), channel_id=1, source_target_pairs={{0,4},{2,6},{4,0},{6,2},{8,12},{10,14},{12,8},{14,10},{1,5},{3,7},... | collective-permute-start | bytes 884744 | tf_op jit(solution)/shard_map/ppermute | solution.py:533
  62.2 19.3 %collective-permute-start.29 = (bf16[32,4608]{1,0:T(8,128)(2,1)S(1)}, bf16[32,4608]{1,0:T(8,128)(2,1)S(1)}, u32[]{:S(2)}, u32[]{:S(2)}) collective-permute-start(bf16[32,4608]{1,0:T(8,128)(2,1)S(1)} %get-tuple-element.101), channel_id=1, source_target_pairs={{4,8},{6,10},{8,4},{10,6},{5,9},{7,11},{9,5},{11,7},{20,24},{22,26... | collective-permute-start | bytes 884744 | tf_op jit(solution)/shard_map/ppermute | solution.py:533
  66.3 45.1 %collective-permute-start.36 = (f32[1024,256]{1,0:T(8,128)S(1)}, f32[1024,256]{1,0:T(8,128)S(1)}, u32[]{:S(2)}, u32[]{:S(2)}) collective-permute-start(f32[1024,256]{1,0:T(8,128)S(1)} %get-tuple-element.110), channel_id=1, source_target_pairs={{0,1},{1,0},{2,3},{3,2},{4,5},{5,4},{6,7},{7,6},{8,9},{9,8},{10,11... | collective-permute-start | bytes 3145736 | tf_op jit(solution)/shard_map/ppermute | solution.py:544
  74.5 36.9 %collective-permute-start.37 = (f32[1024,256]{1,0:T(8,128)S(1)}, f32[1024,256]{1,0:T(8,128)S(1)}, u32[]{:S(2)}, u32[]{:S(2)}) collective-permute-start(f32[1024,256]{1,0:T(8,128)S(1)} %get-tuple-element.112), channel_id=1, source_target_pairs={{0,1},{1,0},{2,3},{3,2},{4,5},{5,4},{6,7},{7,6},{8,9},{9,8},{10,11... | collective-permute-start | bytes 3145736 | tf_op jit(solution)/shard_map/ppermute | solution.py:544
  79.2 7.7 %collective-permute-start.28 = (bf16[32,4608]{1,0:T(8,128)(2,1)S(1)}, bf16[32,4608]{1,0:T(8,128)(2,1)S(1)}, u32[]{:S(2)}, u32[]{:S(2)}) collective-permute-start(bf16[32,4608]{1,0:T(8,128)(2,1)S(1)} %get-tuple-element.100), channel_id=1, source_target_pairs={{0,4},{2,6},{4,0},{6,2},{8,12},{10,14},{12,8},{14,10},{1,5},{3,7},... | collective-permute-start | bytes 884744 | tf_op jit(solution)/shard_map/ppermute | solution.py:533
  79.3 9.6 %collective-permute-start.31 = (bf16[32,4608]{1,0:T(8,128)(2,1)S(1)}, bf16[32,4608]{1,0:T(8,128)(2,1)S(1)}, u32[]{:S(2)}, u32[]{:S(2)}) collective-permute-start(bf16[32,4608]{1,0:T(8,128)(2,1)S(1)} %get-tuple-element.103), channel_id=1, source_target_pairs={{4,8},{6,10},{8,4},{10,6},{5,9},{7,11},{9,5},{11,7},{20,24},{22,26... | collective-permute-start | bytes 884744 | tf_op jit(solution)/shard_map/ppermute | solution.py:533
  82.2 11.0 %collective-permute-start.30 = (bf16[32,4608]{1,0:T(8,128)(2,1)S(1)}, bf16[32,4608]{1,0:T(8,128)(2,1)S(1)}, u32[]{:S(2)}, u32[]{:S(2)}) collective-permute-start(bf16[32,4608]{1,0:T(8,128)(2,1)S(1)} %get-tuple-element.102), channel_id=1, source_target_pairs={{0,4},{2,6},{4,0},{6,2},{8,12},{10,14},{12,8},{14,10},{1,5},{3,7},... | collective-permute-start | bytes 884744 | tf_op jit(solution)/shard_map/ppermute | solution.py:533
  86.9 8.4 %collective-permute-start.33 = (bf16[32,4608]{1,0:T(8,128)(2,1)S(1)}, bf16[32,4608]{1,0:T(8,128)(2,1)S(1)}, u32[]{:S(2)}, u32[]{:S(2)}) collective-permute-start(bf16[32,4608]{1,0:T(8,128)(2,1)S(1)} %get-tuple-element.105), channel_id=1, source_target_pairs={{4,8},{6,10},{8,4},{10,6},{5,9},{7,11},{9,5},{11,7},{20,24},{22,26... | collective-permute-start | bytes 884744 | tf_op jit(solution)/shard_map/ppermute | solution.py:533
  89.6 9.6 %collective-permute-start.32 = (bf16[32,4608]{1,0:T(8,128)(2,1)S(1)}, bf16[32,4608]{1,0:T(8,128)(2,1)S(1)}, u32[]{:S(2)}, u32[]{:S(2)}) collective-permute-start(bf16[32,4608]{1,0:T(8,128)(2,1)S(1)} %get-tuple-element.104), channel_id=1, source_target_pairs={{0,4},{2,6},{4,0},{6,2},{8,12},{10,14},{12,8},{14,10},{1,5},{3,7},... | collective-permute-start | bytes 884744 | tf_op jit(solution)/shard_map/ppermute | solution.py:533
  93.2 7.9 %collective-permute-start.34 = (bf16[32,4608]{1,0:T(8,128)(2,1)S(1)}, bf16[32,4608]{1,0:T(8,128)(2,1)S(1)}, u32[]{:S(2)}, u32[]{:S(2)}) collective-permute-start(bf16[32,4608]{1,0:T(8,128)(2,1)S(1)} %get-tuple-element.106), channel_id=1, source_target_pairs={{4,8},{6,10},{8,4},{10,6},{5,9},{7,11},{9,5},{11,7},{20,24},{22,26... | collective-permute-start | bytes 884744 | tf_op jit(solution)/shard_map/ppermute | solution.py:533
  (7 other events, 88.7 us)
